TPU v7x, 32 devices: a whole 2x2x4 slice. The times are simulated.
32 devices in a mesh: grp: 2 (over y), inst: 4 (over x, core), slab: 4 (over z).
Axes of the slice: x: 2, y: 2, z: 4, core: 2. Of those that a mesh axis runs over, the one named last changes fastest.
Arguments:
- states: float32 [8, 5, 256, 256], P(('grp', 'inst'), None, 'slab'), parts along dimension 0, may hold values from -6 to 6
- volumes: float32 [8, 256, 256], P(('grp', 'inst'), 'slab'), parts along dimension 0, may hold values from 0.5 to 2
- row_normals: float32 [8, 2, 256, 256], P(('grp', 'inst'), None, 'slab'), parts along dimension 0, may hold values from -4 to 4
- col_normals: float32 [8, 2, 256, 256], P(('grp', 'inst'), None, 'slab'), parts along dimension 0, may hold values from -4 to 4
- face_links: int32 [4, 256], P('slab'), may hold values from 0 to 255, each once within a row
- jacobians: float32 [2, 5, 5], replicated, may hold values from -2.5 to 2.5
Outputs:
- solution: float32 [8, 5, 256, 256], P(('grp', 'inst'), None, 'slab'), parts along dimension 0
There are 2 independent parts, one for each index of `grp`. A program takes and returns all parts, laid end to end along the dimension named above; an argument that names none is the same for every part. Nothing has to cross between parts.
Inputs may be any that keep to these rules, and one draw needn't show every extreme that they name: Each row of face_links names every one of the 256 columns once.
All inputs are finite; a program needn't handle non-finite values.
Results may differ from a plain program's by a relative error of at most 0.0001.
Values sent between devices are 32-bit elements; how exact they have to be, the bound alone decides.
No kernel may reach another device: no remote copies, remote signals or barrier semaphores. Data moves between devices by JAX's collectives and lax.ppermute only.
A program may use at most 64 MiB of HBM per device.

v0:
```python
import jax
import jax.numpy as jnp
import numpy as np
from jax import lax
from jax.sharding import PartitionSpec as P

ITERS = 2


frequency = 0.5
pseudo_step = 0.2
nyquist_damping = 0.25


def from_behind(x, axis, by):
    length = lax.axis_size(axis)
    return lax.ppermute(x, axis, [(i, (i + by) % length) for i in range(length)])


def spectral_table(instances):
    offsets = np.arange(instances)[:, None] - np.arange(instances)[None, :]
    phases = np.pi * offsets / instances
    sine_safe = np.where(offsets == 0, 1.0, np.sin(phases))
    parity = np.where(offsets % 2 == 0, 1.0, -1.0)
    matrix = np.where(offsets == 0, 0.0, 0.5 * frequency * parity * np.cos(phases) / sine_safe)
    matrix = matrix + nyquist_damping * parity
    return jnp.asarray(matrix, jnp.float32)


def face_flux(normals, lower_side, upper_side, jacobians):
    summed = lower_side + upper_side
    first_part = jnp.einsum("vw,nwac->nvac", jacobians[0], summed, precision=lax.Precision.HIGHEST)
    second_part = jnp.einsum("vw,nwac->nvac", jacobians[1], summed, precision=lax.Precision.HIGHEST)
    along_x = normals[:, 0:1]
    along_y = normals[:, 1:2]
    return 0.5 * (along_x * first_part + along_y * second_part) - 0.5 * (
        jnp.abs(along_x) + jnp.abs(along_y)
    ) * (upper_side - lower_side)


def body(states, volumes, row_normals, col_normals, face_links, jacobians):
    instances = lax.axis_size("inst")
    instance = lax.axis_index("inst")
    spectral = spectral_table(instances)
    own_row = spectral[instance]
    row_count = states.shape[2]
    volume_start = jnp.zeros(volumes.shape[1:], jnp.float32)
    volume_block_part = lax.all_gather(volumes, "inst", axis=0, tiled=True)
    volume_coefficients = lax.slice_in_dim(own_row, 0, volume_block_part.shape[0], axis=0)
    volume_rate = (
        volume_start
        + jnp.einsum(
            "m,mac->ac", volume_coefficients, volume_block_part, precision=lax.Precision.HIGHEST
        )
    )[None]
    links_own = face_links[0]
    order_own = jnp.argsort(links_own)
    flow_field = states
    for iteration in range(ITERS):
        state_start = jnp.zeros(flow_field.shape[1:], jnp.float32)
        block_part = lax.all_gather(flow_field, "inst", axis=0, tiled=True)
        coefficients = lax.slice_in_dim(own_row, 0, block_part.shape[0], axis=0)
        time_rate = (
            state_start
            + jnp.einsum("m,mvac->vac", coefficients, block_part, precision=lax.Precision.HIGHEST)
        )[None]
        previous = from_behind(flow_field[:, :, row_count - 1, :], "slab", 1)
        ghost_row = jnp.take(previous, links_own, axis=2)
        lower_cells = jnp.concatenate([ghost_row[:, :, None, :], flow_field[:, :, :-1, :]], axis=2)
        row_flux = face_flux(row_normals, lower_cells, flow_field, jacobians)
        sent_flux = jnp.take(row_flux[:, :, 0, :], order_own, axis=2)
        arriving = from_behind(sent_flux, "slab", -1)
        row_above = jnp.concatenate([row_flux[:, :, 1:, :], arriving[:, :, None, :]], axis=2)
        col_flux = face_flux(col_normals, jnp.roll(flow_field, 1, axis=3), flow_field, jacobians)
        col_right = jnp.roll(col_flux, -1, axis=3)
        rate = (
            volumes[:, None] * time_rate
            + flow_field * volume_rate[:, None]
            + (row_above - row_flux)
            + (col_right - col_flux)
        )
        flow_field = flow_field - pseudo_step * rate / volumes[:, None]
    return flow_field


def solution(mesh):
    return jax.shard_map(
        body,
        mesh=mesh,
        in_specs=(
            P(("grp", "inst"), None, "slab", None),
            P(("grp", "inst"), "slab", None),
            P(("grp", "inst"), None, "slab", None),
            P(("grp", "inst"), None, "slab", None),
            P("slab", None),
            P(),
        ),
        out_specs=P(("grp", "inst"), None, "slab", None),
        check_vma=False,
    )
```

profile of v0, /device:TPU:0, one launch (start us, length us, event | category | flops | bytes accessed | tf_op | source)
XLA Modules:
  0.0 73.1 jit_solution(13627711750278070170)
XLA Ops:
  6.5 0.7 all-gather.3.cloned.1.call-update
  7.3 0.8 %slice.81 = f32[1,5,1,256]{3,2,1,0:T(1,128)S(1)} slice(f32[1,5,64,256]{3,2,1,0:T(8,128)} %param.9), slice={[0:1], [0:5], [63:64], [0:256]} | slice | bytes 10240 | tf_op jit(solution)/shard_map/slice | solution.py:67
  8.2 3.1 %collective-permute-start = (f32[1,5,256]{1,2,0:T(8,128)S(1)}, f32[1,5,256]{1,2,0:T(8,128)S(1)}, u32[]{:S(2)}, u32[]{:S(2)}) collective-permute-start(f32[1,5,256]{1,2,0:T(8,128)S(1)} %bitcast.212), channel_id=1, source_target_pairs={{0,1},{1,2},{2,3},{3,0},{4,5},{5,6},{6,7},{7,4},{8,9},{9,10},{10,1... | collective-permute-start | bytes 15368 | tf_op jit(solution)/shard_map/ppermute | solution.py:17
  11.3 0.7 compare_and_fusion.1
  12.0 0.7 compare_select_fusion.1
  12.7 3.8 %sort.17 = (s32[256]{0:T(256)}, s32[256]{0:T(256)S(1)}) sort(s32[256]{0:T(256)} %bitcast.219, s32[256]{0:T(256)S(1)} %iota.4), dimensions={0}, to_apply=%region_0.2 | sort | flops 2048 | bytes 4096 | tf_op jit(solution)/shard_map/jit(argsort)/sort | solution.py:57
  16.5 0.8 %fusion.72 = (f32[1,5,5]{2,0,1:T(1,128)S(1)}, f32[1,5,5]{2,0,1:T(1,128)S(1)}) fusion(f32[2,5,5]{2,0,1:T(2,128)} %param.14), kind=kLoop, calls=%fused_computation.114 | loop fusion | bytes 400 | tf_op jit(solution)/shard_map/slice | solution.py:32
  17.3 0.9 %slice_bitcast_fusion.3 = (f32[64,256]{1,0:T(8,128)S(1)}, f32[64,256]{1,0:T(8,128)S(1)}, f32[64,256]{1,0:T(8,128)S(1)}) fusion(f32[1,2,64,256]{3,2,1,0:T(8,128)} %param.11), kind=kLoop, calls=%fused_computation.84 | loop fusion | flops 65536 | bytes 327680 | tf_op jit(solution)/shard_map/mul | solution.py:36
  18.2 0.9 %slice_bitcast_fusion.1 = (f32[64,256]{1,0:T(8,128)S(1)}, f32[64,256]{1,0:T(8,128)S(1)}, f32[64,256]{1,0:T(8,128)S(1)}) fusion(f32[1,2,64,256]{3,2,1,0:T(8,128)} %param.12), kind=kLoop, calls=%fused_computation.82 | loop fusion | flops 65536 | bytes 327680 | tf_op jit(solution)/shard_map/mul | solution.py:36
  19.1 7.8 %all_gather.10 = f32[4,64,256]{2,1,0:T(8,128)S(1)} all-gather(f32[1,64,256]{2,1,0:T(8,128)} %param.10), channel_id=1, replica_groups=mesh['grp'=2,'inst'=4,'slab'=4] {'inst'}, dimensions={0}, use_global_device_ids=true | all-gather | bytes 327680 | tf_op jit(solution)/shard_map/all_gather | solution.py:48
  26.9 1.4 %fusion.57 = f32[1,64,256]{2,0,1:T(1,128)S(1)} fusion(f32[4,64,256]{2,1,0:T(8,128)S(1)} %all_gather.10, f32[4,4]{1,0:T(4,128)} %constant.26.clone, s32[]{:T(128)S(6)} %select_n.18), kind=kOutput, calls=%fused_computation.76 | convolution fusion | flops 786432 | bytes 328196 | tf_op jit(solution)/shard_map/m,mac->ac/dot_general | solution.py:52
  28.8 0.8 %fusion.15 = f32[1,64,256,5]{2,3,1,0:T(8,128)S(1)} fusion(f32[1,5,64,256]{3,2,1,0:T(8,128)S(1)} %copy-done, f32[1,5,64,255]{3,1,2,0:T(8,128)S(1)} %copy.97, f32[1,5,64,1]{3,1,2,0:T(8,128)S(1)} %copy.98, f32[64,256]{1,0:T(8,128)S(1)} %get-tuple-element.10, f32[1,5,5]{2,0,1:T(1,128)S(1)} %get-tuple-element.15), kind=kOutput, calls=%fused_computation.27 | convolution fusion | flops 5160960 | bytes 1048676 | tf_op jit(solution)/shard_map/vw,nwac->nvac/dot_general | solution.py:33
  29.6 1.1 %fusion.14 = f32[1,5,64,256]{3,1,2,0:T(8,128)S(1)} fusion(f32[1,64,256,5]{2,3,1,0:T(8,128)S(1)} %fusion.15, f32[1,5,64,256]{3,2,1,0:T(8,128)S(1)} %copy-done, f32[1,5,64,255]{3,1,2,0:T(8,128)S(1)} %copy.97, f32[1,5,64,1]{3,1,2,0:T(8,128)S(1)} %copy.98, f32[64,256]{1,0:T(8,128)S(1)} %get-tuple-element.9, f32[64,256]{1,0:T(8,128)S(1)} %get-tuple-element.8, ...), kind=kOutput, calls=%fused_computation.26 | convolution fusion | flops 5652480 | bytes 1441892 | tf_op jit(solution)/shard_map/vw,nwac->nvac/dot_general | solution.py:32
  31.2 0.7 gather_fusion
  32.0 0.8 %fusion.9 = f32[1,64,256,5]{2,3,1,0:T(8,128)S(1)} fusion(f32[1,5,63,256]{3,1,2,0:T(8,128)S(1)} %copy.96, f32[1,5,1,256]{3,1,2,0:T(8,128)S(1)} %fusion.60, f32[1,5,64,256]{3,2,1,0:T(8,128)S(1)} %copy-done, f32[64,256]{1,0:T(8,128)S(1)} %get-tuple-element.13, f32[1,5,5]{2,0,1:T(1,128)S(1)} %get-tuple-element.15), kind=kOutput, calls=%fused_computation.21 | convolution fusion | flops 5160960 | bytes 1048676 | tf_op jit(solution)/shard_map/vw,nwac->nvac/dot_general | solution.py:33
  32.8 1.0 %fusion.8 = f32[1,5,64,256]{3,1,2,0:T(8,128)S(1)} fusion(f32[1,64,256,5]{2,3,1,0:T(8,128)S(1)} %fusion.9, f32[1,5,63,256]{3,1,2,0:T(8,128)S(1)} %copy.96, f32[1,5,1,256]{3,1,2,0:T(8,128)S(1)} %fusion.60, f32[1,5,64,256]{3,2,1,0:T(8,128)S(1)} %copy-done, f32[64,256]{1,0:T(8,128)S(1)} %get-tuple-element.12, f32[64,256]{1,0:T(8,128)S(1)} %get-tuple-element.11, ...), kind=kOutput, calls=%fused_computation.20 | convolution fusion | flops 5652480 | bytes 1441892 | tf_op jit(solution)/shard_map/vw,nwac->nvac/dot_general | solution.py:32
  34.1 0.7 %gather_fusion.1 = f32[256,5]{1,0:T(8,128)S(1)} fusion(f32[5,256]{0,1:T(8,128)S(1)} %copy.36, s32[1024]{0:T(1024)S(1)} %pad_clamp_fusion), kind=kCustom, calls=%fused_computation.1.clone | custom fusion | bytes 11264 | tf_op jit(solution)/shard_map/jit(_take)/gather | solution.py:71
  34.9 1.9 %collective-permute-start.1 = (f32[1,5,256]{2,1,0:T(8,128)S(1)}, f32[1,5,256]{2,1,0:T(8,128)S(1)}, u32[]{:S(2)}, u32[]{:S(2)}) collective-permute-start(f32[1,5,256]{2,1,0:T(8,128)S(1)} %bitcast_select_fusion.2), channel_id=1, source_target_pairs={{0,3},{1,0},{2,1},{3,2},{4,7},{5,4},{6,5},{7,6},{8,11},{9,8},{10,9... | collective-permute-start | bytes 15368 | tf_op jit(solution)/shard_map/ppermute | solution.py:17
  36.8 4.2 %fusion.2 = f32[1,5,64,256]{3,0,2,1:T(1,128)S(1)} fusion(f32[4,5,64,256]{3,2,1,0:T(8,128)} %all-gather.3.cloned.1.call-done, f32[4,4]{1,0:T(4,128)} %constant.26.clone, s32[]{:T(128)S(6)} %select_n.18), kind=kOutput, calls=%fused_computation.6 | convolution fusion | flops 3932160 | bytes 1638916 | tf_op jit(solution)/shard_map/m,mvac->vac/dot_general | solution.py:65
  41.0 0.6 fusion.32
  41.7 0.8 %copy.43 = f32[1,5,64,256]{3,2,1,0:T(8,128)} copy(f32[1,5,64,256]{3,1,2,0:T(8,128)S(1)} %fusion.32) | data formatting | bytes 655360 | tf_op jit(solution)/shard_map/sub | solution.py:82
  43.1 0.7 fusion.27
  43.9 0.9 %fusion.26 = f32[1,5,64,256]{3,1,2,0:T(8,128)S(1)} fusion(f32[1,64,256,5]{2,3,1,0:T(8,128)S(1)} %fusion.27, f32[1,5,64,256]{3,1,2,0:T(8,128)S(1)} %fusion.32, f32[1,5,64,255]{3,1,2,0:T(8,128)S(1)} %bitcast.205, f32[1,5,64,1]{3,1,2,0:T(8,128)S(1)} %slice.121, f32[64,256]{1,0:T(8,128)S(1)} %copy-done.9, f32[64,256]{1,0:T(8,128)S(1)} %copy-done.7, ...), kind=kOutput, calls=%fused_computation.38 | convolution fusion | flops 5652480 | bytes 1441892 | tf_op jit(solution)/shard_map/vw,nwac->nvac/dot_general | solution.py:32
  45.0 3.4 %collective-permute-done.2 = f32[1,5,256]{2,1,0:T(8,128)S(1)} collective-permute-done((f32[1,5,256]{2,1,0:T(8,128)S(1)}, f32[1,5,256]{2,1,0:T(8,128)S(1)}, u32[]{:S(2)}, u32[]{:S(2)}) %collective-permute-start.2) | collective-permute-done | bytes 5152 | tf_op jit(solution)/shard_map/ppermute | solution.py:17
  48.5 0.7 %gather_fusion.2 = f32[256,5]{1,0:T(8,128)S(1)} fusion(f32[5,256]{0,1:T(8,128)S(1)} %copy.44, s32[1024]{0:T(1024)S(1)} %pad_clamp_fusion.1), kind=kCustom, calls=%fused_computation.2.clone | custom fusion | bytes 11264 | tf_op jit(solution)/shard_map/jit(_take)/gather | solution.py:68
  49.3 0.6 fusion.21
  50.0 0.7 %fusion.20 = f32[1,5,64,256]{3,1,2,0:T(8,128)S(1)} fusion(f32[1,64,256,5]{2,3,1,0:T(8,128)S(1)} %fusion.21, f32[1,5,64,256]{3,1,2,0:T(8,128)S(1)} %fusion.32, f32[1,5,63,256]{3,1,2,0:T(8,128)S(1)} %slice.118, f32[1,5,1,256]{3,1,2,0:T(8,128)S(1)} %fusion.59, f32[64,256]{1,0:T(8,128)S(1)} %get-tuple-element.12, f32[64,256]{1,0:T(8,128)S(1)} %get-tuple-element.11, ...), kind=kOutput, calls=%fused_computation.32 | convolution fusion | flops 5652480 | bytes 1441892 | tf_op jit(solution)/shard_map/vw,nwac->nvac/dot_general | solution.py:32
  51.0 0.7 %gather_fusion.3 = f32[256,5]{1,0:T(8,128)S(1)} fusion(f32[5,256]{0,1:T(8,128)S(1)} %copy.46, s32[1024]{0:T(1024)S(1)} %pad_clamp_fusion), kind=kCustom, calls=%fused_computation.3.clone | custom fusion | bytes 11264 | tf_op jit(solution)/shard_map/jit(_take)/gather | solution.py:71
  51.8 0.7 collective-permute-start.3
  52.4 8.2 %all-gather.5.cloned.1.call-done = f32[4,5,64,256]{3,2,1,0:T(8,128)} async-done(((f32[1,5,64,256]{3,2,1,0:T(8,128)}), f32[4,5,64,256]{3,2,1,0:T(8,128)}) %all-gather.5.cloned.1.call-update) | async-done | bytes 1310736 | tf_op jit(solution)/shard_map/all_gather | solution.py:61
  60.6 4.2 %fusion = f32[1,5,64,256]{3,0,2,1:T(1,128)S(1)} fusion(f32[4,5,64,256]{3,2,1,0:T(8,128)} %all-gather.5.cloned.1.call-done, f32[4,4]{1,0:T(4,128)} %constant.26.clone, s32[]{:T(128)S(6)} %select_n.18), kind=kOutput, calls=%fused_computation.4 | convolution fusion | flops 3932160 | bytes 1638916 | tf_op jit(solution)/shard_map/m,mvac->vac/dot_general | solution.py:65
  65.4 0.8 %copy.48 = f32[1,5,64,256]{3,2,1,0:T(8,128)} copy(f32[1,5,64,256]{3,1,2,0:T(8,128)S(1)} %fusion.37) | data formatting | bytes 655360 | tf_op jit(solution)/shard_map/sub | solution.py:82
  (76 shorter events, 3.2 us)
Async XLA Ops:
  6.5 21.8 %copy-start = (f32[1,5,64,256]{3,2,1,0:T(8,128)S(1)}, f32[1,5,64,256]{3,2,1,0:T(8,128)}, u32[]{:S(2)}) copy-start(f32[1,5,64,256]{3,2,1,0:T(8,128)} %param.9) | copy-start | bytes 983044
  6.5 30.2 %all-gather.3.cloned.1.call-start = ((), (), s32[]{:S(2)}) async-start(), calls=%async_computation | async-start | bytes 1638400 | tf_op jit(solution)/shard_map/all_gather | solution.py:61
  7.3 53.4 %all-gather.5.cloned.1.call-start = ((), (), s32[]{:S(2)}) async-start(), calls=%async_computation.1 | async-start | bytes 1638400 | tf_op jit(solution)/shard_map/all_gather | solution.py:61
  8.2 22.9 %collective-permute-start = (f32[1,5,256]{1,2,0:T(8,128)S(1)}, f32[1,5,256]{1,2,0:T(8,128)S(1)}, u32[]{:S(2)}, u32[]{:S(2)}) collective-permute-start(f32[1,5,256]{1,2,0:T(8,128)S(1)} %bitcast.212), channel_id=1, source_target_pairs={{0,1},{1,2},{2,3},{3,0},{4,5},{5,6},{6,7},{7,4},{8,9},{9,10},{10,1... | collective-permute-start | bytes 15368 | tf_op jit(solution)/shard_map/ppermute | solution.py:17
  12.0 20.0 %copy-start.12 = (pred[256]{0:T(512)(128)(4,1)}, pred[256]{0:T(512)(128)(4,1)S(1)}, u32[]{:S(2)}) copy-start(pred[256]{0:T(512)(128)(4,1)S(1)} %compare_and_fusion.1) | copy-start | bytes 772
  19.1 10.5 %copy-start.10 = (f32[64,256]{1,0:T(8,128)}, f32[64,256]{1,0:T(8,128)S(1)}, u32[]{:S(2)}) copy-start(f32[64,256]{1,0:T(8,128)S(1)} %get-tuple-element.10) | copy-start | bytes 196612
  19.1 10.5 %copy-start.6 = (f32[64,256]{1,0:T(8,128)}, f32[64,256]{1,0:T(8,128)S(1)}, u32[]{:S(2)}) copy-start(f32[64,256]{1,0:T(8,128)S(1)} %get-tuple-element.8) | copy-start | bytes 196612
  19.1 10.5 %copy-start.8 = (f32[64,256]{1,0:T(8,128)}, f32[64,256]{1,0:T(8,128)S(1)}, u32[]{:S(2)}) copy-start(f32[64,256]{1,0:T(8,128)S(1)} %get-tuple-element.9) | copy-start | bytes 196612
  28.3 6.6 %copy-start.14 = (pred[256]{0:T(512)(128)(4,1)}, pred[256]{0:T(512)(128)(4,1)S(1)}, u32[]{:S(2)}) copy-start(pred[256]{0:T(512)(128)(4,1)S(1)} %compare_and_fusion) | copy-start | bytes 772
  30.7 1.2 %copy-start.3 = (f32[1,5,64,256]{3,1,2,0:T(8,128)}, f32[1,5,64,256]{3,1,2,0:T(8,128)S(1)}, u32[]{:S(2)}) copy-start(f32[1,5,64,256]{3,1,2,0:T(8,128)S(1)} %fusion.14) | copy-start | bytes 983044
  33.8 7.2 %copy-start.4 = (f32[1,5,64,256]{3,1,2,0:T(8,128)S(1)}, f32[1,5,64,256]{3,1,2,0:T(8,128)}, u32[]{:S(2)}) copy-start(f32[1,5,64,256]{3,1,2,0:T(8,128)} %copy-done.3) | copy-start | bytes 983044
  33.9 7.2 %slice-start.1 = ((f32[1,5,64,256]{3,1,2,0:T(8,128)}), f32[1,5,64,1]{3,1,2,0:T(8,128)S(1)}, s32[]{:S(2)}) async-start(f32[1,5,64,256]{3,1,2,0:T(8,128)} %copy-done.3), calls=%async_computation.3 | async-start | bytes 524288 | tf_op jit(solution)/shard_map/jit(_roll_static)/slice | solution.py:75
  33.9 7.2 %copy-start.5 = (f32[1,64,256]{2,1,0:T(8,128)S(1)}, f32[1,64,256]{2,1,0:T(8,128)}, u32[]{:S(2)}) copy-start(f32[1,64,256]{2,1,0:T(8,128)} %param.10) | copy-start | bytes 196612
  34.9 6.1 %collective-permute-start.1 = (f32[1,5,256]{2,1,0:T(8,128)S(1)}, f32[1,5,256]{2,1,0:T(8,128)S(1)}, u32[]{:S(2)}, u32[]{:S(2)}) collective-permute-start(f32[1,5,256]{2,1,0:T(8,128)S(1)} %bitcast_select_fusion.2), channel_id=1, source_target_pairs={{0,3},{1,0},{2,1},{3,2},{4,7},{5,4},{6,5},{7,6},{8,11},{9,8},{10,9... | collective-permute-start | bytes 15368 | tf_op jit(solution)/shard_map/ppermute | solution.py:17
  41.7 1.5 %copy-start.11 = (f32[64,256]{1,0:T(8,128)S(1)}, f32[64,256]{1,0:T(8,128)}, u32[]{:S(2)}) copy-start(f32[64,256]{1,0:T(8,128)} %copy-done.10) | copy-start | bytes 196612
  42.5 1.3 %copy-start.7 = (f32[64,256]{1,0:T(8,128)S(1)}, f32[64,256]{1,0:T(8,128)}, u32[]{:S(2)}) copy-start(f32[64,256]{1,0:T(8,128)} %copy-done.6) | copy-start | bytes 196612
  42.5 1.3 %copy-start.9 = (f32[64,256]{1,0:T(8,128)S(1)}, f32[64,256]{1,0:T(8,128)}, u32[]{:S(2)}) copy-start(f32[64,256]{1,0:T(8,128)} %copy-done.8) | copy-start | bytes 196612
  42.7 5.7 %collective-permute-start.2 = (f32[1,5,256]{2,1,0:T(8,128)S(1)}, f32[1,5,256]{2,1,0:T(8,128)S(1)}, u32[]{:S(2)}, u32[]{:S(2)}) collective-permute-start(f32[1,5,256]{2,1,0:T(8,128)S(1)} %slice_bitcast_fusion.5), channel_id=1, source_target_pairs={{0,1},{1,2},{2,3},{3,0},{4,5},{5,6},{6,7},{7,4},{8,9},{9,10},{10,1... | collective-permute-start | bytes 15368 | tf_op jit(solution)/shard_map/ppermute | solution.py:17
  44.7 3.8 %copy-start.1 = (f32[1,5,64,256]{3,1,2,0:T(8,128)}, f32[1,5,64,256]{3,1,2,0:T(8,128)S(1)}, u32[]{:S(2)}) copy-start(f32[1,5,64,256]{3,1,2,0:T(8,128)S(1)} %fusion.26) | copy-start | bytes 983044
  44.7 4.6 %copy-start.13 = (pred[256]{0:T(512)(128)(4,1)S(1)}, pred[256]{0:T(512)(128)(4,1)}, u32[]{:S(2)}) copy-start(pred[256]{0:T(512)(128)(4,1)} %copy-done.12) | copy-start | bytes 772
  50.7 1.0 %copy-start.15 = (pred[256]{0:T(512)(128)(4,1)S(1)}, pred[256]{0:T(512)(128)(4,1)}, u32[]{:S(2)}) copy-start(pred[256]{0:T(512)(128)(4,1)} %copy-done.14) | copy-start | bytes 772
  50.7 14.1 %copy-start.2 = (f32[1,5,64,256]{3,1,2,0:T(8,128)S(1)}, f32[1,5,64,256]{3,1,2,0:T(8,128)}, u32[]{:S(2)}) copy-start(f32[1,5,64,256]{3,1,2,0:T(8,128)} %copy-done.1) | copy-start | bytes 983044
  50.8 14.1 %slice-start = ((f32[1,5,64,256]{3,1,2,0:T(8,128)}), f32[1,5,64,1]{3,1,2,0:T(8,128)S(1)}, s32[]{:S(2)}) async-start(f32[1,5,64,256]{3,1,2,0:T(8,128)} %copy-done.1), calls=%async_computation.2 | async-start | bytes 524288 | tf_op jit(solution)/shard_map/jit(_roll_static)/slice | solution.py:75
  51.8 13.1 %collective-permute-start.3 = (f32[1,5,256]{2,1,0:T(8,128)S(1)}, f32[1,5,256]{2,1,0:T(8,128)S(1)}, u32[]{:S(2)}, u32[]{:S(2)}) collective-permute-start(f32[1,5,256]{2,1,0:T(8,128)S(1)} %bitcast_select_fusion), channel_id=1, source_target_pairs={{0,3},{1,0},{2,1},{3,2},{4,7},{5,4},{6,5},{7,6},{8,11},{9,8},{10,9... | collective-permute-start | bytes 15368 | tf_op jit(solution)/shard_map/ppermute | solution.py:17
Sparse Core Ops, SparseCore 0:
  8.9 22.2 all-gather.2
  42.7 17.9 all-gather.4
where the time goes:
time: 73.5 us; the launch traced here: 73.1 us
  matrix products  16.5 us (22%)
  between operations  13.9 us (19%)
  waiting for transfers between devices  12.3 us (17%)
  local copies, waits for them, and re-layouts  8.29 us (11%)
  other arithmetic  8.2 us (11%)
  blocking collectives  7.77 us (11%)
  starting transfers between devices  6.09 us (8%)
    dot_general x2, matrix products, body(): jnp.einsum('m,mvac->vac', coefficients, block_part, precision=lax.Precisi...  8.48 us
    all_gather x2, waiting for transfers between devices, body(): block_part = lax.all_gather(flow_field, 'inst', axis=0, tiled=True)  8.17 us
    all_gather x1, blocking collectives, body(): volume_block_part = lax.all_gather(volumes, 'inst', axis=0, tiled=True)  7.77 us
    ppermute x4, starting transfers between devices, from_behind(): lax.ppermute(x, axis, [(i, (i + by) % length) for i in range(length)])  6.05 us
    sort x1, other arithmetic, body(): order_own = jnp.argsort(links_own)  3.84 us
    dot_general x4, matrix products, face_flux(): jnp.einsum('vw,nwac->nvac', jacobians[0], summed, precision=lax.Precision...  3.73 us
    ppermute x4, waiting for transfers between devices, from_behind(): lax.ppermute(x, axis, [(i, (i + by) % length) for i in range(length)])  3.38 us
    dot_general x4, matrix products, face_flux(): jnp.einsum('vw,nwac->nvac', jacobians[1], summed, precision=lax.Precision...  2.95 us
  transfers between devices with their start and end apart: 6, of which 2 were waited for; matrix products, arithmetic and copies ran while one was open for 41% of the time, Pallas kernels for 0%

commit v1 on v0

v1 whole, which is shorter than its diff:
```python
import functools

import jax
import jax.numpy as jnp
import numpy as np
from jax import lax
from jax.experimental import pallas as pl
from jax.experimental.pallas import tpu as pltpu
from jax.sharding import PartitionSpec as P

ITERS = 2


frequency = 0.5
pseudo_step = 0.2
nyquist_damping = 0.25


def spectral_table(instances):
    offsets = np.arange(instances)[:, None] - np.arange(instances)[None, :]
    phases = np.pi * offsets / instances
    sine_safe = np.where(offsets == 0, 1.0, np.sin(phases))
    parity = np.where(offsets % 2 == 0, 1.0, -1.0)
    matrix = np.where(offsets == 0, 0.0, 0.5 * frequency * parity * np.cos(phases) / sine_safe)
    matrix = matrix + nyquist_damping * parity
    return jnp.asarray(matrix, jnp.float32)


def row_step(rows):
    return rows if rows % 8 == 0 else 1


def pack_kernel(n, rows, states, volumes, row_normals, col_normals, links, *outs):
    nvar, depth = states.shape[1], states.shape[2]
    bufs, edges = outs[:n], outs[n:]
    me = lax.axis_index("inst")

    def put(ref, at, row_below, row_in, row_outer):
        for v in range(nvar):
            ref[pl.ds(at + v, 1), :] = states[0, v, pl.ds(row_below, 1), :]
            ref[pl.ds(at + nvar + v, 1), :] = states[0, v, pl.ds(row_in, 1), :]
        at = at + 2 * nvar
        ref[pl.ds(at, 1), :] = volumes[0, pl.ds(row_in, 1), :]
        for d in range(2):
            ref[pl.ds(at + 1 + d, 1), :] = row_normals[0, d, pl.ds(row_outer, 1), :]
            ref[pl.ds(at + 3 + d, 1), :] = col_normals[0, d, pl.ds(row_in, 1), :]

    def put_inner(ref, at, row):
        for d in range(2):
            ref[pl.ds(at + d, 1), :] = row_normals[0, d, pl.ds(row, 1), :]

    for k in range(n):
        buf = bufs[k]
        block = jnp.bitwise_xor(me, k)
        lo = pl.multiple_of(block * rows, rows)
        at = 0
        step = row_step(rows)
        for r in range(0, rows, step):
            here = pl.ds(lo + r, step)
            for v in range(nvar):
                buf[pl.ds(v * rows + r, step), :] = states[0, v, here, :]
            buf[pl.ds(nvar * rows + r, step), :] = volumes[0, here, :]
            for d in range(2):
                buf[pl.ds((nvar + 1 + d) * rows + r, step), :] = row_normals[0, d, here, :]
                buf[pl.ds((nvar + 3 + d) * rows + r, step), :] = col_normals[0, d, here, :]
        at = (nvar + 5) * rows
        below_1, below_2 = jnp.maximum(lo - 1, 0), jnp.maximum(lo - 2, 0)
        above_1, above_2 = jnp.minimum(lo + rows, depth - 1), jnp.minimum(lo + rows + 1, depth - 1)
        put(buf, at, below_2, below_1, below_1)
        at += 2 * nvar + 5
        put(buf, at, above_2, above_1, above_2)
        put_inner(buf, at + 2 * nvar + 5, above_1)
    for k in range(n):
        edge = edges[k]
        upward = me == k
        put(
            edge,
            0,
            jnp.where(upward, depth - 2, 1),
            jnp.where(upward, depth - 1, 0),
            jnp.where(upward, depth - 1, 1),
        )
        put_inner(edge, 2 * nvar + 5, 0)
        edge[pl.ds(2 * nvar + 7, 1), :] = links[...].astype(jnp.float32)


def split_dot(x, onehot, transposed):
    high = x.astype(jnp.bfloat16)
    rest = x - high.astype(jnp.float32)
    middle = rest.astype(jnp.bfloat16)
    low = (rest - middle.astype(jnp.float32)).astype(jnp.bfloat16)
    count = x.shape[0]
    stacked = jnp.concatenate([high, middle, low], axis=0)
    out = lax.dot_general(
        stacked,
        onehot,
        (((1,), (1 if transposed else 0,)), ((), ())),
        preferred_element_type=jnp.float32,
    )
    return out[:count] + (out[count : 2 * count] + out[2 * count :])


def compute_kernel(n, rows, nvar, iterations, table, jacobians, links, *refs):
    bufs, edges, outs = refs[:n], refs[n : 2 * n], refs[2 * n : 3 * n]
    halo, rim, flow = refs[3 * n :]
    columns = links.shape[1]
    main = (nvar + 5) * rows
    below_at, above_at = main, main + 2 * nvar + 5
    me = lax.axis_index("inst")
    first, last = me == 0, me == n - 1
    half = [[[0.5 * jacobians[d, v, w] for w in range(nvar)] for v in range(nvar)] for d in range(2)]
    weights = [
        [pseudo_step * table[jnp.bitwise_xor(me, k), jnp.bitwise_xor(me, j)] for j in range(n)]
        for k in range(n)
    ]

    for k in range(n):
        for t in range(2 * nvar + 5):
            halo[t, pl.ds(k, 1), :] = jnp.where(
                first, edges[k][pl.ds(t, 1), :], bufs[k][pl.ds(below_at + t, 1), :]
            )
        for t in range(2 * nvar + 7):
            halo[t, pl.ds(n + k, 1), :] = jnp.where(
                last, edges[k][pl.ds(t, 1), :], bufs[k][pl.ds(above_at + t, 1), :]
            )
        for d in range(2):
            halo[2 * nvar + 5 + d, pl.ds(k, 1), :] = bufs[k][pl.ds((nvar + 1 + d) * rows, 1), :]

    own = lax.broadcasted_iota(jnp.int32, (1, columns), 1)
    cell = lax.broadcasted_iota(jnp.int32, (columns, columns), 0)
    links_above = edges[0][pl.ds(2 * nvar + 7, 1), :].astype(jnp.int32)
    onehot_below = (cell == jnp.where(first, links[...], own)).astype(jnp.float32).astype(jnp.bfloat16)
    onehot_above = (cell == jnp.where(last, links_above, own)).astype(jnp.float32).astype(jnp.bfloat16)
    side = lax.broadcasted_iota(jnp.int32, (2 * n, columns), 0)
    is_below = side < n
    place = jnp.where(is_below, side, side - n)

    def crossed(values, back):
        stacked = jnp.concatenate(values, axis=0)
        through_below = split_dot(stacked, onehot_below, back)
        through_above = split_dot(stacked, onehot_above, back)
        return [
            jnp.where(
                is_below,
                through_below[2 * n * v : 2 * n * (v + 1)],
                through_above[2 * n * v : 2 * n * (v + 1)],
            )
            for v in range(nvar)
        ]

    def transformed(values):
        return [
            [sum(half[d][v][w] * values[w] for w in range(nvar)) for v in range(nvar)] for d in range(2)
        ]

    def flux(normal, lower, lower_j, upper, upper_j):
        spread = 0.5 * (jnp.abs(normal[0]) + jnp.abs(normal[1]))
        return [
            normal[0] * (lower_j[0][v] + upper_j[0][v])
            + normal[1] * (lower_j[1][v] + upper_j[1][v])
            - spread * (upper[v] - lower[v])
            for v in range(nvar)
        ]

    def col_change(normal, values, values_j):
        left = [pltpu.roll(x, 1, 1) for x in values]
        left_j = [[pltpu.roll(x, 1, 1) for x in values_j[d]] for d in range(2)]
        across = flux(normal, left, left_j, values, values_j)
        return [pltpu.roll(x, columns - 1, 1) - x for x in across]

    def pick(mask, a, b):
        return [jnp.where(mask, x, y) for x, y in zip(a, b)]

    def spread_sum(x):
        total = None
        for j in range(n):
            factor = jnp.zeros(x.shape, jnp.float32)
            for k in range(n):
                factor = jnp.where(place == k, weights[k][j], factor)
            row = jnp.where(is_below, x[j : j + 1], x[n + j : n + j + 1])
            total = factor * row if total is None else total + factor * row
        return total

    row_index = lax.broadcasted_iota(jnp.int32, (rows, columns), 0)

    def plane(k, p):
        return bufs[k][pl.ds(p * rows, rows), :]

    inner = [halo[nvar + v] for v in range(nvar)]
    for iteration in range(iterations):
        final = iteration == iterations - 1

        def cells(k, v):
            return plane(k, v) if iteration == 0 else flow[iteration - 1, k, v]

        for k in range(n):
            for v in range(nvar):
                if iteration == 0:
                    rim[v, pl.ds(k, 1), :] = bufs[k][pl.ds(v * rows, 1), :]
                    rim[v, pl.ds(n + k, 1), :] = bufs[k][pl.ds(v * rows + rows - 1, 1), :]
                else:
                    rim[v, pl.ds(k, 1), :] = flow[iteration - 1, k, v, pl.ds(0, 1), :]
                    rim[v, pl.ds(n + k, 1), :] = flow[iteration - 1, k, v, pl.ds(rows - 1, 1), :]
        edge_rows = [rim[v] for v in range(nvar)]
        lower = crossed(pick(is_below, inner, edge_rows), False)
        upper = pick(is_below, edge_rows, inner)
        inner_face = [halo[2 * nvar + 5], halo[2 * nvar + 6]]
        flux_inner = flux(inner_face, lower, transformed(lower), upper, transformed(upper))
        flux_back = crossed(flux_inner, True)
        if not final:
            outer = [halo[v] for v in range(nvar)]
            low, high = pick(is_below, outer, inner), pick(is_below, inner, outer)
            outer_face = [halo[2 * nvar + 1], halo[2 * nvar + 2]]
            flux_outer = flux(outer_face, low, transformed(low), high, transformed(high))
            change = [
                jnp.where(is_below, flux_back[v] - flux_outer[v], flux_outer[v] - flux_inner[v])
                for v in range(nvar)
            ]
            inner_col = [halo[2 * nvar + 3], halo[2 * nvar + 4]]
            beside = col_change(inner_col, inner, transformed(inner))
            volume = halo[2 * nvar]
            inverse = 1.0 / volume
            volume_rate = spread_sum(volume)
            inner_next = [
                inner[v]
                - spread_sum(inner[v])
                - inverse * (inner[v] * volume_rate + pseudo_step * (change[v] + beside[v]))
                for v in range(nvar)
            ]
        for k in range(n):
            values = [cells(k, v) for v in range(nvar)]
            values_j = transformed(values)
            shifted = [pltpu.roll(x, 1, 0) for x in values]
            shifted_j = [[pltpu.roll(x, 1, 0) for x in values_j[d]] for d in range(2)]
            row_face = [plane(k, nvar + 1), plane(k, nvar + 2)]
            col_face = [plane(k, nvar + 3), plane(k, nvar + 4)]
            row_flux = flux(row_face, shifted, shifted_j, values, values_j)
            row_flux = [
                jnp.where(row_index == 0, flux_inner[v][k : k + 1], row_flux[v]) for v in range(nvar)
            ]
            row_above = [
                jnp.where(
                    row_index == rows - 1,
                    flux_back[v][n + k : n + k + 1],
                    pltpu.roll(row_flux[v], rows - 1, 0),
                )
                for v in range(nvar)
            ]
            beside = col_change(col_face, values, values_j)
            inverse = 1.0 / plane(k, nvar)
            volume_rate = sum(weights[k][j] * plane(j, nvar) for j in range(n))
            for v in range(nvar):
                time_rate = sum(weights[k][j] * cells(j, v) for j in range(n))
                change = pseudo_step * ((row_above[v] - row_flux[v]) + beside[v])
                moved = values[v] - time_rate - inverse * (values[v] * volume_rate + change)
                if final:
                    outs[k][v] = moved
                else:
                    flow[iteration, k, v] = moved
        if not final:
            inner = inner_next


def unpack_kernel(n, rows, *refs):
    blocks, out = refs[:n], refs[n]
    me = lax.axis_index("inst")
    for k in range(n):
        block = jnp.bitwise_xor(me, k)
        lo = pl.multiple_of(block * rows, rows)
        step = row_step(rows)
        for v in range(out.shape[1]):
            for r in range(0, rows, step):
                out[0, v, pl.ds(lo + r, step), :] = blocks[k][v, pl.ds(r, step), :]


def body(states, volumes, row_normals, col_normals, face_links, jacobians):
    n = lax.axis_size("inst")
    slabs = lax.axis_size("slab")
    _, nvar, depth, columns = states.shape
    rows = depth // n
    buffer_rows = (nvar + 5) * rows + 4 * nvar + 12
    edge_rows = -(-(2 * nvar + 8) // 8) * 8

    def f32(*shape):
        return jax.ShapeDtypeStruct(shape, jnp.float32)

    vmem = pl.BlockSpec(memory_space=pltpu.VMEM)
    smem = pl.BlockSpec(memory_space=pltpu.SMEM)

    packed = pl.pallas_call(
        functools.partial(pack_kernel, n, rows),
        out_shape=[f32(buffer_rows, columns)] * n + [f32(edge_rows, columns)] * n,
        in_specs=[vmem] * 5,
        out_specs=[vmem] * (2 * n),
        name="pack",
    )(states, volumes, row_normals, col_normals, face_links)
    sent, sent_edges = packed[:n], packed[n:]

    def swapped(x, k):
        return lax.ppermute(x, "inst", [(i, i ^ k) for i in range(n)])

    received = [sent[0]] + [swapped(sent[k], k) for k in range(1, n)]

    def to_edge(x, k):
        pairs = []
        for s in range(slabs):
            pairs.append((k * slabs + s, (s + 1) % slabs))
            pairs.append(((n - 1 - k) * slabs + s, (n - 1) * slabs + (s - 1) % slabs))
        return lax.ppermute(x, ("inst", "slab"), pairs)

    edges = [to_edge(sent_edges[k], k) for k in range(n)]

    results = pl.pallas_call(
        functools.partial(compute_kernel, n, rows, nvar, ITERS),
        out_shape=[f32(nvar, rows, columns)] * n,
        in_specs=[smem, smem, vmem] + [vmem] * (2 * n),
        out_specs=[vmem] * n,
        scratch_shapes=[
            pltpu.VMEM((2 * nvar + 7, 2 * n, columns), jnp.float32),
            pltpu.VMEM((nvar, 2 * n, columns), jnp.float32),
            pltpu.VMEM((ITERS - 1, n, nvar, rows, columns), jnp.float32),
        ],
        compiler_params=pltpu.CompilerParams(vmem_limit_bytes=32 * 1024 * 1024),
        name="iterate",
    )(spectral_table(n), jacobians, face_links, *received, *edges)

    returned = [results[0]] + [swapped(results[k], k) for k in range(1, n)]
    return pl.pallas_call(
        functools.partial(unpack_kernel, n, rows),
        out_shape=f32(1, nvar, depth, columns),
        in_specs=[vmem] * n,
        out_specs=vmem,
        name="unpack",
    )(*returned)


def solution(mesh):
    return jax.shard_map(
        body,
        mesh=mesh,
        in_specs=(
            P(("grp", "inst"), None, "slab", None),
            P(("grp", "inst"), "slab", None),
            P(("grp", "inst"), None, "slab", None),
            P(("grp", "inst"), None, "slab", None),
            P("slab", None),
            P(),
        ),
        out_specs=P(("grp", "inst"), None, "slab", None),
        check_vma=False,
    )
```

time: 73.5 us -> 37.6 us (0.51)
  matrix products: 16.5 us -> 0 us
  between operations: 13.9 us -> 0.12 us
  starting transfers between devices: 6.09 us -> 16.2 us
  other arithmetic: 8.2 us -> 0 us
  blocking collectives: 7.77 us -> 0 us
  Pallas kernels: 0 us -> 6.82 us
  local copies, waits for them, and re-layouts: 8.29 us -> 2.19 us
    dot_general x11 -> x0, matrix products: 16.5 us -> none  [the longest x2 8.48 us: body(): jnp.einsum('m,mvac->vac', coefficients, block_part, precision=lax.Precisi...]
    ppermute x4 -> x10, starting transfers between devices: 6.05 us -> 16.2 us  [the longest x4 11.3 us: to_edge(): return lax.ppermute(x, ('inst', 'slab'), pairs)]
    ppermute x4 -> x10, waiting for transfers between devices: 3.38 us -> 11.9 us  [the longest x4 7.57 us: to_edge(): return lax.ppermute(x, ('inst', 'slab'), pairs)]
    all_gather x2 -> x0, waiting for transfers between devices: 8.17 us -> none  [body(): block_part = lax.all_gather(flow_field, 'inst', axis=0, tiled=True)]
    all_gather x1 -> x0, blocking collectives: 7.77 us -> none  [body(): volume_block_part = lax.all_gather(volumes, 'inst', axis=0, tiled=True)]
    pallas_call x0 -> x3, Pallas kernels: none -> 6.82 us  [the longest x1 2.89 us: body(): pl.pallas_call(functools.partial(compute_kernel, n, rows, nvar, ITERS), o...]
    sort x1 -> x0, other arithmetic: 3.84 us -> none  [body(): order_own = jnp.argsort(links_own)]
    gather x8 -> x0, local copies, waits for them, and re-layouts: 3.22 us -> none  [the longest x4 1.62 us: body(): sent_flux = jnp.take(row_flux[:, :, 0, :], order_own, axis=2)]
  transfers between devices with their start and end apart: 6 -> 10, of which waited for: 2 -> 6; matrix products, arithmetic and copies ran while one was open for 41% -> 0% of each run, Pallas kernels for 0% -> 0%
where the time goes in v1:
time: 37.6 us; the launch traced here: 37.3 us
  starting transfers between devices  16.2 us (43%)
  waiting for transfers between devices  11.9 us (32%)
  Pallas kernels  6.82 us (18%)
  local copies, waits for them, and re-layouts  2.19 us (6%)
    ppermute x4, starting transfers between devices, to_edge(): return lax.ppermute(x, ('inst', 'slab'), pairs)  11.3 us
    ppermute x4, waiting for transfers between devices, to_edge(): return lax.ppermute(x, ('inst', 'slab'), pairs)  7.57 us
    ppermute x6, starting transfers between devices, swapped(): return lax.ppermute(x, 'inst', [(i, i ^ k) for i in range(n)])  4.97 us
    ppermute x6, waiting for transfers between devices, swapped(): return lax.ppermute(x, 'inst', [(i, i ^ k) for i in range(n)])  4.37 us
    pallas_call x1, Pallas kernels, body(): pl.pallas_call(functools.partial(compute_kernel, n, rows, nvar, ITERS), o...  2.89 us
    unnamed x17, local copies, waits for them, and re-layouts  2.19 us
    pallas_call x1, Pallas kernels, body(): pl.pallas_call(functools.partial(pack_kernel, n, rows), out_shape=[f32(bu...  2.16 us
    pallas_call x1, Pallas kernels, body(): pl.pallas_call(functools.partial(unpack_kernel, n, rows), out_shape=f32(1...  1.76 us
  transfers between devices with their start and end apart: 10, of which 6 were waited for; matrix products, arithmetic and copies ran while one was open for 0% of the time, Pallas kernels for 0%

profile of v1, /device:TPU:0, one launch (start us, length us, event | category | flops | bytes accessed | tf_op | source)
XLA Modules:
  0.0 37.3 jit_solution(4427305442367982637)
XLA Ops:
  0.0 2.2 %pack.1 = (f32[192,256]{1,0:T(8,128)}, f32[192,256]{1,0:T(8,128)}, f32[192,256]{1,0:T(8,128)}, f32[192,256]{1,0:T(8,128)}, f32[24,256]{1,0:T(8,128)}, /*index=5*...) custom-call(f32[1,5,64,256]{3,2,1,0:T(8,128)} %states.1, f32[1,64,256]{2,1,0:T(8,128)} %volumes.1, ...), custom_call_target="tpu_custom_call" | custom-call | tf_op jit(solution)/shard_map/pack/pallas_call | solution.py:290
  2.2 0.5 %collective-permute-start = (f32[192,256]{1,0:T(8,128)}, f32[192,256]{1,0:T(8,128)S(1)}, u32[]{:S(2)}, u32[]{:S(2)}) collective-permute-start(f32[192,256]{1,0:T(8,128)} %get-tuple-element.18), channel_id=1, source_target_pairs={{0,4},{4,0},{8,12},{12,8},{1,5},{5,1},{9,13},{13,9},{2,6},{6,2},{1... | collective-permute-start | bytes 589832 | tf_op jit(solution)/shard_map/ppermute | solution.py:300
  2.6 2.6 %collective-permute-start.1 = (f32[192,256]{1,0:T(8,128)}, f32[192,256]{1,0:T(8,128)S(1)}, u32[]{:S(2)}, u32[]{:S(2)}) collective-permute-start(f32[192,256]{1,0:T(8,128)} %get-tuple-element.19), channel_id=1, source_target_pairs={{0,8},{4,12},{8,0},{12,4},{1,9},{5,13},{9,1},{13,5},{2,10},{6,14},... | collective-permute-start | bytes 589832 | tf_op jit(solution)/shard_map/ppermute | solution.py:300
  5.2 0.1 collective-permute-start.2
  5.3 3.7 %collective-permute-start.3 = (f32[24,256]{1,0:T(8,128)}, f32[24,256]{1,0:T(8,128)S(1)}, u32[]{:S(2)}, u32[]{:S(2)}) collective-permute-start(f32[24,256]{1,0:T(8,128)} %get-tuple-element.21), channel_id=1, source_target_pairs={{0,1},{12,15},{1,2},{13,12},{2,3},{14,13},{3,0},{15,14},{16,17},{2... | collective-permute-start | bytes 73736 | tf_op jit(solution)/shard_map/ppermute | solution.py:309
  9.0 1.3 %collective-permute-start.4 = (f32[24,256]{1,0:T(8,128)}, f32[24,256]{1,0:T(8,128)S(1)}, u32[]{:S(2)}, u32[]{:S(2)}) collective-permute-start(f32[24,256]{1,0:T(8,128)} %get-tuple-element.22), channel_id=1, source_target_pairs={{4,1},{8,15},{5,2},{9,12},{6,3},{10,13},{7,0},{11,14},{20,17},{24,... | collective-permute-start | bytes 73736 | tf_op jit(solution)/shard_map/ppermute | solution.py:309
  10.3 2.7 %collective-permute-done.3.refs_4_ = f32[24,256]{1,0:T(8,128)S(1)} collective-permute-done((f32[24,256]{1,0:T(8,128)}, f32[24,256]{1,0:T(8,128)S(1)}, u32[]{:S(2)}, u32[]{:S(2)}) %collective-permute-start.3) | collective-permute-done | bytes 24608 | tf_op jit(solution)/shard_map/ppermute | solution.py:309
  13.0 1.3 %collective-permute-start.5 = (f32[24,256]{1,0:T(8,128)}, f32[24,256]{1,0:T(8,128)S(1)}, u32[]{:S(2)}, u32[]{:S(2)}) collective-permute-start(f32[24,256]{1,0:T(8,128)} %get-tuple-element.23), channel_id=1, source_target_pairs={{8,1},{4,15},{9,2},{5,12},{10,3},{6,13},{11,0},{7,14},{24,17},{20,... | collective-permute-start | bytes 73736 | tf_op jit(solution)/shard_map/ppermute | solution.py:309
  14.3 1.8 %collective-permute-done.4.refs_5_ = f32[24,256]{1,0:T(8,128)S(1)} collective-permute-done((f32[24,256]{1,0:T(8,128)}, f32[24,256]{1,0:T(8,128)S(1)}, u32[]{:S(2)}, u32[]{:S(2)}) %collective-permute-start.4) | collective-permute-done | bytes 24608 | tf_op jit(solution)/shard_map/ppermute | solution.py:309
  16.1 5.0 %collective-permute-start.6 = (f32[24,256]{1,0:T(8,128)}, f32[24,256]{1,0:T(8,128)S(1)}, u32[]{:S(2)}, u32[]{:S(2)}) collective-permute-start(f32[24,256]{1,0:T(8,128)} %get-tuple-element.24), channel_id=1, source_target_pairs={{12,1},{0,15},{13,2},{1,12},{14,3},{2,13},{15,0},{3,14},{28,17},{1... | collective-permute-start | bytes 73736 | tf_op jit(solution)/shard_map/ppermute | solution.py:309
  21.1 0.0 copy-done.7
  21.1 0.0 copy-start.3
  21.2 0.0 copy-start.2
  21.2 0.5 %collective-permute-done.5.refs_6_ = f32[24,256]{1,0:T(8,128)S(1)} collective-permute-done((f32[24,256]{1,0:T(8,128)}, f32[24,256]{1,0:T(8,128)S(1)}, u32[]{:S(2)}, u32[]{:S(2)}) %collective-permute-start.5) | collective-permute-done | bytes 24608 | tf_op jit(solution)/shard_map/ppermute | solution.py:309
  21.6 2.6 %collective-permute-done.6.refs_7_ = f32[24,256]{1,0:T(8,128)S(1)} collective-permute-done((f32[24,256]{1,0:T(8,128)}, f32[24,256]{1,0:T(8,128)S(1)}, u32[]{:S(2)}, u32[]{:S(2)}) %collective-permute-start.6) | collective-permute-done | bytes 24608 | tf_op jit(solution)/shard_map/ppermute | solution.py:309
  24.2 0.0 collective-permute-done.refs_1_
  24.2 0.0 collective-permute-done.1.refs_2_
  24.2 0.0 collective-permute-done.2.refs_3_
  24.2 0.0 copy-start
  24.2 0.9 %copy-done = f32[192,256]{1,0:T(8,128)S(1)} copy-done((f32[192,256]{1,0:T(8,128)S(1)}, f32[192,256]{1,0:T(8,128)}, u32[]{:S(2)}) %copy-start) | copy-done | bytes 196632
  25.1 2.9 %iterate.1 = (f32[5,16,256]{2,1,0:T(8,128)S(1)}, f32[5,16,256]{2,1,0:T(8,128)S(1)}, f32[5,16,256]{2,1,0:T(8,128)S(1)}, f32[5,16,256]{2,1,0:T(8,128)S(1)}) custom-call(f32[4,4]{1,0:T(4,128)S(1)} %copy-done.3, f32[2,5,5]{2,1,0:T(8,128)S(1)} %copy.8.jacobians, s32[1,256]{1,0:T(1,128)S(1)} %copy-done.2, f32[192,256]{1,0:T(8,128)S(1)} %copy-done, ...), custom_call_target="tpu_custom_call" | custom-call | tf_op jit(solution)/shard_map/iterate/pallas_call | solution.py:313
  28.0 0.0 copy-start.1
  28.1 0.6 %copy-done.1 = f32[5,16,256]{2,1,0:T(8,128)} copy-done((f32[5,16,256]{2,1,0:T(8,128)}, f32[5,16,256]{2,1,0:T(8,128)S(1)}, u32[]{:S(2)}) %copy-start.1) | copy-done | bytes 81944
  28.7 0.0 collective-permute-start.7
  28.7 0.0 collective-permute-start.8
  28.7 1.9 %collective-permute-start.9 = (f32[5,16,256]{2,1,0:T(8,128)S(1)}, f32[5,16,256]{2,1,0:T(8,128)S(1)}, u32[]{:S(2)}, u32[]{:S(2)}) collective-permute-start(f32[5,16,256]{2,1,0:T(8,128)S(1)} %get-tuple-element.28), channel_id=1, source_target_pairs={{0,12},{4,8},{8,4},{12,0},{1,13},{5,9},{9,5},{13,1},{2,14},{6,10},... | collective-permute-start | bytes 245768 | tf_op jit(solution)/shard_map/ppermute | solution.py:300
  30.5 0.0 collective-permute-done.7.refs_1_
  30.5 3.4 %collective-permute-done.8.refs_2_ = f32[5,16,256]{2,1,0:T(8,128)S(1)} collective-permute-done((f32[5,16,256]{2,1,0:T(8,128)S(1)}, f32[5,16,256]{2,1,0:T(8,128)S(1)}, u32[]{:S(2)}, u32[]{:S(2)}) %collective-permute-start.8) | collective-permute-done | bytes 81952 | tf_op jit(solution)/shard_map/ppermute | solution.py:300
  33.9 1.0 %collective-permute-done.9.refs_3_ = f32[5,16,256]{2,1,0:T(8,128)S(1)} collective-permute-done((f32[5,16,256]{2,1,0:T(8,128)S(1)}, f32[5,16,256]{2,1,0:T(8,128)S(1)}, u32[]{:S(2)}, u32[]{:S(2)}) %collective-permute-start.9) | collective-permute-done | bytes 81952 | tf_op jit(solution)/shard_map/ppermute | solution.py:300
  34.9 0.0 copy-done.5
  34.9 0.6 %copy-done.6 = f32[5,16,256]{2,1,0:T(8,128)} copy-done((f32[5,16,256]{2,1,0:T(8,128)}, f32[5,16,256]{2,1,0:T(8,128)S(1)}, u32[]{:S(2)}) %copy-start.6) | copy-done | bytes 81944
  35.5 1.8 %unpack.1 = f32[1,5,64,256]{3,2,1,0:T(8,128)} custom-call(f32[5,16,256]{2,1,0:T(8,128)} %copy-done.1, f32[5,16,256]{2,1,0:T(8,128)} %copy-done.4, f32[5,16,256]{2,1,0:T(8,128)} %copy-done.5, f32[5,16,256]{2,1,0:T(8,128)} %copy-done.6), custom_call_target="tpu_custom_call" | custom-call | tf_op jit(solution)/shard_map/unpack/pallas_call | solution.py:328
  (8 shorter events, 0.0 us)
Async XLA Ops:
  2.2 22.0 %collective-permute-start = (f32[192,256]{1,0:T(8,128)}, f32[192,256]{1,0:T(8,128)S(1)}, u32[]{:S(2)}, u32[]{:S(2)}) collective-permute-start(f32[192,256]{1,0:T(8,128)} %get-tuple-element.18), channel_id=1, source_target_pairs={{0,4},{4,0},{8,12},{12,8},{1,5},{5,1},{9,13},{13,9},{2,6},{6,2},{1... | collective-permute-start | bytes 589832 | tf_op jit(solution)/shard_map/ppermute | solution.py:300
  2.6 18.5 %copy-start.7 = (f32[2,5,5]{2,0,1:T(2,128)S(1)}, f32[2,5,5]{2,0,1:T(2,128)}, u32[]{:S(2)}) copy-start(f32[2,5,5]{2,0,1:T(2,128)} %param.12) | copy-start | bytes 604
  2.6 21.6 %collective-permute-start.1 = (f32[192,256]{1,0:T(8,128)}, f32[192,256]{1,0:T(8,128)S(1)}, u32[]{:S(2)}, u32[]{:S(2)}) collective-permute-start(f32[192,256]{1,0:T(8,128)} %get-tuple-element.19), channel_id=1, source_target_pairs={{0,8},{4,12},{8,0},{12,4},{1,9},{5,13},{9,1},{13,5},{2,10},{6,14},... | collective-permute-start | bytes 589832 | tf_op jit(solution)/shard_map/ppermute | solution.py:300
  5.2 19.0 %collective-permute-start.2 = (f32[192,256]{1,0:T(8,128)}, f32[192,256]{1,0:T(8,128)S(1)}, u32[]{:S(2)}, u32[]{:S(2)}) collective-permute-start(f32[192,256]{1,0:T(8,128)} %get-tuple-element.20), channel_id=1, source_target_pairs={{0,12},{4,8},{8,4},{12,0},{1,13},{5,9},{9,5},{13,1},{2,14},{6,10},... | collective-permute-start | bytes 589832 | tf_op jit(solution)/shard_map/ppermute | solution.py:300
  5.3 7.7 %collective-permute-start.3 = (f32[24,256]{1,0:T(8,128)}, f32[24,256]{1,0:T(8,128)S(1)}, u32[]{:S(2)}, u32[]{:S(2)}) collective-permute-start(f32[24,256]{1,0:T(8,128)} %get-tuple-element.21), channel_id=1, source_target_pairs={{0,1},{12,15},{1,2},{13,12},{2,3},{14,13},{3,0},{15,14},{16,17},{2... | collective-permute-start | bytes 73736 | tf_op jit(solution)/shard_map/ppermute | solution.py:309
  9.0 7.2 %collective-permute-start.4 = (f32[24,256]{1,0:T(8,128)}, f32[24,256]{1,0:T(8,128)S(1)}, u32[]{:S(2)}, u32[]{:S(2)}) collective-permute-start(f32[24,256]{1,0:T(8,128)} %get-tuple-element.22), channel_id=1, source_target_pairs={{4,1},{8,15},{5,2},{9,12},{6,3},{10,13},{7,0},{11,14},{20,17},{24,... | collective-permute-start | bytes 73736 | tf_op jit(solution)/shard_map/ppermute | solution.py:309
  13.0 8.6 %collective-permute-start.5 = (f32[24,256]{1,0:T(8,128)}, f32[24,256]{1,0:T(8,128)S(1)}, u32[]{:S(2)}, u32[]{:S(2)}) collective-permute-start(f32[24,256]{1,0:T(8,128)} %get-tuple-element.23), channel_id=1, source_target_pairs={{8,1},{4,15},{9,2},{5,12},{10,3},{6,13},{11,0},{7,14},{24,17},{20,... | collective-permute-start | bytes 73736 | tf_op jit(solution)/shard_map/ppermute | solution.py:309
  16.1 8.0 %collective-permute-start.6 = (f32[24,256]{1,0:T(8,128)}, f32[24,256]{1,0:T(8,128)S(1)}, u32[]{:S(2)}, u32[]{:S(2)}) collective-permute-start(f32[24,256]{1,0:T(8,128)} %get-tuple-element.24), channel_id=1, source_target_pairs={{12,1},{0,15},{13,2},{1,12},{14,3},{2,13},{15,0},{3,14},{28,17},{1... | collective-permute-start | bytes 73736 | tf_op jit(solution)/shard_map/ppermute | solution.py:309
  21.1 3.1 %copy-start.3 = (f32[4,4]{1,0:T(4,128)S(1)}, f32[4,4]{1,0:T(4,128)}, u32[]{:S(2)}) copy-start(f32[4,4]{1,0:T(4,128)} %constant.2.clone.table) | copy-start | bytes 196
  21.2 3.0 %copy-start.2 = (s32[1,256]{1,0:T(1,128)S(1)}, s32[1,256]{1,0:T(1,128)}, u32[]{:S(2)}) copy-start(s32[1,256]{1,0:T(1,128)} %links.3) | copy-start | bytes 3076
  24.2 0.9 %copy-start = (f32[192,256]{1,0:T(8,128)S(1)}, f32[192,256]{1,0:T(8,128)}, u32[]{:S(2)}) copy-start(f32[192,256]{1,0:T(8,128)} %get-tuple-element.17.refs_0_) | copy-start | bytes 589828
  28.0 0.6 %copy-start.1 = (f32[5,16,256]{2,1,0:T(8,128)}, f32[5,16,256]{2,1,0:T(8,128)S(1)}, u32[]{:S(2)}) copy-start(f32[5,16,256]{2,1,0:T(8,128)S(1)} %get-tuple-element.25.refs_0_) | copy-start | bytes 245764
  28.7 1.9 %collective-permute-start.7 = (f32[5,16,256]{2,1,0:T(8,128)S(1)}, f32[5,16,256]{2,1,0:T(8,128)S(1)}, u32[]{:S(2)}, u32[]{:S(2)}) collective-permute-start(f32[5,16,256]{2,1,0:T(8,128)S(1)} %get-tuple-element.26), channel_id=1, source_target_pairs={{0,4},{4,0},{8,12},{12,8},{1,5},{5,1},{9,13},{13,9},{2,6},{6,2},{1... | collective-permute-start | bytes 245768 | tf_op jit(solution)/shard_map/ppermute | solution.py:300
  28.7 5.2 %collective-permute-start.8 = (f32[5,16,256]{2,1,0:T(8,128)S(1)}, f32[5,16,256]{2,1,0:T(8,128)S(1)}, u32[]{:S(2)}, u32[]{:S(2)}) collective-permute-start(f32[5,16,256]{2,1,0:T(8,128)S(1)} %get-tuple-element.27), channel_id=1, source_target_pairs={{0,8},{4,12},{8,0},{12,4},{1,9},{5,13},{9,1},{13,5},{2,10},{6,14},... | collective-permute-start | bytes 245768 | tf_op jit(solution)/shard_map/ppermute | solution.py:300
  28.7 6.2 %collective-permute-start.9 = (f32[5,16,256]{2,1,0:T(8,128)S(1)}, f32[5,16,256]{2,1,0:T(8,128)S(1)}, u32[]{:S(2)}, u32[]{:S(2)}) collective-permute-start(f32[5,16,256]{2,1,0:T(8,128)S(1)} %get-tuple-element.28), channel_id=1, source_target_pairs={{0,12},{4,8},{8,4},{12,0},{1,13},{5,9},{9,5},{13,1},{2,14},{6,10},... | collective-permute-start | bytes 245768 | tf_op jit(solution)/shard_map/ppermute | solution.py:300
  30.5 4.4 %copy-start.4 = (f32[5,16,256]{2,1,0:T(8,128)}, f32[5,16,256]{2,1,0:T(8,128)S(1)}, u32[]{:S(2)}) copy-start(f32[5,16,256]{2,1,0:T(8,128)S(1)} %collective-permute-done.7.refs_1_) | copy-start | bytes 245764
  33.9 1.0 %copy-start.5 = (f32[5,16,256]{2,1,0:T(8,128)}, f32[5,16,256]{2,1,0:T(8,128)S(1)}, u32[]{:S(2)}) copy-start(f32[5,16,256]{2,1,0:T(8,128)S(1)} %collective-permute-done.8.refs_2_) | copy-start | bytes 245764
  34.9 0.6 %copy-start.6 = (f32[5,16,256]{2,1,0:T(8,128)}, f32[5,16,256]{2,1,0:T(8,128)S(1)}, u32[]{:S(2)}) copy-start(f32[5,16,256]{2,1,0:T(8,128)S(1)} %collective-permute-done.9.refs_3_) | copy-start | bytes 245764

commit v2 on v1

v2 whole, which is shorter than its diff:
```python
import functools

import jax
import jax.numpy as jnp
import numpy as np
from jax import lax
from jax.experimental import pallas as pl
from jax.experimental.pallas import tpu as pltpu
from jax.sharding import PartitionSpec as P

frequency = 0.5
pseudo_step = 0.2
nyquist_damping = 0.25


def spectral_table(instances):
    offsets = np.arange(instances)[:, None] - np.arange(instances)[None, :]
    phases = np.pi * offsets / instances
    sine_safe = np.where(offsets == 0, 1.0, np.sin(phases))
    parity = np.where(offsets % 2 == 0, 1.0, -1.0)
    matrix = np.where(offsets == 0, 0.0, 0.5 * frequency * parity * np.cos(phases) / sine_safe)
    matrix = matrix + nyquist_damping * parity
    return jnp.asarray(matrix, jnp.float32)


def row_step(rows):
    return rows if rows % 8 == 0 else 1


def pack_kernel(n, rows, *refs):
    sources, bufs, upward, downward, own_links = refs[:5], refs[5 : 5 + n], refs[5 + n], refs[6 + n], refs[7 + n]
    held, sems = refs[8 + n : 13 + n], refs[13 + n]
    copies = [pltpu.make_async_copy(sources[a], held[a], sems.at[a]) for a in range(5)]
    for copy in copies:
        copy.start()
    for copy in copies:
        copy.wait()
    states, volumes, row_normals, col_normals, links = held
    nvar, depth = states.shape[1], states.shape[2]
    me = lax.axis_index("inst")

    def put(ref, at, row_below, row_in, row_outer):
        for v in range(nvar):
            ref[pl.ds(at + v, 1), :] = states[0, v, pl.ds(row_below, 1), :]
            ref[pl.ds(at + nvar + v, 1), :] = states[0, v, pl.ds(row_in, 1), :]
        at = at + 2 * nvar
        ref[pl.ds(at, 1), :] = volumes[0, pl.ds(row_in, 1), :]
        for d in range(2):
            ref[pl.ds(at + 1 + d, 1), :] = row_normals[0, d, pl.ds(row_outer, 1), :]
            ref[pl.ds(at + 3 + d, 1), :] = col_normals[0, d, pl.ds(row_in, 1), :]

    def put_inner(ref, at, row):
        for d in range(2):
            ref[pl.ds(at + d, 1), :] = row_normals[0, d, pl.ds(row, 1), :]

    for k in range(n):
        buf = bufs[k]
        block = jnp.bitwise_xor(me, k)
        lo = pl.multiple_of(block * rows, rows)
        step = row_step(rows)
        for r in range(0, rows, step):
            here = pl.ds(lo + r, step)
            for v in range(nvar):
                buf[pl.ds(v * rows + r, step), :] = states[0, v, here, :]
            buf[pl.ds(nvar * rows + r, step), :] = volumes[0, here, :]
            for d in range(2):
                buf[pl.ds((nvar + 1 + d) * rows + r, step), :] = row_normals[0, d, here, :]
                buf[pl.ds((nvar + 3 + d) * rows + r, step), :] = col_normals[0, d, here, :]
        at = (nvar + 5) * rows
        below_1, below_2 = jnp.maximum(lo - 1, 0), jnp.maximum(lo - 2, 0)
        above_1, above_2 = jnp.minimum(lo + rows, depth - 1), jnp.minimum(lo + rows + 1, depth - 1)
        put(buf, at, below_2, below_1, below_1)
        at += 2 * nvar + 5
        put(buf, at, above_2, above_1, above_2)
        put_inner(buf, at + 2 * nvar + 5, above_1)
    own_links[...] = links[...]
    put(upward, 0, depth - 2, depth - 1, depth - 1)
    put(downward, 0, 1, 0, 1)
    put_inner(downward, 2 * nvar + 5, 0)
    downward[pl.ds(2 * nvar + 7, 1), :] = links[...].astype(jnp.float32)


def edge_kernel(n, below, above, *outs):
    me = lax.axis_index("inst")
    for k in range(n):
        outs[k][...] = jnp.where(jnp.bitwise_xor(me, k) == 0, below[...], above[...])


def split_dot(x, onehot, transposed):
    high = x.astype(jnp.bfloat16)
    rest = x - high.astype(jnp.float32)
    middle = rest.astype(jnp.bfloat16)
    low = (rest - middle.astype(jnp.float32)).astype(jnp.bfloat16)
    count = x.shape[0]
    stacked = jnp.concatenate([high, middle, low], axis=0)
    out = lax.dot_general(
        stacked,
        onehot,
        (((1,), (1 if transposed else 0,)), ((), ())),
        preferred_element_type=jnp.float32,
    )
    return out[:count] + (out[count : 2 * count] + out[2 * count :])


def half_jacobians(jacobians, nvar):
    return [[[0.5 * jacobians[d, v, w] for w in range(nvar)] for v in range(nvar)] for d in range(2)]


def step_weights(table, n):
    me = lax.axis_index("inst")
    return [
        [pseudo_step * table[jnp.bitwise_xor(me, k), jnp.bitwise_xor(me, j)] for j in range(n)]
        for k in range(n)
    ]


def transformed(half, values):
    count = len(values)
    return [
        [sum(half[d][v][w] * values[w] for w in range(count)) for v in range(count)] for d in range(2)
    ]


def face_flux(normal, lower, lower_j, upper, upper_j):
    spread = 0.5 * (jnp.abs(normal[0]) + jnp.abs(normal[1]))
    return [
        normal[0] * (lower_j[0][v] + upper_j[0][v])
        + normal[1] * (lower_j[1][v] + upper_j[1][v])
        - spread * (upper[v] - lower[v])
        for v in range(len(lower))
    ]


def col_change(normal, values, values_j):
    columns = values[0].shape[1]
    left = [pltpu.roll(x, 1, 1) for x in values]
    left_j = [[pltpu.roll(x, 1, 1) for x in values_j[d]] for d in range(2)]
    across = face_flux(normal, left, left_j, values, values_j)
    return [pltpu.roll(x, columns - 1, 1) - x for x in across]


def advance_main(k, rows, half, weights, bufs, cells, first_flux, last_flux, store):
    n, nvar = len(bufs), len(half[0])
    columns = bufs[0].shape[1]
    row_index = lax.broadcasted_iota(jnp.int32, (rows, columns), 0)

    def plane(j, p):
        return bufs[j][pl.ds(p * rows, rows), :]

    values = [cells(k, v) for v in range(nvar)]
    values_j = transformed(half, values)
    shifted = [pltpu.roll(x, 1, 0) for x in values]
    shifted_j = [[pltpu.roll(x, 1, 0) for x in values_j[d]] for d in range(2)]
    row_flux = face_flux([plane(k, nvar + 1), plane(k, nvar + 2)], shifted, shifted_j, values, values_j)
    row_flux = [jnp.where(row_index == 0, first_flux(v), row_flux[v]) for v in range(nvar)]
    row_above = [
        jnp.where(row_index == rows - 1, last_flux(v), pltpu.roll(row_flux[v], rows - 1, 0))
        for v in range(nvar)
    ]
    beside = col_change([plane(k, nvar + 3), plane(k, nvar + 4)], values, values_j)
    inverse = 1.0 / plane(k, nvar)
    volume_rate = sum(weights[k][j] * plane(j, nvar) for j in range(n))
    for v in range(nvar):
        time_rate = sum(weights[k][j] * cells(j, v) for j in range(n))
        change = pseudo_step * ((row_above[v] - row_flux[v]) + beside[v])
        store(v, values[v] - time_rate - inverse * (values[v] * volume_rate + change))


def first_kernel(n, rows, nvar, table, jacobians, *refs):
    bufs, outs = refs[:n], refs[n:]
    half, weights = half_jacobians(jacobians, nvar), step_weights(table, n)

    def cells(k, v):
        return bufs[k][pl.ds(v * rows, rows), :]

    for k in range(n):

        def store(v, value):
            outs[k][v] = value

        advance_main(k, rows, half, weights, bufs, cells, lambda v: 0.0, lambda v: 0.0, store)


def second_kernel(n, rows, nvar, table, jacobians, links, *refs):
    bufs, edges, stepped, outs = refs[:n], refs[n : 2 * n], refs[2 * n : 3 * n], refs[3 * n : 4 * n]
    halo, rim, flow = refs[4 * n :]
    columns = links.shape[1]
    main = (nvar + 5) * rows
    below_at, above_at = main, main + 2 * nvar + 5
    me = lax.axis_index("inst")
    first, last = me == 0, me == n - 1
    half, weights = half_jacobians(jacobians, nvar), step_weights(table, n)

    for k in range(n):
        for t in range(2 * nvar + 5):
            halo[t, pl.ds(k, 1), :] = jnp.where(
                first, edges[k][pl.ds(t, 1), :], bufs[k][pl.ds(below_at + t, 1), :]
            )
        for t in range(2 * nvar + 7):
            halo[t, pl.ds(n + k, 1), :] = jnp.where(
                last, edges[k][pl.ds(t, 1), :], bufs[k][pl.ds(above_at + t, 1), :]
            )
        for d in range(2):
            halo[2 * nvar + 5 + d, pl.ds(k, 1), :] = bufs[k][pl.ds((nvar + 1 + d) * rows, 1), :]
        for v in range(nvar + 1):
            rim[v, pl.ds(k, 1), :] = bufs[k][pl.ds(v * rows, 1), :]
            rim[v, pl.ds(n + k, 1), :] = bufs[k][pl.ds(v * rows + rows - 1, 1), :]
        for v in range(nvar):
            flow[k, v] = stepped[k][v]

    own = lax.broadcasted_iota(jnp.int32, (1, columns), 1)
    cell = lax.broadcasted_iota(jnp.int32, (columns, columns), 0)
    links_above = edges[0][pl.ds(2 * nvar + 7, 1), :].astype(jnp.int32)
    onehot_below = (cell == jnp.where(first, links[...], own)).astype(jnp.float32).astype(jnp.bfloat16)
    onehot_above = (cell == jnp.where(last, links_above, own)).astype(jnp.float32).astype(jnp.bfloat16)
    side = lax.broadcasted_iota(jnp.int32, (2 * n, columns), 0)
    is_below = side < n
    place = jnp.where(is_below, side, side - n)

    def crossed(values, back):
        stacked = jnp.concatenate(values, axis=0)
        through_below = split_dot(stacked, onehot_below, back)
        through_above = split_dot(stacked, onehot_above, back)
        return [
            jnp.where(
                is_below,
                through_below[2 * n * v : 2 * n * (v + 1)],
                through_above[2 * n * v : 2 * n * (v + 1)],
            )
            for v in range(nvar)
        ]

    def pick(mask, a, b):
        return [jnp.where(mask, x, y) for x, y in zip(a, b)]

    factors = []
    for j in range(n):
        factor = jnp.zeros((2 * n, columns), jnp.float32)
        for k in range(n):
            factor = jnp.where(place == k, weights[k][j], factor)
        factors.append(factor)

    def spread_sum(x):
        return sum(
            factors[j] * jnp.where(is_below, x[j : j + 1], x[n + j : n + j + 1]) for j in range(n)
        )

    inner_face = [halo[2 * nvar + 5], halo[2 * nvar + 6]]

    def through_inner(inner, edge):
        lower = crossed(pick(is_below, inner, edge), False)
        upper = pick(is_below, edge, inner)
        across = face_flux(inner_face, lower, transformed(half, lower), upper, transformed(half, upper))
        return across, crossed(across, True)

    inner = [halo[nvar + v] for v in range(nvar)]
    flux_inner, flux_back = through_inner(inner, [rim[v] for v in range(nvar)])

    rim_inverse = pseudo_step / rim[nvar]
    for v in range(nvar):
        rim[v] = rim_inverse * jnp.where(is_below, flux_inner[v], -flux_back[v])
        for k in range(n):
            flow[k, v, pl.ds(0, 1), :] += rim[v, pl.ds(k, 1), :]
            flow[k, v, pl.ds(rows - 1, 1), :] += rim[v, pl.ds(n + k, 1), :]
            rim[v, pl.ds(k, 1), :] = flow[k, v, pl.ds(0, 1), :]
            rim[v, pl.ds(n + k, 1), :] = flow[k, v, pl.ds(rows - 1, 1), :]

    outer = [halo[v] for v in range(nvar)]
    low, high = pick(is_below, outer, inner), pick(is_below, inner, outer)
    outer_face = [halo[2 * nvar + 1], halo[2 * nvar + 2]]
    flux_outer = face_flux(outer_face, low, transformed(half, low), high, transformed(half, high))
    inner_col = [halo[2 * nvar + 3], halo[2 * nvar + 4]]
    beside = col_change(inner_col, inner, transformed(half, inner))
    volume = halo[2 * nvar]
    inverse = 1.0 / volume
    volume_rate = spread_sum(volume)
    stepped_inner = []
    for v in range(nvar):
        change = jnp.where(is_below, flux_back[v] - flux_outer[v], flux_outer[v] - flux_inner[v]) + beside[v]
        stepped_inner.append(
            inner[v] - spread_sum(inner[v]) - inverse * (inner[v] * volume_rate + pseudo_step * change)
        )
    flux_inner, flux_back = through_inner(stepped_inner, [rim[v] for v in range(nvar)])

    def cells(k, v):
        return flow[k, v]

    for k in range(n):

        def store(v, value):
            outs[k][v] = value

        advance_main(
            k,
            rows,
            half,
            weights,
            bufs,
            cells,
            lambda v: flux_inner[v][k : k + 1],
            lambda v: flux_back[v][n + k : n + k + 1],
            store,
        )


def unpack_kernel(n, rows, *refs):
    blocks, out = refs[:n], refs[n]
    me = lax.axis_index("inst")
    for k in range(n):
        block = jnp.bitwise_xor(me, k)
        lo = pl.multiple_of(block * rows, rows)
        step = row_step(rows)
        for v in range(out.shape[1]):
            for r in range(0, rows, step):
                out[0, v, pl.ds(lo + r, step), :] = blocks[k][v, pl.ds(r, step), :]


def body(states, volumes, row_normals, col_normals, face_links, jacobians):
    n = lax.axis_size("inst")
    slabs = lax.axis_size("slab")
    _, nvar, depth, columns = states.shape
    rows = depth // n
    buffer_rows = (nvar + 5) * rows + 4 * nvar + 12
    edge_rows = -(-(2 * nvar + 8) // 8) * 8

    def f32(*shape):
        return jax.ShapeDtypeStruct(shape, jnp.float32)

    params = pltpu.CompilerParams(vmem_limit_bytes=24 * 1024 * 1024)
    vmem = pl.BlockSpec(memory_space=pltpu.VMEM)
    smem = pl.BlockSpec(memory_space=pltpu.SMEM)

    inputs = [
        pltpu.with_memory_space_constraint(x, pltpu.HBM)
        for x in (states, volumes, row_normals, col_normals, face_links)
    ]
    packed = pl.pallas_call(
        functools.partial(pack_kernel, n, rows),
        out_shape=[f32(buffer_rows, columns)] * n + [f32(edge_rows, columns)] * 2
        + [jax.ShapeDtypeStruct(face_links.shape, face_links.dtype)],
        in_specs=[pl.BlockSpec(memory_space=pltpu.HBM)] * 5,
        out_specs=[vmem] * (n + 3),
        scratch_shapes=[pltpu.VMEM(x.shape, x.dtype) for x in inputs] + [pltpu.SemaphoreType.DMA((5,))],
        compiler_params=params,
        name="pack",
    )(*inputs)
    sent, (upward, downward, own_links) = packed[:n], packed[n:]

    def swapped(x, k):
        return lax.ppermute(x, "inst", [(i, i ^ k) for i in range(n)])

    received = [sent[0]] + [swapped(sent[k], k) for k in range(1, n)]
    from_below = lax.ppermute(upward, "slab", [(i, (i + 1) % slabs) for i in range(slabs)])
    from_above = lax.ppermute(downward, "slab", [(i, (i - 1) % slabs) for i in range(slabs)])
    edges = pl.pallas_call(
        functools.partial(edge_kernel, n),
        out_shape=[f32(edge_rows, columns)] * n,
        in_specs=[vmem] * 2,
        out_specs=[vmem] * n,
        compiler_params=params,
        name="edges",
    )(from_below, from_above)
    edges = [edges[0]] + [swapped(edges[k], k) for k in range(1, n)]

    table = spectral_table(n)
    stepped = pl.pallas_call(
        functools.partial(first_kernel, n, rows, nvar),
        out_shape=[f32(nvar, rows, columns)] * n,
        in_specs=[smem, smem] + [vmem] * n,
        out_specs=[vmem] * n,
        compiler_params=params,
        name="first",
    )(table, jacobians, *received)
    results = pl.pallas_call(
        functools.partial(second_kernel, n, rows, nvar),
        out_shape=[f32(nvar, rows, columns)] * n,
        in_specs=[smem, smem, vmem] + [vmem] * (3 * n),
        out_specs=[vmem] * n,
        scratch_shapes=[
            pltpu.VMEM((2 * nvar + 7, 2 * n, columns), jnp.float32),
            pltpu.VMEM((nvar + 1, 2 * n, columns), jnp.float32),
            pltpu.VMEM((n, nvar, rows, columns), jnp.float32),
        ],
        compiler_params=params,
        name="second",
    )(table, jacobians, own_links, *received, *edges, *stepped)

    returned = [results[0]] + [swapped(results[k], k) for k in range(1, n)]
    return pl.pallas_call(
        functools.partial(unpack_kernel, n, rows),
        out_shape=f32(1, nvar, depth, columns),
        in_specs=[vmem] * n,
        out_specs=vmem,
        compiler_params=params,
        name="unpack",
    )(*returned)


def solution(mesh):
    return jax.shard_map(
        body,
        mesh=mesh,
        in_specs=(
            P(("grp", "inst"), None, "slab", None),
            P(("grp", "inst"), "slab", None),
            P(("grp", "inst"), None, "slab", None),
            P(("grp", "inst"), None, "slab", None),
            P("slab", None),
            P(),
        ),
        out_specs=P(("grp", "inst"), None, "slab", None),
        check_vma=False,
    )
```

time: 37.6 us -> 25.8 us (0.69)
  starting transfers between devices: 16.2 us -> 11.6 us
  waiting for transfers between devices: 11.9 us -> 8.28 us
  local copies, waits for them, and re-layouts: 2.19 us -> 0.01 us
  Pallas kernels: 6.82 us -> 5.69 us
    ppermute x4 -> x2, starting transfers between devices: 11.3 us -> 3.84 us  [the longest x1 2.03 us: body(): lax.ppermute(downward, 'slab', [(i, (i - 1) % slabs) for i in range(slabs)])]
    ppermute x4 -> x2, waiting for transfers between devices: 7.57 us -> 2.06 us  [the longest x1 1.91 us: body(): lax.ppermute(upward, 'slab', [(i, (i + 1) % slabs) for i in range(slabs)])]
    ppermute x6 -> x9, starting transfers between devices: 4.97 us -> 7.74 us  [swapped(): return lax.ppermute(x, 'inst', [(i, i ^ k) for i in range(n)])]
    unnamed x17 -> x5, local copies, waits for them, and re-layouts: 2.19 us -> 0.01 us
    ppermute x6 -> x9, waiting for transfers between devices: 4.37 us -> 6.22 us  [swapped(): return lax.ppermute(x, 'inst', [(i, i ^ k) for i in range(n)])]
    pallas_call x1, Pallas kernels: 1.76 us -> 0.76 us  [body(): pl.pallas_call(functools.partial(unpack_kernel, n, rows), out_shape=f32(1...]
    pallas_call x1, Pallas kernels: 2.16 us -> 1.28 us  [body(): pl.pallas_call(functools.partial(pack_kernel, n, rows), out_shape=[f32(bu...]
    pallas_call x1 -> x3, Pallas kernels: 2.89 us -> 3.65 us  [the longest x1 2.15 us: body(): pl.pallas_call(functools.partial(second_kernel, n, rows, nvar), out_shape...]
  transfers between devices with their start and end apart: 10 -> 11, of which waited for: 6 -> 5; matrix products, arithmetic and copies ran while one was open for 0% -> 0% of each run, Pallas kernels for 0% -> 6%
where the time goes in v2:
time: 25.8 us; the launch traced here: 25.6 us
  starting transfers between devices  11.6 us (45%)
  waiting for transfers between devices  8.28 us (32%)
  Pallas kernels  5.69 us (22%)
    ppermute x9, starting transfers between devices, swapped(): return lax.ppermute(x, 'inst', [(i, i ^ k) for i in range(n)])  7.74 us
    ppermute x9, waiting for transfers between devices, swapped(): return lax.ppermute(x, 'inst', [(i, i ^ k) for i in range(n)])  6.22 us
    pallas_call x1, Pallas kernels, body(): pl.pallas_call(functools.partial(second_kernel, n, rows, nvar), out_shape...  2.15 us
    ppermute x1, starting transfers between devices, body(): lax.ppermute(downward, 'slab', [(i, (i - 1) % slabs) for i in range(slabs)])  2.03 us
    ppermute x1, waiting for transfers between devices, body(): lax.ppermute(upward, 'slab', [(i, (i + 1) % slabs) for i in range(slabs)])  1.91 us
    ppermute x1, starting transfers between devices, body(): lax.ppermute(upward, 'slab', [(i, (i + 1) % slabs) for i in range(slabs)])  1.81 us
    pallas_call x1, Pallas kernels, body(): pl.pallas_call(functools.partial(first_kernel, n, rows, nvar), out_shape=...  1.49 us
    pallas_call x1, Pallas kernels, body(): pl.pallas_call(functools.partial(pack_kernel, n, rows), out_shape=[f32(bu...  1.28 us
  transfers between devices with their start and end apart: 11, of which 5 were waited for; matrix products, arithmetic and copies ran while one was open for 0% of the time, Pallas kernels for 6%

profile of v2, /device:TPU:0, one launch (start us, length us, event | category | flops | bytes accessed | tf_op | source)
XLA Modules:
  0.0 25.6 jit_solution(16952544044230104254)
XLA Ops:
  0.0 1.3 %pack.1 = (f32[192,256]{1,0:T(8,128)S(1)}, f32[192,256]{1,0:T(8,128)S(1)}, f32[192,256]{1,0:T(8,128)S(1)}, f32[192,256]{1,0:T(8,128)S(1)}, f32[24,256]{1,0:T(8,1...) custom-call(f32[1,5,64,256]{3,2,1,0:T(8,128)} %refs_0_.1, f32[1,64,256]{2,1,0:T(8,128)} %refs_1_.1, ...), custom_call_target="tpu_custom_call" | custom-call | tf_op jit(solution)/shard_map/pack/pallas_call | solution.py:337
  1.3 0.5 %collective-permute-start = (f32[192,256]{1,0:T(8,128)S(1)}, f32[192,256]{1,0:T(8,128)S(1)}, u32[]{:S(2)}, u32[]{:S(2)}) collective-permute-start(f32[192,256]{1,0:T(8,128)S(1)} %get-tuple-element.26), channel_id=1, source_target_pairs={{0,4},{4,0},{8,12},{12,8},{1,5},{5,1},{9,13},{13,9},{2,6},{6,2},{1... | collective-permute-start | bytes 589832 | tf_op jit(solution)/shard_map/ppermute | solution.py:350
  1.8 2.6 %collective-permute-start.1 = (f32[192,256]{1,0:T(8,128)S(1)}, f32[192,256]{1,0:T(8,128)S(1)}, u32[]{:S(2)}, u32[]{:S(2)}) collective-permute-start(f32[192,256]{1,0:T(8,128)S(1)} %get-tuple-element.27), channel_id=1, source_target_pairs={{0,8},{4,12},{8,0},{12,4},{1,9},{5,13},{9,1},{13,5},{2,10},{6,14},... | collective-permute-start | bytes 589832 | tf_op jit(solution)/shard_map/ppermute | solution.py:350
  4.4 0.1 collective-permute-start.2
  4.4 1.8 %collective-permute-start.3 = (f32[24,256]{1,0:T(8,128)S(1)}, f32[24,256]{1,0:T(8,128)S(1)}, u32[]{:S(2)}, u32[]{:S(2)}) collective-permute-start(f32[24,256]{1,0:T(8,128)S(1)} %get-tuple-element.29), channel_id=1, source_target_pairs={{0,1},{1,2},{2,3},{3,0},{4,5},{5,6},{6,7},{7,4},{8,9},{9,10},{10,1... | collective-permute-start | bytes 73736 | tf_op jit(solution)/shard_map/ppermute | solution.py:353
  6.3 2.0 %collective-permute-start.4 = (f32[24,256]{1,0:T(8,128)S(1)}, f32[24,256]{1,0:T(8,128)S(1)}, u32[]{:S(2)}, u32[]{:S(2)}) collective-permute-start(f32[24,256]{1,0:T(8,128)S(1)} %get-tuple-element.30), channel_id=1, source_target_pairs={{0,3},{1,0},{2,1},{3,2},{4,7},{5,4},{6,5},{7,6},{8,11},{9,8},{10,9... | collective-permute-start | bytes 73736 | tf_op jit(solution)/shard_map/ppermute | solution.py:354
  8.3 1.9 %collective-permute-done.3.below = f32[24,256]{1,0:T(8,128)S(1)} collective-permute-done((f32[24,256]{1,0:T(8,128)S(1)}, f32[24,256]{1,0:T(8,128)S(1)}, u32[]{:S(2)}, u32[]{:S(2)}) %collective-permute-start.3) | collective-permute-done | bytes 24608 | tf_op jit(solution)/shard_map/ppermute | solution.py:353
  10.2 0.2 collective-permute-done.4.above
  10.4 0.0 copy-start.1
  10.4 0.1 collective-permute-start.5
  10.4 1.6 %collective-permute-start.6 = (f32[24,256]{1,0:T(8,128)S(1)}, f32[24,256]{1,0:T(8,128)S(1)}, u32[]{:S(2)}, u32[]{:S(2)}) collective-permute-start(f32[24,256]{1,0:T(8,128)S(1)} %get-tuple-element.33), channel_id=1, source_target_pairs={{0,8},{4,12},{8,0},{12,4},{1,9},{5,13},{9,1},{13,5},{2,10},{6,14},... | collective-permute-start | bytes 73736 | tf_op jit(solution)/shard_map/ppermute | solution.py:350
  12.1 0.0 collective-permute-done.refs_1_
  12.1 0.2 collective-permute-start.7
  12.3 0.0 copy-done.1
  12.3 0.0 copy-start
  12.3 0.0 collective-permute-done.1.refs_2_
  12.3 1.5 %collective-permute-done.2.refs_3_ = f32[192,256]{1,0:T(8,128)S(1)} collective-permute-done((f32[192,256]{1,0:T(8,128)S(1)}, f32[192,256]{1,0:T(8,128)S(1)}, u32[]{:S(2)}, u32[]{:S(2)}) %collective-permute-start.2) | collective-permute-done | bytes 196640 | tf_op jit(solution)/shard_map/ppermute | solution.py:350
  13.8 0.0 copy-done
  13.8 1.5 %first.1 = (f32[5,16,256]{2,1,0:T(8,128)S(1)}, f32[5,16,256]{2,1,0:T(8,128)S(1)}, f32[5,16,256]{2,1,0:T(8,128)S(1)}, f32[5,16,256]{2,1,0:T(8,128)S(1)}) custom-call(f32[4,4]{1,0:T(4,128)S(1)} %copy-done, f32[2,5,5]{2,1,0:T(8,128)S(1)} %copy.9.jacobians, f32[192,256]{1,0:T(8,128)S(1)} %get-tuple-element.25.refs_0_, ...), custom_call_target="tpu_custom_call" | custom-call | tf_op jit(solution)/shard_map/first/pallas_call | solution.py:366
  15.3 0.0 collective-permute-done.5.refs_5_
  15.3 0.0 collective-permute-done.6.refs_6_
  15.3 0.0 collective-permute-done.7.refs_7_
  15.3 2.1 %second.1 = (f32[5,16,256]{2,1,0:T(8,128)S(1)}, f32[5,16,256]{2,1,0:T(8,128)S(1)}, f32[5,16,256]{2,1,0:T(8,128)S(1)}, f32[5,16,256]{2,1,0:T(8,128)S(1)}) custom-call(f32[4,4]{1,0:T(4,128)S(1)} %copy-done, f32[2,5,5]{2,1,0:T(8,128)S(1)} %copy.9.jacobians, s32[1,256]{1,0:T(1,128)S(1)} %get-tuple-element.24.links, f32[192,256]{1,0:T(8,128)S(1)} %get-tuple-element.25.refs_0_, ...), custom_call_target="tpu_custom_call" | custom-call | tf_op jit(solution)/shard_map/second/pallas_call | solution.py:374
  17.5 0.4 %collective-permute-start.8 = (f32[5,16,256]{2,1,0:T(8,128)S(1)}, f32[5,16,256]{2,1,0:T(8,128)S(1)}, u32[]{:S(2)}, u32[]{:S(2)}) collective-permute-start(f32[5,16,256]{2,1,0:T(8,128)S(1)} %get-tuple-element.40), channel_id=1, source_target_pairs={{0,4},{4,0},{8,12},{12,8},{1,5},{5,1},{9,13},{13,9},{2,6},{6,2},{1... | collective-permute-start | bytes 245768 | tf_op jit(solution)/shard_map/ppermute | solution.py:350
  17.9 2.2 %collective-permute-start.9 = (f32[5,16,256]{2,1,0:T(8,128)S(1)}, f32[5,16,256]{2,1,0:T(8,128)S(1)}, u32[]{:S(2)}, u32[]{:S(2)}) collective-permute-start(f32[5,16,256]{2,1,0:T(8,128)S(1)} %get-tuple-element.41), channel_id=1, source_target_pairs={{0,8},{4,12},{8,0},{12,4},{1,9},{5,13},{9,1},{13,5},{2,10},{6,14},... | collective-permute-start | bytes 245768 | tf_op jit(solution)/shard_map/ppermute | solution.py:350
  20.2 0.0 collective-permute-start.10
  20.2 0.0 collective-permute-done.8.refs_1_
  20.2 2.8 %collective-permute-done.9.refs_2_ = f32[5,16,256]{2,1,0:T(8,128)S(1)} collective-permute-done((f32[5,16,256]{2,1,0:T(8,128)S(1)}, f32[5,16,256]{2,1,0:T(8,128)S(1)}, u32[]{:S(2)}, u32[]{:S(2)}) %collective-permute-start.9) | collective-permute-done | bytes 81952 | tf_op jit(solution)/shard_map/ppermute | solution.py:350
  23.0 1.9 %collective-permute-done.10.refs_3_ = f32[5,16,256]{2,1,0:T(8,128)S(1)} collective-permute-done((f32[5,16,256]{2,1,0:T(8,128)S(1)}, f32[5,16,256]{2,1,0:T(8,128)S(1)}, u32[]{:S(2)}, u32[]{:S(2)}) %collective-permute-start.10) | collective-permute-done | bytes 81952 | tf_op jit(solution)/shard_map/ppermute | solution.py:350
  24.9 0.8 %unpack.1 = f32[1,5,64,256]{3,2,1,0:T(8,128)} custom-call(f32[5,16,256]{2,1,0:T(8,128)S(1)} %get-tuple-element.39.refs_0_, f32[5,16,256]{2,1,0:T(8,128)S(1)} %collective-permute-done.8.refs_1_, f32[5,16,256]{2,1,0:T(8,128)S(1)} %collective-permute-done.9.refs_2_, f32[5,16,256]{2,1,0:T(8,128)S(1)} %collective-permute-done.10.refs_3_), custom_call_target="tpu_custom_call" | custom-call | tf_op jit(solution)/shard_map/unpack/pallas_call | solution.py:389
  (2 shorter events, 0.0 us)
Async XLA Ops:
  1.3 10.8 %collective-permute-start = (f32[192,256]{1,0:T(8,128)S(1)}, f32[192,256]{1,0:T(8,128)S(1)}, u32[]{:S(2)}, u32[]{:S(2)}) collective-permute-start(f32[192,256]{1,0:T(8,128)S(1)} %get-tuple-element.26), channel_id=1, source_target_pairs={{0,4},{4,0},{8,12},{12,8},{1,5},{5,1},{9,13},{13,9},{2,6},{6,2},{1... | collective-permute-start | bytes 589832 | tf_op jit(solution)/shard_map/ppermute | solution.py:350
  1.8 10.5 %collective-permute-start.1 = (f32[192,256]{1,0:T(8,128)S(1)}, f32[192,256]{1,0:T(8,128)S(1)}, u32[]{:S(2)}, u32[]{:S(2)}) collective-permute-start(f32[192,256]{1,0:T(8,128)S(1)} %get-tuple-element.27), channel_id=1, source_target_pairs={{0,8},{4,12},{8,0},{12,4},{1,9},{5,13},{9,1},{13,5},{2,10},{6,14},... | collective-permute-start | bytes 589832 | tf_op jit(solution)/shard_map/ppermute | solution.py:350
  4.4 9.4 %collective-permute-start.2 = (f32[192,256]{1,0:T(8,128)S(1)}, f32[192,256]{1,0:T(8,128)S(1)}, u32[]{:S(2)}, u32[]{:S(2)}) collective-permute-start(f32[192,256]{1,0:T(8,128)S(1)} %get-tuple-element.28), channel_id=1, source_target_pairs={{0,12},{4,8},{8,4},{12,0},{1,13},{5,9},{9,5},{13,1},{2,14},{6,10},... | collective-permute-start | bytes 589832 | tf_op jit(solution)/shard_map/ppermute | solution.py:350
  4.4 5.7 %collective-permute-start.3 = (f32[24,256]{1,0:T(8,128)S(1)}, f32[24,256]{1,0:T(8,128)S(1)}, u32[]{:S(2)}, u32[]{:S(2)}) collective-permute-start(f32[24,256]{1,0:T(8,128)S(1)} %get-tuple-element.29), channel_id=1, source_target_pairs={{0,1},{1,2},{2,3},{3,0},{4,5},{5,6},{6,7},{7,4},{8,9},{9,10},{10,1... | collective-permute-start | bytes 73736 | tf_op jit(solution)/shard_map/ppermute | solution.py:353
  6.3 4.1 %collective-permute-start.4 = (f32[24,256]{1,0:T(8,128)S(1)}, f32[24,256]{1,0:T(8,128)S(1)}, u32[]{:S(2)}, u32[]{:S(2)}) collective-permute-start(f32[24,256]{1,0:T(8,128)S(1)} %get-tuple-element.30), channel_id=1, source_target_pairs={{0,3},{1,0},{2,1},{3,2},{4,7},{5,4},{6,5},{7,6},{8,11},{9,8},{10,9... | collective-permute-start | bytes 73736 | tf_op jit(solution)/shard_map/ppermute | solution.py:354
  10.4 2.0 %copy-start.1 = (f32[2,5,5]{2,0,1:T(2,128)S(1)}, f32[2,5,5]{2,0,1:T(2,128)}, u32[]{:S(2)}) copy-start(f32[2,5,5]{2,0,1:T(2,128)} %param.12) | copy-start | bytes 604
  10.4 4.9 %collective-permute-start.5 = (f32[24,256]{1,0:T(8,128)S(1)}, f32[24,256]{1,0:T(8,128)S(1)}, u32[]{:S(2)}, u32[]{:S(2)}) collective-permute-start(f32[24,256]{1,0:T(8,128)S(1)} %get-tuple-element.32), channel_id=1, source_target_pairs={{0,4},{4,0},{8,12},{12,8},{1,5},{5,1},{9,13},{13,9},{2,6},{6,2},{1... | collective-permute-start | bytes 73736 | tf_op jit(solution)/shard_map/ppermute | solution.py:350
  10.4 4.9 %collective-permute-start.6 = (f32[24,256]{1,0:T(8,128)S(1)}, f32[24,256]{1,0:T(8,128)S(1)}, u32[]{:S(2)}, u32[]{:S(2)}) collective-permute-start(f32[24,256]{1,0:T(8,128)S(1)} %get-tuple-element.33), channel_id=1, source_target_pairs={{0,8},{4,12},{8,0},{12,4},{1,9},{5,13},{9,1},{13,5},{2,10},{6,14},... | collective-permute-start | bytes 73736 | tf_op jit(solution)/shard_map/ppermute | solution.py:350
  12.1 3.3 %collective-permute-start.7 = (f32[24,256]{1,0:T(8,128)S(1)}, f32[24,256]{1,0:T(8,128)S(1)}, u32[]{:S(2)}, u32[]{:S(2)}) collective-permute-start(f32[24,256]{1,0:T(8,128)S(1)} %get-tuple-element.34), channel_id=1, source_target_pairs={{0,12},{4,8},{8,4},{12,0},{1,13},{5,9},{9,5},{13,1},{2,14},{6,10},... | collective-permute-start | bytes 73736 | tf_op jit(solution)/shard_map/ppermute | solution.py:350
  12.3 1.5 %copy-start = (f32[4,4]{1,0:T(4,128)S(1)}, f32[4,4]{1,0:T(4,128)}, u32[]{:S(2)}) copy-start(f32[4,4]{1,0:T(4,128)} %constant.2.clone.table) | copy-start | bytes 196
  17.5 2.7 %collective-permute-start.8 = (f32[5,16,256]{2,1,0:T(8,128)S(1)}, f32[5,16,256]{2,1,0:T(8,128)S(1)}, u32[]{:S(2)}, u32[]{:S(2)}) collective-permute-start(f32[5,16,256]{2,1,0:T(8,128)S(1)} %get-tuple-element.40), channel_id=1, source_target_pairs={{0,4},{4,0},{8,12},{12,8},{1,5},{5,1},{9,13},{13,9},{2,6},{6,2},{1... | collective-permute-start | bytes 245768 | tf_op jit(solution)/shard_map/ppermute | solution.py:350
  17.9 5.1 %collective-permute-start.9 = (f32[5,16,256]{2,1,0:T(8,128)S(1)}, f32[5,16,256]{2,1,0:T(8,128)S(1)}, u32[]{:S(2)}, u32[]{:S(2)}) collective-permute-start(f32[5,16,256]{2,1,0:T(8,128)S(1)} %get-tuple-element.41), channel_id=1, source_target_pairs={{0,8},{4,12},{8,0},{12,4},{1,9},{5,13},{9,1},{13,5},{2,10},{6,14},... | collective-permute-start | bytes 245768 | tf_op jit(solution)/shard_map/ppermute | solution.py:350
  20.2 4.7 %collective-permute-start.10 = (f32[5,16,256]{2,1,0:T(8,128)S(1)}, f32[5,16,256]{2,1,0:T(8,128)S(1)}, u32[]{:S(2)}, u32[]{:S(2)}) collective-permute-start(f32[5,16,256]{2,1,0:T(8,128)S(1)} %get-tuple-element.42), channel_id=1, source_target_pairs={{0,12},{4,8},{8,4},{12,0},{1,13},{5,9},{9,5},{13,1},{2,14},{6,10},... | collective-permute-start | bytes 245768 | tf_op jit(solution)/shard_map/ppermute | solution.py:350

commit v3 on v0

v3 whole, which is shorter than its diff:
```python
import functools

import jax
import jax.numpy as jnp
import numpy as np
from jax import lax
from jax.experimental import pallas as pl
from jax.experimental.pallas import tpu as pltpu
from jax.sharding import PartitionSpec as P

frequency = 0.5
pseudo_step = 0.2
nyquist_damping = 0.25

STRIP = 8


def spectral_table(instances):
    offsets = np.arange(instances)[:, None] - np.arange(instances)[None, :]
    phases = np.pi * offsets / instances
    sine_safe = np.where(offsets == 0, 1.0, np.sin(phases))
    parity = np.where(offsets % 2 == 0, 1.0, -1.0)
    matrix = np.where(offsets == 0, 0.0, 0.5 * frequency * parity * np.cos(phases) / sine_safe)
    matrix = matrix + nyquist_damping * parity
    return jnp.asarray(matrix, jnp.float32)


def pack_kernel(states, volumes, row_normals, col_normals, links, near, cell, rows, own_links, upward, downward, sems):
    nvar, depth = states.shape[1], states.shape[2]
    pairs = [
        (states.at[0], near.at[pl.ds(0, nvar)]),
        (volumes, near.at[pl.ds(nvar, 1)]),
        (volumes, cell.at[pl.ds(0, 1)]),
        (col_normals.at[0], cell.at[pl.ds(1, 2)]),
        (row_normals.at[0], rows),
        (links, own_links),
    ]
    copies = [pltpu.make_async_copy(a, b, sems.at[t]) for t, (a, b) in enumerate(pairs)]
    for copy in copies:
        copy.start()
    for copy in copies:
        copy.wait()

    def put(ref, second, edge, face):
        for v in range(nvar):
            ref[pl.ds(v, 1), :] = near[v, pl.ds(second, 1), :]
            ref[pl.ds(nvar + v, 1), :] = near[v, pl.ds(edge, 1), :]
        ref[pl.ds(2 * nvar, 1), :] = near[nvar, pl.ds(edge, 1), :]
        for d in range(2):
            ref[pl.ds(2 * nvar + 1 + d, 1), :] = rows[d, pl.ds(face, 1), :]
            ref[pl.ds(2 * nvar + 3 + d, 1), :] = cell[1 + d, pl.ds(edge, 1), :]

    put(upward, depth - 2, depth - 1, depth - 1)
    put(downward, 1, 0, 1)
    for d in range(2):
        downward[pl.ds(2 * nvar + 5 + d, 1), :] = rows[d, pl.ds(0, 1), :]
    downward[pl.ds(2 * nvar + 7, 1), :] = own_links[...].astype(jnp.float32)


def half_jacobians(jacobians, nvar):
    return [[[0.5 * jacobians[d, v, w] for w in range(nvar)] for v in range(nvar)] for d in range(2)]


def step_weight(table, row, col):
    me = lax.axis_index("inst")
    return pseudo_step * table[jnp.bitwise_xor(me, row), jnp.bitwise_xor(me, col)]


def weighted(weights, values):
    total = weights[0] * values[0]
    for weight, value in zip(weights[1:], values[1:]):
        total = total + weight * value
    return total


def transformed(half, values):
    return [[weighted(half[d][v], values) for v in range(len(values))] for d in range(2)]


def spread_of(normal):
    return 0.5 * (jnp.abs(normal[0]) + jnp.abs(normal[1]))


def own_side(normal, values, values_j):
    spread = spread_of(normal)
    return [
        normal[0] * values_j[0][v] + normal[1] * values_j[1][v] - spread * values[v]
        for v in range(len(values))
    ]


def other_side(normal, values, values_j):
    spread = spread_of(normal)
    return [
        normal[0] * values_j[0][v] + normal[1] * values_j[1][v] + spread * values[v]
        for v in range(len(values))
    ]


def col_change(normal, values, values_j):
    columns = values[0].shape[1]
    upper_normal = [pltpu.roll(x, columns - 1, 1) for x in normal]
    own = own_side(normal, values, values_j)
    other = other_side(upper_normal, values, values_j)
    flux = [a + pltpu.roll(b, 1, 1) for a, b in zip(own, other)]
    return [pltpu.roll(x, columns - 1, 1) - x for x in flux]


def row_changes(count, at, first_flux, last_flux):
    last = None
    ahead = at(0)
    for s in range(count):
        faces, cells, cells_j = ahead
        nvar = len(cells)
        row = lax.broadcasted_iota(jnp.int32, cells[0].shape, 0)
        top, bottom = row == 0, row == STRIP - 1
        rolled_faces = [pltpu.roll(x, STRIP - 1, 0) for x in faces]
        if s + 1 < count:
            ahead = at(s + 1)
            rolled_faces = [
                jnp.where(bottom, pltpu.roll(x, STRIP - 1, 0), y) for x, y in zip(ahead[0], rolled_faces)
            ]
        own = own_side(faces, cells, cells_j)
        rolled = [pltpu.roll(x, 1, 0) for x in other_side(rolled_faces, cells, cells_j)]
        if s == 0:
            flux = [jnp.where(top, first_flux(v), own[v] + rolled[v]) for v in range(nvar)]
        else:
            flux = [own[v] + jnp.where(top, before[v], rolled[v]) for v in range(nvar)]
        lifted = [pltpu.roll(x, STRIP - 1, 0) for x in flux]
        if last is not None:
            yield (
                s - 1,
                last[0],
                last[1],
                [jnp.where(bottom, lifted[v], last[3][v]) - last[2][v] for v in range(nvar)],
            )
        before, last = rolled, (cells, cells_j, flux, lifted)
    yield (
        count - 1,
        last[0],
        last[1],
        [jnp.where(bottom, last_flux(v), last[3][v]) - last[2][v] for v in range(nvar)],
    )


def strip(s):
    return pl.ds(s * STRIP, STRIP)


def face_flux(normal, lower, lower_j, upper, upper_j):
    spread = spread_of(normal)
    return [
        normal[0] * (lower_j[0][v] + upper_j[0][v])
        + normal[1] * (lower_j[1][v] + upper_j[1][v])
        - spread * (upper[v] - lower[v])
        for v in range(len(lower))
    ]


def split_dot(x, onehot, transposed):
    high = x.astype(jnp.bfloat16)
    rest = x - high.astype(jnp.float32)
    middle = rest.astype(jnp.bfloat16)
    low = (rest - middle.astype(jnp.float32)).astype(jnp.bfloat16)
    count = x.shape[0]
    stacked = jnp.concatenate([high, middle, low], axis=0)
    out = lax.dot_general(
        stacked,
        onehot,
        (((1,), (1 if transposed else 0,)), ((), ())),
        preferred_element_type=jnp.float32,
    )
    return out[:count] + (out[count : 2 * count] + out[2 * count :])


def pair(below, above):
    return jnp.concatenate([below, above], axis=0)


def pick(mask, a, b):
    return [jnp.where(mask, x, y) for x, y in zip(a, b)]


def pick_both(mask, a, b):
    return pick(mask, a[0], b[0]), [pick(mask, x, y) for x, y in zip(a[1], b[1])]


def behind(below, above, t):
    return pair(below[pl.ds(t, 1), :], above[pl.ds(t, 1), :])


def crossed(rows, links_below, links_above, stack):
    stack[...] = jnp.zeros(stack.shape, jnp.float32)
    for t, x in enumerate(rows):
        stack[pl.ds(2 * t, 2), :] = x
    columns = stack.shape[1]
    cell = lax.broadcasted_iota(jnp.int32, (columns, columns), 0)
    onehots = [(cell == x).astype(jnp.float32).astype(jnp.bfloat16) for x in (links_below, links_above)]
    stacked = stack[...]
    side = lax.broadcasted_iota(jnp.int32, stacked.shape, 0) % 2
    stack[...] = jnp.where(
        side == 0, split_dot(stacked, onehots[0], False), split_dot(stacked, onehots[1], True)
    )
    return [stack[pl.ds(2 * t, 2), :] for t in range(len(rows))]


def edge_kernel(nvar, jacobians, below, above, near, row_normals, links, early, out, kept, stack):
    depth, columns = near.shape[1], near.shape[2]
    half = half_jacobians(jacobians, nvar)
    is_below = lax.broadcasted_iota(jnp.int32, (2, columns), 0) == 0
    inner_face = [
        pair(row_normals[d, pl.ds(0, 1), :], above[pl.ds(2 * nvar + 5 + d, 1), :]) for d in range(2)
    ]
    rows = [behind(below, above, nvar + v) for v in range(nvar + 1)] + inner_face
    links_above = above[pl.ds(2 * nvar + 7, 1), :].astype(jnp.int32)
    rows = crossed(rows, links[...], links_above, stack)
    rim, volume, face = rows[:nvar], rows[nvar], pick(is_below, inner_face, rows[nvar + 1 :])
    inside = [pair(near[v, pl.ds(0, 1), :], near[v, pl.ds(depth - 1, 1), :]) for v in range(nvar)]
    low, high = pick(is_below, rim, inside), pick(is_below, inside, rim)
    summed = transformed(half, [x + y for x, y in zip(low, high)])
    spread = spread_of(face)
    across = [
        face[0] * summed[0][v] + face[1] * summed[1][v] - spread * (high[v] - low[v]) for v in range(nvar)
    ]
    at = 2 * nvar
    for v in range(nvar):
        out[pl.ds(v, 1), :] = across[v][0:1]
        out[pl.ds(nvar + v, 1), :] = across[v][1:2]
        kept[v] = rim[v]
        kept[nvar + v] = jnp.where(is_below, across[v], -across[v])
    for v, x in enumerate(rim + [volume]):
        out[pl.ds(at + v, 1), :] = x[0:1]
        out[pl.ds(at + nvar + 1 + v, 1), :] = x[1:2]
    kept[2 * nvar] = volume
    for d in range(2):
        kept[2 * nvar + 1 + d] = face[d]
    head = out.shape[0] - 2 * depth
    for d in range(2):
        out[pl.ds(head + d * depth, depth), :] = row_normals[d]


def behind_kernel(nvar, jacobians, below, above, links, out, stack):
    half = half_jacobians(jacobians, nvar)
    is_below = lax.broadcasted_iota(jnp.int32, (2, links.shape[1]), 0) == 0

    def with_j(values):
        return values, transformed(half, values)

    outer, rim = [with_j([behind(below, above, t + v) for v in range(nvar)]) for t in (0, nvar)]
    low, high = pick_both(is_below, outer, rim), pick_both(is_below, rim, outer)
    at = 2 * nvar + 1
    far_flux = face_flux([behind(below, above, at + d) for d in range(2)], *low, *high)
    beside = col_change([behind(below, above, at + 2 + d) for d in range(2)], *rim)
    rows = [jnp.where(is_below, -x, x) + y for x, y in zip(far_flux, beside)]
    links_above = above[pl.ds(2 * nvar + 7, 1), :].astype(jnp.int32)
    for v, x in enumerate(crossed(rows, links[...], links_above, stack)):
        out[v] = x


def state_kernel(states, before, *outs):
    at = 0
    for out in outs:
        out[...] = states[0, pl.ds(at, out.shape[0])]
        at += out.shape[0]


def volume_kernel(cells, before, out):
    out[...] = cells[pl.ds(0, 1)]


def own_flux_kernel(nvar, jacobians, near, cell, row_normals, out):
    strips = out.shape[1] // STRIP
    half = half_jacobians(jacobians, nvar)

    def at(s):
        cells = [near[v, strip(s), :] for v in range(nvar)]
        return [row_normals[d, strip(s), :] for d in range(2)], cells, transformed(half, cells)

    for s, cells, cells_j, along in row_changes(strips, at, lambda v: 0.0, lambda v: 0.0):
        beside = col_change([cell[1 + d, strip(s), :] for d in range(2)], cells, cells_j)
        factor = pseudo_step / cell[0, strip(s), :]
        for v in range(nvar):
            out[v, strip(s), :] = cells[v] - factor * (along[v] + beside[v])


def far_col_kernel(nvar, jacobians, states, cell, out, out_j):
    strips = out.shape[1] // STRIP
    half = half_jacobians(jacobians, nvar)
    for s in range(strips):
        cells = [states[0, v, strip(s), :] for v in range(nvar)]
        cells_j = transformed(half, cells)
        beside = col_change([cell[1 + d, strip(s), :] for d in range(2)], cells, cells_j)
        factor = pseudo_step / cell[0, strip(s), :]
        for v in range(nvar):
            out[v, strip(s), :] = cells[v] - factor * beside[v]
            for d in range(2):
                out_j[d, v, strip(s), :] = cells_j[d][v]


def time_kernel(n, nvar, table, near, beyond, edge, *refs):
    far = n // 2 - 1
    states, cells, *pieces, beyond_volumes = [refs[far * t : far * (t + 1)] for t in range(5)]
    parts, outs = refs[5 * far : 6 * far + 1], refs[6 * far + 1 :]
    beyond_states = [[x.at[v] for x in piece for v in range(x.shape[0])] for piece in zip(*pieces)]
    count = far + 1
    weights = [
        [step_weight(table, 2 * a, 2 * b) for b in range(count)]
        + [step_weight(table, 2 * a, 2 * b + 1) for b in range(count)]
        for a in range(count)
    ]
    strips = outs[0].shape[1] // STRIP
    row = lax.broadcasted_iota(jnp.int32, (STRIP, near.shape[2]), 0)
    for s in range(strips):
        here = [near[nvar, strip(s), :]] + [x[0, strip(s), :] for x in cells]
        sizes = here + [beyond[nvar, strip(s), :]] + [x[0, strip(s), :] for x in beyond_volumes]
        factors = [weighted(weights[a], sizes) / here[a] for a in range(count)]
        for v in range(nvar):
            values = [near[v, strip(s), :]] + [x[0, v, strip(s), :] for x in states]
            values = values + [beyond[v, strip(s), :]] + [x[v][strip(s), :] for x in beyond_states]
            moved = [
                parts[a][v, strip(s), :] - weighted(weights[a], values) - factors[a] * values[a]
                for a in range(count)
            ]
            if s == 0:
                moved[0] = moved[0] + jnp.where(row == 0, pseudo_step * edge[pl.ds(v, 1), :], 0.0) / here[0]
            if s == strips - 1:
                lacking = jnp.where(row == STRIP - 1, pseudo_step * edge[pl.ds(nvar + v, 1), :], 0.0)
                moved[0] = moved[0] - lacking / here[0]
            for a in range(count):
                outs[a][v, strip(s), :] = moved[a]


def base_kernel(n, nvar, table, jacobians, stepped, near, beyond, cell, row_normals, *refs):
    far = n // 2 - 1
    cells_of, beyond_volumes, out = refs[:far], refs[far : 2 * far], refs[2 * far]
    strips = out.shape[1] // STRIP
    half = half_jacobians(jacobians, nvar)
    weights = [step_weight(table, 0, 2 * b) for b in range(far + 1)]
    weights = weights + [step_weight(table, 0, 2 * b + 1) for b in range(far + 1)]

    def at(s):
        cells = [stepped[v, strip(s), :] for v in range(nvar)]
        return [row_normals[d, strip(s), :] for d in range(2)], cells, transformed(half, cells)

    for s, cells, cells_j, along in row_changes(strips, at, lambda v: 0.0, lambda v: 0.0):
        beside = col_change([cell[1 + d, strip(s), :] for d in range(2)], cells, cells_j)
        sizes = [near[nvar, strip(s), :]] + [x[0, strip(s), :] for x in cells_of]
        sizes = sizes + [beyond[nvar, strip(s), :]] + [x[0, strip(s), :] for x in beyond_volumes]
        inverse = 1.0 / sizes[0]
        kept = (1.0 - weights[0]) - inverse * weighted(weights, sizes)
        for v in range(nvar):
            out[v, strip(s), :] = kept * cells[v] - (pseudo_step * inverse) * (along[v] + beside[v])


def far_step_kernel(n, nvar, table, stepped, base, edge, *refs):
    far = n // 2 - 1
    edges, states, cells_of, parts, transforms = [refs[far * t : far * (t + 1)] for t in range(5)]
    shared, out = refs[5 * far :]
    depth = stepped.shape[1]
    strips = depth // STRIP
    mine = [step_weight(table, 0, 2 * b) for b in range(far + 1)]
    other = [step_weight(table, 1, 2 * b) for b in range(far + 1)]
    head = edge.shape[0] - 2 * depth

    def changes(a):
        def at(s):
            faces = [edges[a][pl.ds(head + d * depth + s * STRIP, STRIP), :] for d in range(2)]
            cells = [states[a][0, v, strip(s), :] for v in range(nvar)]
            return faces, cells, [[transforms[a][d, v, strip(s), :] for v in range(nvar)] for d in range(2)]

        return row_changes(
            strips, at, lambda v: edges[a][pl.ds(v, 1), :], lambda v: edges[a][pl.ds(nvar + v, 1), :]
        )

    for moves in zip(*[changes(a) for a in range(far)]):
        s = moves[0][0]
        factors = [pseudo_step / cells_of[a][0, strip(s), :] for a in range(far)]
        for v in range(nvar):
            given = other[0] * stepped[v, strip(s), :]
            taken = base[v, strip(s), :]
            for a in range(far):
                value = parts[a][v, strip(s), :] - factors[a] * moves[a][3][v]
                given = given + other[1 + a] * value
                taken = taken - mine[1 + a] * value
            shared[pl.ds(v * depth + s * STRIP, STRIP), :] = given
            out[v, strip(s), :] = taken
    rims = pl.ds(2 * nvar, 2 * nvar + 2)
    shared[pl.ds(nvar * depth, 2 * nvar + 2), :] = weighted(
        other, [edge[rims, :]] + [edges[a][rims, :] for a in range(far)]
    )


def rim_kernel(n, nvar, table, jacobians, edge, kept, others, near, stepped, *refs):
    far = n // 2 - 1
    edges, out = refs[:far], refs[far]
    depth, columns = stepped.shape[1], stepped.shape[2]
    half = half_jacobians(jacobians, nvar)
    weights = [step_weight(table, 0, 2 * b) for b in range(far + 1)]
    is_below = lax.broadcasted_iota(jnp.int32, (2, columns), 0) == 0
    at = 2 * nvar

    def rim(v):
        return weighted(
            weights,
            [
                pair(ref[pl.ds(at + v, 1), :], ref[pl.ds(at + nvar + 1 + v, 1), :])
                for ref in [edge] + list(edges)
            ],
        )

    inverse = 1.0 / kept[2 * nvar]
    volume_rate = rim(nvar)
    face = [kept[2 * nvar + 1], kept[2 * nvar + 2]]
    spread = spread_of(face)
    inside = [pair(stepped[v, pl.ds(0, 1), :], stepped[v, pl.ds(depth - 1, 1), :]) for v in range(nvar)]
    inside_j = transformed(half, inside)
    for v in range(nvar):
        change = pseudo_step * (kept[nvar + v] + others[v])
        out[v] = kept[v] - rim(v) - inverse * (kept[v] * volume_rate + change)
        out[nvar + v] = inverse * kept[v]
        out[2 * nvar + v] = (
            face[0] * inside_j[0][v]
            + face[1] * inside_j[1][v]
            + jnp.where(is_below, -spread, spread) * inside[v]
        )
    volume = pair(near[nvar, pl.ds(0, 1), :], near[nvar, pl.ds(depth - 1, 1), :])
    factor = pseudo_step / volume
    out[3 * nvar] = jnp.where(is_below, factor, -factor)


def final_kernel(nvar, jacobians, rims, kept, base, shared, out, held, sems):
    depth, columns = base.shape[1], base.shape[2]
    strips = depth // STRIP
    half = half_jacobians(jacobians, nvar)
    is_below = lax.broadcasted_iota(jnp.int32, (2, columns), 0) == 0

    def summed(v):
        return pair(shared[pl.ds(nvar * depth + v, 1), :], shared[pl.ds(nvar * depth + nvar + 1 + v, 1), :])

    def value(v, s):
        return base[v, strip(s), :] - shared[pl.ds(v * depth + s * STRIP, STRIP), :]

    copies = []

    def send(t, first, count):
        where = pl.ds(first * STRIP, count * STRIP)
        copies.append(pltpu.make_async_copy(held.at[:, where], out.at[0, :, where], sems.at[t]))
        copies[-1].start()

    for s in range(1, strips - 1):
        for v in range(nvar):
            held[v, strip(s), :] = value(v, s)
    send(0, 1, strips - 2)
    volume_rate = summed(nvar)
    outside = [rims[v] - summed(v) - rims[nvar + v] * volume_rate for v in range(nvar)]
    outside_j = transformed(half, outside)
    face = [kept[2 * nvar + 1], kept[2 * nvar + 2]]
    spread = spread_of(face)
    signed = jnp.where(is_below, spread, -spread)
    row = lax.broadcasted_iota(jnp.int32, (STRIP, columns), 0)
    for v in range(nvar):
        across = face[0] * outside_j[0][v] + face[1] * outside_j[1][v] + signed * outside[v]
        lacking = rims[3 * nvar] * (across + rims[2 * nvar + v])
        held[v, strip(0), :] = value(v, 0) + jnp.where(row == 0, lacking[0:1], 0.0)
        held[v, strip(strips - 1), :] = value(v, strips - 1) + jnp.where(
            row == STRIP - 1, lacking[1:2], 0.0
        )
    send(1, 0, 1)
    send(2, strips - 1, 1)
    for copy in copies:
        copy.wait()


def body(states, volumes, row_normals, col_normals, face_links, jacobians):
    n = lax.axis_size("inst")
    slabs = lax.axis_size("slab")
    _, nvar, depth, columns = states.shape
    far = list(range(2, n, 2))
    down_rows = -(-(2 * nvar + 8) // 8) * 8
    up_rows = down_rows + 8
    head = -(-(4 * nvar + 2) // 8) * 8

    def f32(*shape):
        return jax.ShapeDtypeStruct(shape, jnp.float32)

    vmem = pl.BlockSpec(memory_space=pltpu.VMEM)
    smem = pl.BlockSpec(memory_space=pltpu.SMEM)
    hbm = pl.BlockSpec(memory_space=pltpu.HBM)
    params = pltpu.CompilerParams(vmem_limit_bytes=24 * 1024 * 1024)
    table = spectral_table(n)

    def call(kernel, name, shapes, *operands, scratch=(), out_spec=vmem):
        single = not isinstance(shapes, list)
        return pl.pallas_call(
            kernel,
            out_shape=shapes,
            in_specs=[smem if x is table or x is jacobians else vmem for x in operands],
            out_specs=out_spec if single else [out_spec] * len(shapes),
            scratch_shapes=list(scratch),
            compiler_params=params,
            name=name,
        )(*operands)

    def swapped(x, k):
        return lax.ppermute(x, "inst", [(i, i ^ k) for i in range(n)])

    state_of = {k: swapped(states, k) for k in far}
    inputs = [
        pltpu.with_memory_space_constraint(x, pltpu.HBM)
        for x in (states, volumes, row_normals, col_normals, face_links)
    ]
    near, own_cell, own_rows, own_links, upward, downward = pl.pallas_call(
        pack_kernel,
        out_shape=[
            f32(nvar + 1, depth, columns),
            f32(3, depth, columns),
            f32(2, depth, columns),
            jax.ShapeDtypeStruct(face_links.shape, face_links.dtype),
            f32(up_rows, columns),
            f32(down_rows, columns),
        ],
        in_specs=[hbm] * 5,
        out_specs=[vmem] * 6,
        scratch_shapes=[pltpu.SemaphoreType.DMA((6,))],
        compiler_params=params,
        name="pack",
    )(*inputs)
    cell_of = {k: swapped(own_cell, k) for k in far}
    below = lax.ppermute(upward, "slab", [(i, (i + 1) % slabs) for i in range(slabs)])
    above = lax.ppermute(downward, "slab", [(i, (i - 1) % slabs) for i in range(slabs)])
    field = f32(nvar, depth, columns)
    parts = [
        call(functools.partial(own_flux_kernel, nvar), "own_flux", field, jacobians, near, own_cell, own_rows)
    ]
    edge, kept = call(
        functools.partial(edge_kernel, nvar),
        "edges",
        [f32(head + 2 * depth, columns), f32(2 * nvar + 3, 2, columns)],
        jacobians,
        below,
        above,
        near,
        own_rows,
        own_links,
        parts[0],
        scratch=[pltpu.VMEM((-(-(2 * nvar + 6) // 8) * 8, columns), jnp.float32)],
    )
    others = call(
        functools.partial(behind_kernel, nvar),
        "behind",
        f32(nvar, 2, columns),
        jacobians,
        below,
        above,
        own_links,
        scratch=[pltpu.VMEM((-(-2 * nvar // 8) * 8, columns), jnp.float32)],
    )
    edge_of = {k: swapped(edge, k) for k in far}
    beyond = swapped(near, 1)
    pieces = [f32(count, depth, columns) for count in (nvar - nvar // 2, nvar // 2)]
    beyond_states = []
    for k in far:
        beyond_states.append([swapped(x, 1) for x in call(state_kernel, "states", pieces, state_of[k], edge)])
    beyond_volumes = {
        k: swapped(call(volume_kernel, "volumes", f32(1, depth, columns), cell_of[k], others), 1) for k in far
    }

    transforms = {}
    for k in far:
        part, transforms[k] = call(
            functools.partial(far_col_kernel, nvar),
            "far_col",
            [field, f32(2, nvar, depth, columns)],
            jacobians,
            state_of[k],
            cell_of[k],
        )
        parts.append(part)
    stepped, *parts = call(
        functools.partial(time_kernel, n, nvar),
        "time",
        [field] * (len(far) + 1),
        table,
        near,
        beyond,
        edge,
        *[state_of[k] for k in far],
        *[cell_of[k] for k in far],
        *[x[0] for x in beyond_states],
        *[x[1] for x in beyond_states],
        *[beyond_volumes[k] for k in far],
        *parts,
    )
    base = call(
        functools.partial(base_kernel, n, nvar),
        "base",
        field,
        table,
        jacobians,
        stepped,
        near,
        beyond,
        own_cell,
        own_rows,
        *[cell_of[k] for k in far],
        *[beyond_volumes[k] for k in far],
    )
    shared, base = call(
        functools.partial(far_step_kernel, n, nvar),
        "far_step",
        [f32(nvar * depth + 16, columns), field],
        table,
        stepped,
        base,
        edge,
        *[edge_of[k] for k in far],
        *[state_of[k] for k in far],
        *[cell_of[k] for k in far],
        *parts,
        *[transforms[k] for k in far],
    )
    rims = call(
        functools.partial(rim_kernel, n, nvar),
        "rims",
        f32(3 * nvar + 1, 2, columns),
        table,
        jacobians,
        edge,
        kept,
        others,
        near,
        stepped,
        *[edge_of[k] for k in far],
    )
    return call(
        functools.partial(final_kernel, nvar),
        "final",
        f32(1, nvar, depth, columns),
        jacobians,
        rims,
        kept,
        base,
        swapped(shared, 1),
        scratch=[pltpu.VMEM((nvar, depth, columns), jnp.float32), pltpu.SemaphoreType.DMA((3,))],
        out_spec=hbm,
    )


def solution(mesh):
    return jax.shard_map(
        body,
        mesh=mesh,
        in_specs=(
            P(("grp", "inst"), None, "slab", None),
            P(("grp", "inst"), "slab", None),
            P(("grp", "inst"), None, "slab", None),
            P(("grp", "inst"), None, "slab", None),
            P("slab", None),
            P(),
        ),
        out_specs=P(("grp", "inst"), None, "slab", None),
        check_vma=False,
    )
```

time: 73.5 us -> 23.3 us (0.32)
  matrix products: 16.5 us -> 0 us
  between operations: 13.9 us -> 0.14 us
  Pallas kernels: 0 us -> 11.1 us
  waiting for transfers between devices: 12.3 us -> 1.66 us
  local copies, waits for them, and re-layouts: 8.29 us -> 0.01 us
  other arithmetic: 8.2 us -> 0 us
  blocking collectives: 7.77 us -> 0 us
  starting transfers between devices: 6.09 us -> 10.2 us
    dot_general x11 -> x0, matrix products: 16.5 us -> none  [the longest x2 8.48 us: body(): jnp.einsum('m,mvac->vac', coefficients, block_part, precision=lax.Precisi...]
    pallas_call x0 -> x12, Pallas kernels: none -> 11.1 us  [the longest x11 9.93 us: call(): pl.pallas_call(kernel, out_shape=shapes, in_specs=[smem if x is table or...]
    all_gather x2 -> x0, waiting for transfers between devices: 8.17 us -> none  [body(): block_part = lax.all_gather(flow_field, 'inst', axis=0, tiled=True)]
    all_gather x1 -> x0, blocking collectives: 7.77 us -> none  [body(): volume_block_part = lax.all_gather(volumes, 'inst', axis=0, tiled=True)]
    ppermute x4 -> x10, starting transfers between devices: 6.05 us -> 10.2 us  [the longest x8 6.08 us: swapped(): return lax.ppermute(x, 'inst', [(i, i ^ k) for i in range(n)])]
    sort x1 -> x0, other arithmetic: 3.84 us -> none  [body(): order_own = jnp.argsort(links_own)]
    gather x8 -> x0, local copies, waits for them, and re-layouts: 3.22 us -> none  [the longest x4 1.62 us: body(): sent_flux = jnp.take(row_flux[:, :, 0, :], order_own, axis=2)]
    slice x13 -> x0, local copies, waits for them, and re-layouts: 2.28 us -> none  [the longest x1 0.79 us: body(): previous = from_behind(flow_field[:, :, row_count - 1, :], 'slab', 1)]
  transfers between devices with their start and end apart: 6 -> 10, of which waited for: 2 -> 3; matrix products, arithmetic and copies ran while one was open for 41% -> 0% of each run, Pallas kernels for 0% -> 38%
where the time goes in v3:
time: 23.3 us; the launch traced here: 23.1 us
  Pallas kernels  11.1 us (48%)
  starting transfers between devices  10.2 us (44%)
  waiting for transfers between devices  1.66 us (7%)
    pallas_call x11, Pallas kernels, call(): pl.pallas_call(kernel, out_shape=shapes, in_specs=[smem if x is table or...  9.93 us
    ppermute x8, starting transfers between devices, swapped(): return lax.ppermute(x, 'inst', [(i, i ^ k) for i in range(n)])  6.08 us
    ppermute x1, starting transfers between devices, body(): lax.ppermute(upward, 'slab', [(i, (i + 1) % slabs) for i in range(slabs)])  2.1 us
    ppermute x1, starting transfers between devices, body(): lax.ppermute(downward, 'slab', [(i, (i - 1) % slabs) for i in range(slabs)])  2.03 us
    pallas_call x1, Pallas kernels, body(): pl.pallas_call(pack_kernel, out_shape=[f32(nvar + 1, depth, columns), f32...  1.2 us
    ppermute x8, waiting for transfers between devices, swapped(): return lax.ppermute(x, 'inst', [(i, i ^ k) for i in range(n)])  0.89 us
    ppermute x1, waiting for transfers between devices, body(): lax.ppermute(downward, 'slab', [(i, (i - 1) % slabs) for i in range(slabs)])  0.77 us
  transfers between devices with their start and end apart: 10, of which 3 were waited for; matrix products, arithmetic and copies ran while one was open for 0% of the time, Pallas kernels for 38%

profile of v3, /device:TPU:0, one launch (start us, length us, event | category | flops | bytes accessed | tf_op | source)
XLA Modules:
  0.0 23.1 jit_solution(802606112538625602)
XLA Ops:
  0.0 2.9 %collective-permute-start.3 = (f32[1,5,64,256]{3,2,1,0:T(8,128)}, f32[1,5,64,256]{3,2,1,0:T(8,128)S(1)}, u32[]{:S(2)}, u32[]{:S(2)}) collective-permute-start(f32[1,5,64,256]{3,2,1,0:T(8,128)} %states.2), channel_id=1, source_target_pairs={{0,8},{4,12},{8,0},{12,4},{1,9},{5,13},{9,1},{13,5},{2,10},{6,14},... | collective-permute-start | bytes 983048 | tf_op jit(solution)/shard_map/ppermute | solution.py:505
  2.9 1.2 %pack.1 = (f32[6,64,256]{2,1,0:T(8,128)S(1)}, f32[3,64,256]{2,1,0:T(8,128)S(1)}, f32[2,64,256]{2,1,0:T(8,128)S(1)}, s32[1,256]{1,0:T(1,128)S(1)}, f32[32,256]{1,0:T(8,128)S(1)}, /*index=5*/f32[24,256]{1,0:T(8,128)S(1)}) custom-call(f32[1,5,64,256]{3,2,1,0:T(8,128)} %states.2, f32[1,64,256]{2,1,0:T(8,128)} %volumes.2, f32[1,2,64,256]{3,2,1,0:T(8,128)} %row_normals.1, ...), custom_call_target="tpu_custom_call" | custom-call | tf_op jit(solution)/shard_map/pack/pallas_call | solution.py:512
  4.1 0.0 copy-start.1
  4.2 0.1 collective-permute-start.2
  4.2 0.1 collective-permute-start.4
  4.3 2.1 %collective-permute-start = (f32[32,256]{1,0:T(8,128)S(1)}, f32[32,256]{1,0:T(8,128)S(1)}, u32[]{:S(2)}, u32[]{:S(2)}) collective-permute-start(f32[32,256]{1,0:T(8,128)S(1)} %get-tuple-element.21), channel_id=1, source_target_pairs={{0,1},{1,2},{2,3},{3,0},{4,5},{5,6},{6,7},{7,4},{8,9},{9,10},{10,1... | collective-permute-start | bytes 98312 | tf_op jit(solution)/shard_map/ppermute | solution.py:529
  6.4 2.0 %collective-permute-start.1 = (f32[24,256]{1,0:T(8,128)S(1)}, f32[24,256]{1,0:T(8,128)S(1)}, u32[]{:S(2)}, u32[]{:S(2)}) collective-permute-start(f32[24,256]{1,0:T(8,128)S(1)} %get-tuple-element.22), channel_id=1, source_target_pairs={{0,3},{1,0},{2,1},{3,2},{4,7},{5,4},{6,5},{7,6},{8,11},{9,8},{10,9... | collective-permute-start | bytes 73736 | tf_op jit(solution)/shard_map/ppermute | solution.py:530
  8.4 0.0 copy-done.1
  8.4 1.4 %own_flux.1.early.refs_5_ = f32[5,64,256]{2,1,0:T(8,128)S(1)} custom-call(f32[2,5,5]{2,1,0:T(8,128)S(1)} %copy.14.jacobians, f32[6,64,256]{2,1,0:T(8,128)S(1)} %get-tuple-element.23.near, f32[3,64,256]{2,1,0:T(8,128)S(1)} %get-tuple-element.26.cell, f32[2,64,256]{2,1,0:T(8,128)S(1)} %get-tuple-element.24.row_normals), custom_call_target="tpu_custom_call" | custom-call | tf_op jit(solution)/shard_map/own_flux/pallas_call | solution.py:494
  9.8 0.8 %collective-permute-done.1.above = f32[24,256]{1,0:T(8,128)S(1)} collective-permute-done((f32[24,256]{1,0:T(8,128)S(1)}, f32[24,256]{1,0:T(8,128)S(1)}, u32[]{:S(2)}, u32[]{:S(2)}) %collective-permute-start.1) | collective-permute-done | bytes 24608 | tf_op jit(solution)/shard_map/ppermute | solution.py:530
  10.6 0.0 collective-permute-done.below
  10.6 0.9 %edges.1 = (f32[152,256]{1,0:T(8,128)S(1)}, f32[13,2,256]{2,1,0:T(2,128)S(1)}) custom-call(f32[2,5,5]{2,1,0:T(8,128)S(1)} %copy.14.jacobians, f32[32,256]{1,0:T(8,128)S(1)} %collective-permute-done.below, f32[24,256]{1,0:T(8,128)S(1)} %collective-permute-done.1.above, f32[6,64,256]{2,1,0:T(8,128)S(1)} %get-tuple-element.23.near, ...), custom_call_target="tpu_custom_call" | custom-call | tf_op jit(solution)/shard_map/edges/pallas_call | solution.py:494
  11.5 0.2 collective-permute-done.3.states.refs_0_.refs_1_
  11.7 0.1 collective-permute-start.5
  11.8 2.1 %collective-permute-start.8 = (f32[152,256]{1,0:T(8,128)S(1)}, f32[152,256]{1,0:T(8,128)S(1)}, u32[]{:S(2)}, u32[]{:S(2)}) collective-permute-start(f32[152,256]{1,0:T(8,128)S(1)} %get-tuple-element.27.before.edge), channel_id=1, source_target_pairs={{0,8},{4,12},{8,0},{12,4},{1,9},{5,13},{9,1},{13,5},{2,10},{6,14},... | collective-permute-start | bytes 466952 | tf_op jit(solution)/shard_map/ppermute | solution.py:505
  13.9 0.2 collective-permute-start.6
  14.1 1.0 %behind.1.before.others = f32[5,2,256]{2,1,0:T(2,128)S(1)} custom-call(f32[2,5,5]{2,1,0:T(8,128)S(1)} %copy.14.jacobians, f32[32,256]{1,0:T(8,128)S(1)} %collective-permute-done.below, f32[24,256]{1,0:T(8,128)S(1)} %collective-permute-done.1.above, s32[1,256]{1,0:T(1,128)S(1)} %get-tuple-element.25.links), custom_call_target="tpu_custom_call" | custom-call | tf_op jit(solution)/shard_map/behind/pallas_call | solution.py:494
  15.1 0.0 collective-permute-done.4.cells.cell.refs_1_.refs_0_.refs_2_
  15.1 0.4 %collective-permute-start.7 = (f32[1,64,256]{2,1,0:T(8,128)S(1)}, f32[1,64,256]{2,1,0:T(8,128)S(1)}, u32[]{:S(2)}, u32[]{:S(2)}) collective-permute-start(f32[1,64,256]{2,1,0:T(8,128)S(1)} %volumes.3), channel_id=1, source_target_pairs={{0,4},{4,0},{8,12},{12,8},{1,5},{5,1},{9,13},{13,9},{2,6},{6,2},{1... | collective-permute-start | bytes 196616 | tf_op jit(solution)/shard_map/ppermute | solution.py:505
  15.6 1.2 %far_col.1 = (f32[5,64,256]{2,1,0:T(8,128)S(1)}, f32[2,5,64,256]{3,2,1,0:T(8,128)S(1)}) custom-call(f32[2,5,5]{2,1,0:T(8,128)S(1)} %copy.14.jacobians, f32[1,5,64,256]{3,2,1,0:T(8,128)S(1)} %collective-permute-done.3.states.refs_0_.refs_1_, f32[3,64,256]{2,1,0:T(8,128)S(1)} %collective-permute-done.4.cells.cell.refs_1_.refs_0_.refs_2_), custom_call_target="tpu_custom_call" | custom-call | tf_op jit(solution)/shard_map/far_col/pallas_call | solution.py:494
  16.7 0.0 collective-permute-done.7.refs_4_.refs_1_
  16.7 0.0 collective-permute-done.2.beyond
  16.7 0.0 collective-permute-done.6.refs_3_
  16.7 0.0 collective-permute-done.5.refs_2_
  16.8 0.9 %time.1 = (f32[5,64,256]{2,1,0:T(8,128)S(1)}, f32[5,64,256]{2,1,0:T(8,128)S(1)}) custom-call(f32[4,4]{1,0:T(4,128)S(1)} %copy-done, f32[6,64,256]{2,1,0:T(8,128)S(1)} %get-tuple-element.23.near, f32[6,64,256]{2,1,0:T(8,128)S(1)} %collective-permute-done.2.beyond, f32[152,256]{1,0:T(8,128)S(1)} %get-tuple-element.27.before.edge, ...), custom_call_target="tpu_custom_call" | custom-call | tf_op jit(solution)/shard_map/time/pallas_call | solution.py:494
  17.6 1.4 %base.1 = f32[5,64,256]{2,1,0:T(8,128)S(1)} custom-call(f32[4,4]{1,0:T(4,128)S(1)} %copy-done, f32[2,5,5]{2,1,0:T(8,128)S(1)} %copy.14.jacobians, f32[5,64,256]{2,1,0:T(8,128)S(1)} %get-tuple-element.32.stepped, f32[6,64,256]{2,1,0:T(8,128)S(1)} %get-tuple-element.23.near, f32[6,64,256]{2,1,0:T(8,128)S(1)} %collective-permute-done.2.beyond, ...), custom_call_target="tpu_custom_call" | custom-call | tf_op jit(solution)/shard_map/base/pallas_call | solution.py:494
  19.1 0.0 collective-permute-done.8.refs_0_
  19.1 0.9 %far_step.1 = (f32[336,256]{1,0:T(8,128)S(1)}, f32[5,64,256]{2,1,0:T(8,128)S(1)}) custom-call(f32[4,4]{1,0:T(4,128)S(1)} %copy-done, f32[5,64,256]{2,1,0:T(8,128)S(1)} %get-tuple-element.32.stepped, f32[5,64,256]{2,1,0:T(8,128)S(1)} %base.1, f32[152,256]{1,0:T(8,128)S(1)} %get-tuple-element.27.before.edge, f32[152,256]{1,0:T(8,128)S(1)} %collective-permute-done.8.refs_0_, ...), custom_call_target="tpu_custom_call" | custom-call | tf_op jit(solution)/shard_map/far_step/pallas_call | solution.py:494
  20.0 0.2 collective-permute-start.9
  20.2 0.8 %rims.1 = f32[16,2,256]{2,1,0:T(2,128)S(1)} custom-call(f32[4,4]{1,0:T(4,128)S(1)} %copy-done, f32[2,5,5]{2,1,0:T(8,128)S(1)} %copy.14.jacobians, f32[152,256]{1,0:T(8,128)S(1)} %get-tuple-element.27.before.edge, f32[13,2,256]{2,1,0:T(2,128)S(1)} %get-tuple-element.28.kept, f32[5,2,256]{2,1,0:T(2,128)S(1)} %behind.1.before.others, ...), custom_call_target="tpu_custom_call" | custom-call | tf_op jit(solution)/shard_map/rims/pallas_call | solution.py:494
  21.0 0.7 %collective-permute-done.9.shared = f32[336,256]{1,0:T(8,128)S(1)} collective-permute-done((f32[336,256]{1,0:T(8,128)S(1)}, f32[336,256]{1,0:T(8,128)S(1)}, u32[]{:S(2)}, u32[]{:S(2)}) %collective-permute-start.9) | collective-permute-done | bytes 344096 | tf_op jit(solution)/shard_map/ppermute | solution.py:505
  21.7 1.4 %final.1 = f32[1,5,64,256]{3,2,1,0:T(8,128)} custom-call(f32[2,5,5]{2,1,0:T(8,128)S(1)} %copy.14.jacobians, f32[16,2,256]{2,1,0:T(2,128)S(1)} %rims.1, f32[13,2,256]{2,1,0:T(2,128)S(1)} %get-tuple-element.28.kept, f32[5,64,256]{2,1,0:T(8,128)S(1)} %get-tuple-element.35.base, f32[336,256]{1,0:T(8,128)S(1)} %collective-permute-done.9.shared), custom_call_target="tpu_custom_call" | custom-call | tf_op jit(solution)/shard_map/final/pallas_call | solution.py:494
  (5 shorter events, 0.0 us)
Async XLA Ops:
  0.0 11.7 %collective-permute-start.3 = (f32[1,5,64,256]{3,2,1,0:T(8,128)}, f32[1,5,64,256]{3,2,1,0:T(8,128)S(1)}, u32[]{:S(2)}, u32[]{:S(2)}) collective-permute-start(f32[1,5,64,256]{3,2,1,0:T(8,128)} %states.2), channel_id=1, source_target_pairs={{0,8},{4,12},{8,0},{12,4},{1,9},{5,13},{9,1},{13,5},{2,10},{6,14},... | collective-permute-start | bytes 983048 | tf_op jit(solution)/shard_map/ppermute | solution.py:505
  4.1 4.3 %copy-start.1 = (f32[2,5,5]{2,0,1:T(2,128)S(1)}, f32[2,5,5]{2,0,1:T(2,128)}, u32[]{:S(2)}) copy-start(f32[2,5,5]{2,0,1:T(2,128)} %param.12) | copy-start | bytes 604
  4.2 12.6 %collective-permute-start.2 = (f32[6,64,256]{2,1,0:T(8,128)S(1)}, f32[6,64,256]{2,1,0:T(8,128)S(1)}, u32[]{:S(2)}, u32[]{:S(2)}) collective-permute-start(f32[6,64,256]{2,1,0:T(8,128)S(1)} %get-tuple-element.23.near), channel_id=1, source_target_pairs={{0,4},{4,0},{8,12},{12,8},{1,5},{5,1},{9,13},{13,9},{2,6},{6,2},{1... | collective-permute-start | bytes 1179656 | tf_op jit(solution)/shard_map/ppermute | solution.py:505
  4.2 10.9 %collective-permute-start.4 = (f32[3,64,256]{2,1,0:T(8,128)S(1)}, f32[3,64,256]{2,1,0:T(8,128)S(1)}, u32[]{:S(2)}, u32[]{:S(2)}) collective-permute-start(f32[3,64,256]{2,1,0:T(8,128)S(1)} %get-tuple-element.26.cell), channel_id=1, source_target_pairs={{0,8},{4,12},{8,0},{12,4},{1,9},{5,13},{9,1},{13,5},{2,10},{6,14},... | collective-permute-start | bytes 589832 | tf_op jit(solution)/shard_map/ppermute | solution.py:505
  4.3 6.3 %collective-permute-start = (f32[32,256]{1,0:T(8,128)S(1)}, f32[32,256]{1,0:T(8,128)S(1)}, u32[]{:S(2)}, u32[]{:S(2)}) collective-permute-start(f32[32,256]{1,0:T(8,128)S(1)} %get-tuple-element.21), channel_id=1, source_target_pairs={{0,1},{1,2},{2,3},{3,0},{4,5},{5,6},{6,7},{7,4},{8,9},{9,10},{10,1... | collective-permute-start | bytes 98312 | tf_op jit(solution)/shard_map/ppermute | solution.py:529
  6.4 4.2 %collective-permute-start.1 = (f32[24,256]{1,0:T(8,128)S(1)}, f32[24,256]{1,0:T(8,128)S(1)}, u32[]{:S(2)}, u32[]{:S(2)}) collective-permute-start(f32[24,256]{1,0:T(8,128)S(1)} %get-tuple-element.22), channel_id=1, source_target_pairs={{0,3},{1,0},{2,1},{3,2},{4,7},{5,4},{6,5},{7,6},{8,11},{9,8},{10,9... | collective-permute-start | bytes 73736 | tf_op jit(solution)/shard_map/ppermute | solution.py:530
  11.7 5.0 %collective-permute-start.5 = (f32[3,64,256]{2,1,0:T(8,128)S(1)}, f32[3,64,256]{2,1,0:T(8,128)S(1)}, u32[]{:S(2)}, u32[]{:S(2)}) collective-permute-start(f32[3,64,256]{2,1,0:T(8,128)S(1)} %get-tuple-element.29), channel_id=1, source_target_pairs={{0,4},{4,0},{8,12},{12,8},{1,5},{5,1},{9,13},{13,9},{2,6},{6,2},{1... | collective-permute-start | bytes 589832 | tf_op jit(solution)/shard_map/ppermute | solution.py:505
  11.8 7.3 %collective-permute-start.8 = (f32[152,256]{1,0:T(8,128)S(1)}, f32[152,256]{1,0:T(8,128)S(1)}, u32[]{:S(2)}, u32[]{:S(2)}) collective-permute-start(f32[152,256]{1,0:T(8,128)S(1)} %get-tuple-element.27.before.edge), channel_id=1, source_target_pairs={{0,8},{4,12},{8,0},{12,4},{1,9},{5,13},{9,1},{13,5},{2,10},{6,14},... | collective-permute-start | bytes 466952 | tf_op jit(solution)/shard_map/ppermute | solution.py:505
  13.9 2.8 %collective-permute-start.6 = (f32[2,64,256]{2,1,0:T(8,128)S(1)}, f32[2,64,256]{2,1,0:T(8,128)S(1)}, u32[]{:S(2)}, u32[]{:S(2)}) collective-permute-start(f32[2,64,256]{2,1,0:T(8,128)S(1)} %get-tuple-element.30), channel_id=1, source_target_pairs={{0,4},{4,0},{8,12},{12,8},{1,5},{5,1},{9,13},{13,9},{2,6},{6,2},{1... | collective-permute-start | bytes 393224 | tf_op jit(solution)/shard_map/ppermute | solution.py:505
  15.1 1.6 %collective-permute-start.7 = (f32[1,64,256]{2,1,0:T(8,128)S(1)}, f32[1,64,256]{2,1,0:T(8,128)S(1)}, u32[]{:S(2)}, u32[]{:S(2)}) collective-permute-start(f32[1,64,256]{2,1,0:T(8,128)S(1)} %volumes.3), channel_id=1, source_target_pairs={{0,4},{4,0},{8,12},{12,8},{1,5},{5,1},{9,13},{13,9},{2,6},{6,2},{1... | collective-permute-start | bytes 196616 | tf_op jit(solution)/shard_map/ppermute | solution.py:505
  15.5 1.2 %copy-start = (f32[4,4]{1,0:T(4,128)S(1)}, f32[4,4]{1,0:T(4,128)}, u32[]{:S(2)}) copy-start(f32[4,4]{1,0:T(4,128)} %constant.2.clone.table) | copy-start | bytes 196
  20.0 1.7 %collective-permute-start.9 = (f32[336,256]{1,0:T(8,128)S(1)}, f32[336,256]{1,0:T(8,128)S(1)}, u32[]{:S(2)}, u32[]{:S(2)}) collective-permute-start(f32[336,256]{1,0:T(8,128)S(1)} %get-tuple-element.36), channel_id=1, source_target_pairs={{0,4},{4,0},{8,12},{12,8},{1,5},{5,1},{9,13},{13,9},{2,6},{6,2},{1... | collective-permute-start | bytes 1032200 | tf_op jit(solution)/shard_map/ppermute | solution.py:505

commit v4 on v3

--- a/solution.py
+++ b/solution.py
@@ -22,7 +22,7 @@
     parity = np.where(offsets % 2 == 0, 1.0, -1.0)
     matrix = np.where(offsets == 0, 0.0, 0.5 * frequency * parity * np.cos(phases) / sine_safe)
     matrix = matrix + nyquist_damping * parity
-    return jnp.asarray(matrix, jnp.float32)
+    return matrix.astype(np.float32)
 
 
 def pack_kernel(states, volumes, row_normals, col_normals, links, near, cell, rows, own_links, upward, downward, sems):
@@ -57,13 +57,20 @@
     downward[pl.ds(2 * nvar + 7, 1), :] = own_links[...].astype(jnp.float32)
 
 
-def half_jacobians(jacobians, nvar):
-    return [[[0.5 * jacobians[d, v, w] for w in range(nvar)] for v in range(nvar)] for d in range(2)]
-
-
-def step_weight(table, row, col):
+def half_jacobians(coefs, nvar):
+    return [
+        [[coefs[pl.ds((d * nvar + v) * nvar + w, 1), :] for w in range(nvar)] for v in range(nvar)]
+        for d in range(2)
+    ]
+
+
+def step_weight(n, row, col):
     me = lax.axis_index("inst")
-    return pseudo_step * table[jnp.bitwise_xor(me, row), jnp.bitwise_xor(me, col)]
+    values = [np.float32(pseudo_step) * spectral_table(n)[i ^ row, i ^ col] for i in range(n)]
+    weight = values[0]
+    for i in range(1, n):
+        weight = jnp.where(me == i, values[i], weight)
+    return weight
 
 
 def weighted(weights, values):
@@ -204,9 +211,9 @@
     return [stack[pl.ds(2 * t, 2), :] for t in range(len(rows))]
 
 
-def edge_kernel(nvar, jacobians, below, above, near, row_normals, links, early, out, kept, stack):
+def edge_kernel(nvar, coefs, below, above, near, row_normals, links, early, out, kept, stack):
     depth, columns = near.shape[1], near.shape[2]
-    half = half_jacobians(jacobians, nvar)
+    half = half_jacobians(coefs, nvar)
     is_below = lax.broadcasted_iota(jnp.int32, (2, columns), 0) == 0
     inner_face = [
         pair(row_normals[d, pl.ds(0, 1), :], above[pl.ds(2 * nvar + 5 + d, 1), :]) for d in range(2)
@@ -239,8 +246,8 @@
         out[pl.ds(head + d * depth, depth), :] = row_normals[d]
 
 
-def behind_kernel(nvar, jacobians, below, above, links, out, stack):
-    half = half_jacobians(jacobians, nvar)
+def behind_kernel(nvar, coefs, below, above, links, out, stack):
+    half = half_jacobians(coefs, nvar)
     is_below = lax.broadcasted_iota(jnp.int32, (2, links.shape[1]), 0) == 0
 
     def with_j(values):
@@ -264,13 +271,19 @@
         at += out.shape[0]
 
 
-def volume_kernel(cells, before, out):
+def volume_kernel(cells, before, also, out):
     out[...] = cells[pl.ds(0, 1)]
 
 
-def own_flux_kernel(nvar, jacobians, near, cell, row_normals, out):
+def own_flux_kernel(nvar, jacobians, near, cell, row_normals, out, coefs):
     strips = out.shape[1] // STRIP
-    half = half_jacobians(jacobians, nvar)
+    for d in range(2):
+        for v in range(nvar):
+            for w in range(nvar):
+                coefs[pl.ds((d * nvar + v) * nvar + w, 1), :] = jnp.full(
+                    (1, coefs.shape[1]), 0.5 * jacobians[d, v, w], jnp.float32
+                )
+    half = half_jacobians(coefs, nvar)
 
     def at(s):
         cells = [near[v, strip(s), :] for v in range(nvar)]
@@ -283,9 +296,9 @@
             out[v, strip(s), :] = cells[v] - factor * (along[v] + beside[v])
 
 
-def far_col_kernel(nvar, jacobians, states, cell, out, out_j):
+def far_col_kernel(nvar, coefs, states, cell, out, out_j):
     strips = out.shape[1] // STRIP
-    half = half_jacobians(jacobians, nvar)
+    half = half_jacobians(coefs, nvar)
     for s in range(strips):
         cells = [states[0, v, strip(s), :] for v in range(nvar)]
         cells_j = transformed(half, cells)
@@ -297,15 +310,15 @@
                 out_j[d, v, strip(s), :] = cells_j[d][v]
 
 
-def time_kernel(n, nvar, table, near, beyond, edge, *refs):
+def time_kernel(n, nvar, near, beyond, edge, *refs):
     far = n // 2 - 1
-    states, cells, *pieces, beyond_volumes = [refs[far * t : far * (t + 1)] for t in range(5)]
-    parts, outs = refs[5 * far : 6 * far + 1], refs[6 * far + 1 :]
+    states, cells, *pieces, beyond_volumes = [refs[far * t : far * (t + 1)] for t in range(6)]
+    parts, outs = refs[6 * far : 7 * far + 1], refs[7 * far + 1 :]
     beyond_states = [[x.at[v] for x in piece for v in range(x.shape[0])] for piece in zip(*pieces)]
     count = far + 1
     weights = [
-        [step_weight(table, 2 * a, 2 * b) for b in range(count)]
-        + [step_weight(table, 2 * a, 2 * b + 1) for b in range(count)]
+        [step_weight(n, 2 * a, 2 * b) for b in range(count)]
+        + [step_weight(n, 2 * a, 2 * b + 1) for b in range(count)]
         for a in range(count)
     ]
     strips = outs[0].shape[1] // STRIP
@@ -330,13 +343,13 @@
                 outs[a][v, strip(s), :] = moved[a]
 
 
-def base_kernel(n, nvar, table, jacobians, stepped, near, beyond, cell, row_normals, *refs):
+def base_kernel(n, nvar, coefs, stepped, near, beyond, cell, row_normals, *refs):
     far = n // 2 - 1
     cells_of, beyond_volumes, out = refs[:far], refs[far : 2 * far], refs[2 * far]
     strips = out.shape[1] // STRIP
-    half = half_jacobians(jacobians, nvar)
-    weights = [step_weight(table, 0, 2 * b) for b in range(far + 1)]
-    weights = weights + [step_weight(table, 0, 2 * b + 1) for b in range(far + 1)]
+    half = half_jacobians(coefs, nvar)
+    weights = [step_weight(n, 0, 2 * b) for b in range(far + 1)]
+    weights = weights + [step_weight(n, 0, 2 * b + 1) for b in range(far + 1)]
 
     def at(s):
         cells = [stepped[v, strip(s), :] for v in range(nvar)]
@@ -352,14 +365,14 @@
             out[v, strip(s), :] = kept * cells[v] - (pseudo_step * inverse) * (along[v] + beside[v])
 
 
-def far_step_kernel(n, nvar, table, stepped, base, edge, *refs):
+def far_step_kernel(n, nvar, stepped, edge, *refs):
     far = n // 2 - 1
     edges, states, cells_of, parts, transforms = [refs[far * t : far * (t + 1)] for t in range(5)]
     shared, out = refs[5 * far :]
     depth = stepped.shape[1]
     strips = depth // STRIP
-    mine = [step_weight(table, 0, 2 * b) for b in range(far + 1)]
-    other = [step_weight(table, 1, 2 * b) for b in range(far + 1)]
+    mine = [step_weight(n, 0, 2 * b) for b in range(far + 1)]
+    other = [step_weight(n, 1, 2 * b) for b in range(far + 1)]
     head = edge.shape[0] - 2 * depth
 
     def changes(a):
@@ -377,11 +390,11 @@
         factors = [pseudo_step / cells_of[a][0, strip(s), :] for a in range(far)]
         for v in range(nvar):
             given = other[0] * stepped[v, strip(s), :]
-            taken = base[v, strip(s), :]
+            taken = None
             for a in range(far):
                 value = parts[a][v, strip(s), :] - factors[a] * moves[a][3][v]
                 given = given + other[1 + a] * value
-                taken = taken - mine[1 + a] * value
+                taken = mine[1 + a] * value if taken is None else taken + mine[1 + a] * value
             shared[pl.ds(v * depth + s * STRIP, STRIP), :] = given
             out[v, strip(s), :] = taken
     rims = pl.ds(2 * nvar, 2 * nvar + 2)
@@ -390,12 +403,12 @@
     )
 
 
-def rim_kernel(n, nvar, table, jacobians, edge, kept, others, near, stepped, *refs):
+def rim_kernel(n, nvar, coefs, edge, kept, others, near, stepped, *refs):
     far = n // 2 - 1
     edges, out = refs[:far], refs[far]
     depth, columns = stepped.shape[1], stepped.shape[2]
-    half = half_jacobians(jacobians, nvar)
-    weights = [step_weight(table, 0, 2 * b) for b in range(far + 1)]
+    half = half_jacobians(coefs, nvar)
+    weights = [step_weight(n, 0, 2 * b) for b in range(far + 1)]
     is_below = lax.broadcasted_iota(jnp.int32, (2, columns), 0) == 0
     at = 2 * nvar
 
@@ -428,17 +441,18 @@
     out[3 * nvar] = jnp.where(is_below, factor, -factor)
 
 
-def final_kernel(nvar, jacobians, rims, kept, base, shared, out, held, sems):
+def final_kernel(nvar, coefs, rims, kept, base, taken, shared, out, held, sems):
     depth, columns = base.shape[1], base.shape[2]
     strips = depth // STRIP
-    half = half_jacobians(jacobians, nvar)
+    half = half_jacobians(coefs, nvar)
     is_below = lax.broadcasted_iota(jnp.int32, (2, columns), 0) == 0
 
     def summed(v):
         return pair(shared[pl.ds(nvar * depth + v, 1), :], shared[pl.ds(nvar * depth + nvar + 1 + v, 1), :])
 
     def value(v, s):
-        return base[v, strip(s), :] - shared[pl.ds(v * depth + s * STRIP, STRIP), :]
+        other = taken[v, strip(s), :] + shared[pl.ds(v * depth + s * STRIP, STRIP), :]
+        return base[v, strip(s), :] - other
 
     copies = []
 
@@ -487,14 +501,13 @@
     smem = pl.BlockSpec(memory_space=pltpu.SMEM)
     hbm = pl.BlockSpec(memory_space=pltpu.HBM)
     params = pltpu.CompilerParams(vmem_limit_bytes=24 * 1024 * 1024)
-    table = spectral_table(n)
 
     def call(kernel, name, shapes, *operands, scratch=(), out_spec=vmem):
         single = not isinstance(shapes, list)
         return pl.pallas_call(
             kernel,
             out_shape=shapes,
-            in_specs=[smem if x is table or x is jacobians else vmem for x in operands],
+            in_specs=[smem if x is jacobians else vmem for x in operands],
             out_specs=out_spec if single else [out_spec] * len(shapes),
             scratch_shapes=list(scratch),
             compiler_params=params,
@@ -529,27 +542,34 @@
     below = lax.ppermute(upward, "slab", [(i, (i + 1) % slabs) for i in range(slabs)])
     above = lax.ppermute(downward, "slab", [(i, (i - 1) % slabs) for i in range(slabs)])
     field = f32(nvar, depth, columns)
-    parts = [
-        call(functools.partial(own_flux_kernel, nvar), "own_flux", field, jacobians, near, own_cell, own_rows)
-    ]
+    own_part, coefs = call(
+        functools.partial(own_flux_kernel, nvar),
+        "own_flux",
+        [field, f32(-(-2 * nvar * nvar // 8) * 8, columns)],
+        jacobians,
+        near,
+        own_cell,
+        own_rows,
+    )
+    parts = [own_part]
     edge, kept = call(
         functools.partial(edge_kernel, nvar),
         "edges",
         [f32(head + 2 * depth, columns), f32(2 * nvar + 3, 2, columns)],
-        jacobians,
+        coefs,
         below,
         above,
         near,
         own_rows,
         own_links,
-        parts[0],
+        own_part,
         scratch=[pltpu.VMEM((-(-(2 * nvar + 6) // 8) * 8, columns), jnp.float32)],
     )
     others = call(
         functools.partial(behind_kernel, nvar),
         "behind",
         f32(nvar, 2, columns),
-        jacobians,
+        coefs,
         below,
         above,
         own_links,
@@ -557,13 +577,13 @@
     )
     edge_of = {k: swapped(edge, k) for k in far}
     beyond = swapped(near, 1)
-    pieces = [f32(count, depth, columns) for count in (nvar - nvar // 2, nvar // 2)]
-    beyond_states = []
+    pieces = [f32(count, depth, columns) for count in (2, 2, nvar - 4)]
+    beyond_states, beyond_volumes = [], dict()
     for k in far:
-        beyond_states.append([swapped(x, 1) for x in call(state_kernel, "states", pieces, state_of[k], edge)])
-    beyond_volumes = {
-        k: swapped(call(volume_kernel, "volumes", f32(1, depth, columns), cell_of[k], others), 1) for k in far
-    }
+        copies = call(state_kernel, "states", pieces, state_of[k], edge)
+        beyond_states.append([swapped(x, 1) for x in copies])
+        held = call(volume_kernel, "volumes", f32(1, depth, columns), cell_of[k], others, copies[-1])
+        beyond_volumes[k] = swapped(held, 1)
 
     transforms = {}
     for k in far:
@@ -571,7 +591,7 @@
             functools.partial(far_col_kernel, nvar),
             "far_col",
             [field, f32(2, nvar, depth, columns)],
-            jacobians,
+            coefs,
             state_of[k],
             cell_of[k],
         )
@@ -580,7 +600,6 @@
         functools.partial(time_kernel, n, nvar),
         "time",
         [field] * (len(far) + 1),
-        table,
         near,
         beyond,
         edge,
@@ -588,6 +607,7 @@
         *[cell_of[k] for k in far],
         *[x[0] for x in beyond_states],
         *[x[1] for x in beyond_states],
+        *[x[2] for x in beyond_states],
         *[beyond_volumes[k] for k in far],
         *parts,
     )
@@ -595,8 +615,7 @@
         functools.partial(base_kernel, n, nvar),
         "base",
         field,
-        table,
-        jacobians,
+        coefs,
         stepped,
         near,
         beyond,
@@ -605,13 +624,11 @@
         *[cell_of[k] for k in far],
         *[beyond_volumes[k] for k in far],
     )
-    shared, base = call(
+    shared, taken = call(
         functools.partial(far_step_kernel, n, nvar),
         "far_step",
         [f32(nvar * depth + 16, columns), field],
-        table,
         stepped,
-        base,
         edge,
         *[edge_of[k] for k in far],
         *[state_of[k] for k in far],
@@ -623,8 +640,7 @@
         functools.partial(rim_kernel, n, nvar),
         "rims",
         f32(3 * nvar + 1, 2, columns),
-        table,
-        jacobians,
+        coefs,
         edge,
         kept,
         others,
@@ -636,10 +652,11 @@
         functools.partial(final_kernel, nvar),
         "final",
         f32(1, nvar, depth, columns),
-        jacobians,
+        coefs,
         rims,
         kept,
         base,
+        taken,
         swapped(shared, 1),
         scratch=[pltpu.VMEM((nvar, depth, columns), jnp.float32), pltpu.SemaphoreType.DMA((3,))],
         out_spec=hbm,

time: 23.3 us -> 21.4 us (0.918)
  Pallas kernels: 11.1 us -> 5.96 us
  waiting for transfers between devices: 1.66 us -> 5.2 us
  starting transfers between devices: 10.2 us -> 9.96 us
    pallas_call x11, Pallas kernels: 9.93 us -> 4.76 us  [call(): pl.pallas_call(kernel, out_shape=shapes, in_specs=[smem if x is jacobians...]
    ppermute x8 -> x9, waiting for transfers between devices: 0.89 us -> 4.47 us  [swapped(): return lax.ppermute(x, 'inst', [(i, i ^ k) for i in range(n)])]
    ppermute x8 -> x9, starting transfers between devices: 6.08 us -> 5.84 us  [swapped(): return lax.ppermute(x, 'inst', [(i, i ^ k) for i in range(n)])]
  transfers between devices with their start and end apart: 10 -> 11, of which waited for: 3 -> 6; matrix products, arithmetic and copies ran while one was open for 0% -> 0% of each run, Pallas kernels for 38% -> 23%
where the time goes in v4:
time: 21.4 us; the launch traced here: 21.2 us
  starting transfers between devices  9.96 us (47%)
  Pallas kernels  5.96 us (28%)
  waiting for transfers between devices  5.2 us (24%)
    ppermute x9, starting transfers between devices, swapped(): return lax.ppermute(x, 'inst', [(i, i ^ k) for i in range(n)])  5.84 us
    pallas_call x11, Pallas kernels, call(): pl.pallas_call(kernel, out_shape=shapes, in_specs=[smem if x is jacobians...  4.76 us
    ppermute x9, waiting for transfers between devices, swapped(): return lax.ppermute(x, 'inst', [(i, i ^ k) for i in range(n)])  4.47 us
    ppermute x1, starting transfers between devices, body(): lax.ppermute(upward, 'slab', [(i, (i + 1) % slabs) for i in range(slabs)])  2.1 us
    ppermute x1, starting transfers between devices, body(): lax.ppermute(downward, 'slab', [(i, (i - 1) % slabs) for i in range(slabs)])  2.03 us
    pallas_call x1, Pallas kernels, body(): pl.pallas_call(pack_kernel, out_shape=[f32(nvar + 1, depth, columns), f32...  1.2 us
    ppermute x1, waiting for transfers between devices, body(): lax.ppermute(downward, 'slab', [(i, (i - 1) % slabs) for i in range(slabs)])  0.73 us
  transfers between devices with their start and end apart: 11, of which 6 were waited for; matrix products, arithmetic and copies ran while one was open for 0% of the time, Pallas kernels for 23%

profile of v4, /device:TPU:0, one launch (start us, length us, event | category | flops | bytes accessed | tf_op | source)
XLA Modules:
  0.0 21.2 jit_solution(806484694334147115)
XLA Ops:
  0.0 2.9 %collective-permute-start.3 = (f32[1,5,64,256]{3,2,1,0:T(8,128)}, f32[1,5,64,256]{3,2,1,0:T(8,128)S(1)}, u32[]{:S(2)}, u32[]{:S(2)}) collective-permute-start(f32[1,5,64,256]{3,2,1,0:T(8,128)} %states.2), channel_id=1, source_target_pairs={{0,8},{4,12},{8,0},{12,4},{1,9},{5,13},{9,1},{13,5},{2,10},{6,14},... | collective-permute-start | bytes 983048 | tf_op jit(solution)/shard_map/ppermute | solution.py:518
  2.9 1.2 %pack.1 = (f32[6,64,256]{2,1,0:T(8,128)S(1)}, f32[3,64,256]{2,1,0:T(8,128)S(1)}, f32[2,64,256]{2,1,0:T(8,128)S(1)}, s32[1,256]{1,0:T(1,128)S(1)}, f32[32,256]{1,0:T(8,128)S(1)}, /*index=5*/f32[24,256]{1,0:T(8,128)S(1)}) custom-call(f32[1,5,64,256]{3,2,1,0:T(8,128)} %states.2, f32[1,64,256]{2,1,0:T(8,128)} %volumes.2, f32[1,2,64,256]{3,2,1,0:T(8,128)} %row_normals.1, ...), custom_call_target="tpu_custom_call" | custom-call | tf_op jit(solution)/shard_map/pack/pallas_call | solution.py:525
  4.1 0.0 copy-start
  4.2 0.1 collective-permute-start.2
  4.2 0.1 collective-permute-start.4
  4.3 2.1 %collective-permute-start = (f32[32,256]{1,0:T(8,128)S(1)}, f32[32,256]{1,0:T(8,128)S(1)}, u32[]{:S(2)}, u32[]{:S(2)}) collective-permute-start(f32[32,256]{1,0:T(8,128)S(1)} %get-tuple-element.28), channel_id=1, source_target_pairs={{0,1},{1,2},{2,3},{3,0},{4,5},{5,6},{6,7},{7,4},{8,9},{9,10},{10,1... | collective-permute-start | bytes 98312 | tf_op jit(solution)/shard_map/ppermute | solution.py:542
  6.4 2.0 %collective-permute-start.1 = (f32[24,256]{1,0:T(8,128)S(1)}, f32[24,256]{1,0:T(8,128)S(1)}, u32[]{:S(2)}, u32[]{:S(2)}) collective-permute-start(f32[24,256]{1,0:T(8,128)S(1)} %get-tuple-element.29), channel_id=1, source_target_pairs={{0,3},{1,0},{2,1},{3,2},{4,7},{5,4},{6,5},{7,6},{8,11},{9,8},{10,9... | collective-permute-start | bytes 73736 | tf_op jit(solution)/shard_map/ppermute | solution.py:543
  8.4 1.4 %own_flux.1 = (f32[5,64,256]{2,1,0:T(8,128)S(1)}, f32[56,256]{1,0:T(8,128)S(1)}) custom-call(f32[2,5,5]{2,1,0:T(8,128)S(1)} %copy.7.jacobians, f32[6,64,256]{2,1,0:T(8,128)S(1)} %get-tuple-element.24.near, f32[3,64,256]{2,1,0:T(8,128)S(1)} %get-tuple-element.25.cell, f32[2,64,256]{2,1,0:T(8,128)S(1)} %get-tuple-element.26.row_normals), custom_call_target="tpu_custom_call" | custom-call | tf_op jit(solution)/shard_map/own_flux/pallas_call | solution.py:507
  9.9 0.7 %collective-permute-done.1.above = f32[24,256]{1,0:T(8,128)S(1)} collective-permute-done((f32[24,256]{1,0:T(8,128)S(1)}, f32[24,256]{1,0:T(8,128)S(1)}, u32[]{:S(2)}, u32[]{:S(2)}) %collective-permute-start.1) | collective-permute-done | bytes 24608 | tf_op jit(solution)/shard_map/ppermute | solution.py:543
  10.6 0.0 collective-permute-done.below
  10.6 0.3 %edges.1 = (f32[152,256]{1,0:T(8,128)S(1)}, f32[13,2,256]{2,1,0:T(2,128)S(1)}) custom-call(f32[56,256]{1,0:T(8,128)S(1)} %get-tuple-element.27.coefs, f32[32,256]{1,0:T(8,128)S(1)} %collective-permute-done.below, f32[24,256]{1,0:T(8,128)S(1)} %collective-permute-done.1.above, f32[6,64,256]{2,1,0:T(8,128)S(1)} %get-tuple-element.24.near, ...), custom_call_target="tpu_custom_call" | custom-call | tf_op jit(solution)/shard_map/edges/pallas_call | solution.py:507
  10.9 1.6 %collective-permute-start.9 = (f32[152,256]{1,0:T(8,128)S(1)}, f32[152,256]{1,0:T(8,128)S(1)}, u32[]{:S(2)}, u32[]{:S(2)}) collective-permute-start(f32[152,256]{1,0:T(8,128)S(1)} %get-tuple-element.32.before.edge), channel_id=1, source_target_pairs={{0,8},{4,12},{8,0},{12,4},{1,9},{5,13},{9,1},{13,5},{2,10},{6,14},... | collective-permute-start | bytes 466952 | tf_op jit(solution)/shard_map/ppermute | solution.py:518
  12.4 0.0 collective-permute-done.3.states.refs_0_.refs_1_
  12.5 0.1 collective-permute-start.5
  12.5 0.5 %collective-permute-start.6 = (f32[2,64,256]{2,1,0:T(8,128)S(1)}, f32[2,64,256]{2,1,0:T(8,128)S(1)}, u32[]{:S(2)}, u32[]{:S(2)}) collective-permute-start(f32[2,64,256]{2,1,0:T(8,128)S(1)} %get-tuple-element.35), channel_id=1, source_target_pairs={{0,4},{4,0},{8,12},{12,8},{1,5},{5,1},{9,13},{13,9},{2,6},{6,2},{1... | collective-permute-start | bytes 393224 | tf_op jit(solution)/shard_map/ppermute | solution.py:518
  13.0 0.4 %behind.1.before.others = f32[5,2,256]{2,1,0:T(2,128)S(1)} custom-call(f32[56,256]{1,0:T(8,128)S(1)} %get-tuple-element.27.coefs, f32[32,256]{1,0:T(8,128)S(1)} %collective-permute-done.below, f32[24,256]{1,0:T(8,128)S(1)} %collective-permute-done.1.above, s32[1,256]{1,0:T(1,128)S(1)} %get-tuple-element.30.links), custom_call_target="tpu_custom_call" | custom-call | tf_op jit(solution)/shard_map/behind/pallas_call | solution.py:507
  13.4 2.5 %collective-permute-done.4.cells.cell.refs_1_.refs_0_.refs_2_ = f32[3,64,256]{2,1,0:T(8,128)S(1)} collective-permute-done((f32[3,64,256]{2,1,0:T(8,128)S(1)}, f32[3,64,256]{2,1,0:T(8,128)S(1)}, u32[]{:S(2)}, u32[]{:S(2)}) %collective-permute-start.4) | collective-permute-done | bytes 196640 | tf_op jit(solution)/shard_map/ppermute | solution.py:518
  15.9 0.0 collective-permute-start.7
  15.9 0.0 collective-permute-done.2.beyond
  15.9 0.6 %collective-permute-start.8 = (f32[1,64,256]{2,1,0:T(8,128)S(1)}, f32[1,64,256]{2,1,0:T(8,128)S(1)}, u32[]{:S(2)}, u32[]{:S(2)}) collective-permute-start(f32[1,64,256]{2,1,0:T(8,128)S(1)} %volumes.3), channel_id=1, source_target_pairs={{0,4},{4,0},{8,12},{12,8},{1,5},{5,1},{9,13},{13,9},{2,6},{6,2},{1... | collective-permute-start | bytes 196616 | tf_op jit(solution)/shard_map/ppermute | solution.py:518
  16.5 0.5 %far_col.1 = (f32[5,64,256]{2,1,0:T(8,128)S(1)}, f32[2,5,64,256]{3,2,1,0:T(8,128)S(1)}) custom-call(f32[56,256]{1,0:T(8,128)S(1)} %get-tuple-element.27.coefs, f32[1,5,64,256]{3,2,1,0:T(8,128)S(1)} %collective-permute-done.3.states.refs_0_.refs_1_, f32[3,64,256]{2,1,0:T(8,128)S(1)} %collective-permute-done.4.cells.cell.refs_1_.refs_0_.refs_2_), custom_call_target="tpu_custom_call" | custom-call | tf_op jit(solution)/shard_map/far_col/pallas_call | solution.py:507
  17.0 0.1 collective-permute-done.7.refs_4_
  17.2 0.2 %collective-permute-done.8.refs_5_.refs_1_ = f32[1,64,256]{2,1,0:T(8,128)S(1)} collective-permute-done((f32[1,64,256]{2,1,0:T(8,128)S(1)}, f32[1,64,256]{2,1,0:T(8,128)S(1)}, u32[]{:S(2)}, u32[]{:S(2)}) %collective-permute-start.8) | collective-permute-done | bytes 65568 | tf_op jit(solution)/shard_map/ppermute | solution.py:518
  17.4 0.0 collective-permute-done.5.refs_2_
  17.4 0.2 %time.1 = (f32[5,64,256]{2,1,0:T(8,128)S(1)}, f32[5,64,256]{2,1,0:T(8,128)S(1)}) custom-call(f32[6,64,256]{2,1,0:T(8,128)S(1)} %get-tuple-element.24.near, f32[6,64,256]{2,1,0:T(8,128)S(1)} %collective-permute-done.2.beyond, f32[152,256]{1,0:T(8,128)S(1)} %get-tuple-element.32.before.edge, ...), custom_call_target="tpu_custom_call" | custom-call | tf_op jit(solution)/shard_map/time/pallas_call | solution.py:507
  17.6 0.8 %collective-permute-done.9.refs_0_ = f32[152,256]{1,0:T(8,128)S(1)} collective-permute-done((f32[152,256]{1,0:T(8,128)S(1)}, f32[152,256]{1,0:T(8,128)S(1)}, u32[]{:S(2)}, u32[]{:S(2)}) %collective-permute-start.9) | collective-permute-done | bytes 155680 | tf_op jit(solution)/shard_map/ppermute | solution.py:518
  18.4 0.3 %far_step.1 = (f32[336,256]{1,0:T(8,128)S(1)}, f32[5,64,256]{2,1,0:T(8,128)S(1)}) custom-call(f32[5,64,256]{2,1,0:T(8,128)S(1)} %get-tuple-element.38.stepped, f32[152,256]{1,0:T(8,128)S(1)} %get-tuple-element.32.before.edge, f32[152,256]{1,0:T(8,128)S(1)} %collective-permute-done.9.refs_0_, ...), custom_call_target="tpu_custom_call" | custom-call | tf_op jit(solution)/shard_map/far_step/pallas_call | solution.py:507
  18.7 0.1 collective-permute-start.10
  18.8 0.8 %base.1 = f32[5,64,256]{2,1,0:T(8,128)S(1)} custom-call(f32[56,256]{1,0:T(8,128)S(1)} %get-tuple-element.27.coefs, f32[5,64,256]{2,1,0:T(8,128)S(1)} %get-tuple-element.38.stepped, f32[6,64,256]{2,1,0:T(8,128)S(1)} %get-tuple-element.24.near, f32[6,64,256]{2,1,0:T(8,128)S(1)} %collective-permute-done.2.beyond, f32[3,64,256]{2,1,0:T(8,128)S(1)} %get-tuple-element.25.cell, ...), custom_call_target="tpu_custom_call" | custom-call | tf_op jit(solution)/shard_map/base/pallas_call | solution.py:507
  19.6 0.1 rims.1
  19.7 0.8 %collective-permute-done.10.shared = f32[336,256]{1,0:T(8,128)S(1)} collective-permute-done((f32[336,256]{1,0:T(8,128)S(1)}, f32[336,256]{1,0:T(8,128)S(1)}, u32[]{:S(2)}, u32[]{:S(2)}) %collective-permute-start.10) | collective-permute-done | bytes 344096 | tf_op jit(solution)/shard_map/ppermute | solution.py:518
  20.5 0.8 %final.1 = f32[1,5,64,256]{3,2,1,0:T(8,128)} custom-call(f32[56,256]{1,0:T(8,128)S(1)} %get-tuple-element.27.coefs, f32[16,2,256]{2,1,0:T(2,128)S(1)} %rims.1, f32[13,2,256]{2,1,0:T(2,128)S(1)} %get-tuple-element.33.kept, f32[5,64,256]{2,1,0:T(8,128)S(1)} %base.1, f32[5,64,256]{2,1,0:T(8,128)S(1)} %get-tuple-element.41.taken, ...), custom_call_target="tpu_custom_call" | custom-call | tf_op jit(solution)/shard_map/final/pallas_call | solution.py:507
  (5 shorter events, 0.0 us)
Async XLA Ops:
  0.0 12.4 %collective-permute-start.3 = (f32[1,5,64,256]{3,2,1,0:T(8,128)}, f32[1,5,64,256]{3,2,1,0:T(8,128)S(1)}, u32[]{:S(2)}, u32[]{:S(2)}) collective-permute-start(f32[1,5,64,256]{3,2,1,0:T(8,128)} %states.2), channel_id=1, source_target_pairs={{0,8},{4,12},{8,0},{12,4},{1,9},{5,13},{9,1},{13,5},{2,10},{6,14},... | collective-permute-start | bytes 983048 | tf_op jit(solution)/shard_map/ppermute | solution.py:518
  4.1 4.3 %copy-start = (f32[2,5,5]{2,0,1:T(2,128)S(1)}, f32[2,5,5]{2,0,1:T(2,128)}, u32[]{:S(2)}) copy-start(f32[2,5,5]{2,0,1:T(2,128)} %param.11) | copy-start | bytes 604
  4.2 11.8 %collective-permute-start.2 = (f32[6,64,256]{2,1,0:T(8,128)S(1)}, f32[6,64,256]{2,1,0:T(8,128)S(1)}, u32[]{:S(2)}, u32[]{:S(2)}) collective-permute-start(f32[6,64,256]{2,1,0:T(8,128)S(1)} %get-tuple-element.24.near), channel_id=1, source_target_pairs={{0,4},{4,0},{8,12},{12,8},{1,5},{5,1},{9,13},{13,9},{2,6},{6,2},{1... | collective-permute-start | bytes 1179656 | tf_op jit(solution)/shard_map/ppermute | solution.py:518
  4.2 11.7 %collective-permute-start.4 = (f32[3,64,256]{2,1,0:T(8,128)S(1)}, f32[3,64,256]{2,1,0:T(8,128)S(1)}, u32[]{:S(2)}, u32[]{:S(2)}) collective-permute-start(f32[3,64,256]{2,1,0:T(8,128)S(1)} %get-tuple-element.25.cell), channel_id=1, source_target_pairs={{0,8},{4,12},{8,0},{12,4},{1,9},{5,13},{9,1},{13,5},{2,10},{6,14},... | collective-permute-start | bytes 589832 | tf_op jit(solution)/shard_map/ppermute | solution.py:518
  4.3 6.3 %collective-permute-start = (f32[32,256]{1,0:T(8,128)S(1)}, f32[32,256]{1,0:T(8,128)S(1)}, u32[]{:S(2)}, u32[]{:S(2)}) collective-permute-start(f32[32,256]{1,0:T(8,128)S(1)} %get-tuple-element.28), channel_id=1, source_target_pairs={{0,1},{1,2},{2,3},{3,0},{4,5},{5,6},{6,7},{7,4},{8,9},{9,10},{10,1... | collective-permute-start | bytes 98312 | tf_op jit(solution)/shard_map/ppermute | solution.py:542
  6.4 4.2 %collective-permute-start.1 = (f32[24,256]{1,0:T(8,128)S(1)}, f32[24,256]{1,0:T(8,128)S(1)}, u32[]{:S(2)}, u32[]{:S(2)}) collective-permute-start(f32[24,256]{1,0:T(8,128)S(1)} %get-tuple-element.29), channel_id=1, source_target_pairs={{0,3},{1,0},{2,1},{3,2},{4,7},{5,4},{6,5},{7,6},{8,11},{9,8},{10,9... | collective-permute-start | bytes 73736 | tf_op jit(solution)/shard_map/ppermute | solution.py:543
  10.9 7.5 %collective-permute-start.9 = (f32[152,256]{1,0:T(8,128)S(1)}, f32[152,256]{1,0:T(8,128)S(1)}, u32[]{:S(2)}, u32[]{:S(2)}) collective-permute-start(f32[152,256]{1,0:T(8,128)S(1)} %get-tuple-element.32.before.edge), channel_id=1, source_target_pairs={{0,8},{4,12},{8,0},{12,4},{1,9},{5,13},{9,1},{13,5},{2,10},{6,14},... | collective-permute-start | bytes 466952 | tf_op jit(solution)/shard_map/ppermute | solution.py:518
  12.5 4.9 %collective-permute-start.5 = (f32[2,64,256]{2,1,0:T(8,128)S(1)}, f32[2,64,256]{2,1,0:T(8,128)S(1)}, u32[]{:S(2)}, u32[]{:S(2)}) collective-permute-start(f32[2,64,256]{2,1,0:T(8,128)S(1)} %get-tuple-element.34), channel_id=1, source_target_pairs={{0,4},{4,0},{8,12},{12,8},{1,5},{5,1},{9,13},{13,9},{2,6},{6,2},{1... | collective-permute-start | bytes 393224 | tf_op jit(solution)/shard_map/ppermute | solution.py:518
  12.5 4.9 %collective-permute-start.6 = (f32[2,64,256]{2,1,0:T(8,128)S(1)}, f32[2,64,256]{2,1,0:T(8,128)S(1)}, u32[]{:S(2)}, u32[]{:S(2)}) collective-permute-start(f32[2,64,256]{2,1,0:T(8,128)S(1)} %get-tuple-element.35), channel_id=1, source_target_pairs={{0,4},{4,0},{8,12},{12,8},{1,5},{5,1},{9,13},{13,9},{2,6},{6,2},{1... | collective-permute-start | bytes 393224 | tf_op jit(solution)/shard_map/ppermute | solution.py:518
  15.9 1.3 %collective-permute-start.7 = (f32[1,64,256]{2,1,0:T(8,128)S(1)}, f32[1,64,256]{2,1,0:T(8,128)S(1)}, u32[]{:S(2)}, u32[]{:S(2)}) collective-permute-start(f32[1,64,256]{2,1,0:T(8,128)S(1)} %get-tuple-element.36.also), channel_id=1, source_target_pairs={{0,4},{4,0},{8,12},{12,8},{1,5},{5,1},{9,13},{13,9},{2,6},{6,2},{1... | collective-permute-start | bytes 196616 | tf_op jit(solution)/shard_map/ppermute | solution.py:518
  15.9 1.5 %collective-permute-start.8 = (f32[1,64,256]{2,1,0:T(8,128)S(1)}, f32[1,64,256]{2,1,0:T(8,128)S(1)}, u32[]{:S(2)}, u32[]{:S(2)}) collective-permute-start(f32[1,64,256]{2,1,0:T(8,128)S(1)} %volumes.3), channel_id=1, source_target_pairs={{0,4},{4,0},{8,12},{12,8},{1,5},{5,1},{9,13},{13,9},{2,6},{6,2},{1... | collective-permute-start | bytes 196616 | tf_op jit(solution)/shard_map/ppermute | solution.py:518
  18.7 1.7 %collective-permute-start.10 = (f32[336,256]{1,0:T(8,128)S(1)}, f32[336,256]{1,0:T(8,128)S(1)}, u32[]{:S(2)}, u32[]{:S(2)}) collective-permute-start(f32[336,256]{1,0:T(8,128)S(1)} %get-tuple-element.42), channel_id=1, source_target_pairs={{0,4},{4,0},{8,12},{12,8},{1,5},{5,1},{9,13},{13,9},{2,6},{6,2},{1... | collective-permute-start | bytes 1032200 | tf_op jit(solution)/shard_map/ppermute | solution.py:518

commit v5 on v4

--- a/solution.py
+++ b/solution.py
@@ -13,6 +13,7 @@
 nyquist_damping = 0.25
 
 STRIP = 8
+PIECES = (2, 2, 1)
 
 
 def spectral_table(instances):
@@ -28,8 +29,7 @@
 def pack_kernel(states, volumes, row_normals, col_normals, links, near, cell, rows, own_links, upward, downward, sems):
     nvar, depth = states.shape[1], states.shape[2]
     pairs = [
-        (states.at[0], near.at[pl.ds(0, nvar)]),
-        (volumes, near.at[pl.ds(nvar, 1)]),
+        (states.at[0], near),
         (volumes, cell.at[pl.ds(0, 1)]),
         (col_normals.at[0], cell.at[pl.ds(1, 2)]),
         (row_normals.at[0], rows),
@@ -45,7 +45,7 @@
         for v in range(nvar):
             ref[pl.ds(v, 1), :] = near[v, pl.ds(second, 1), :]
             ref[pl.ds(nvar + v, 1), :] = near[v, pl.ds(edge, 1), :]
-        ref[pl.ds(2 * nvar, 1), :] = near[nvar, pl.ds(edge, 1), :]
+        ref[pl.ds(2 * nvar, 1), :] = cell[0, pl.ds(edge, 1), :]
         for d in range(2):
             ref[pl.ds(2 * nvar + 1 + d, 1), :] = rows[d, pl.ds(face, 1), :]
             ref[pl.ds(2 * nvar + 3 + d, 1), :] = cell[1 + d, pl.ds(edge, 1), :]
@@ -264,14 +264,11 @@
         out[v] = x
 
 
-def state_kernel(states, before, *outs):
-    at = 0
-    for out in outs:
-        out[...] = states[0, pl.ds(at, out.shape[0])]
-        at += out.shape[0]
-
-
-def volume_kernel(cells, before, also, out):
+def state_kernel(at, states, before, out):
+    out[...] = states[0, pl.ds(at, out.shape[0])]
+
+
+def volume_kernel(cells, before, out):
     out[...] = cells[pl.ds(0, 1)]
 
 
@@ -296,11 +293,20 @@
             out[v, strip(s), :] = cells[v] - factor * (along[v] + beside[v])
 
 
-def far_col_kernel(nvar, coefs, states, cell, out, out_j):
+def planes(pieces):
+    return [x.at[v] for x in pieces for v in range(x.shape[0])]
+
+
+def families(n):
+    return [0] + list(range(3, n, 2)), [1] + list(range(2, n, 2))
+
+
+def far_col_kernel(nvar, coefs, cell, *refs):
+    states, (out, out_j) = planes(refs[:-2]), refs[-2:]
     strips = out.shape[1] // STRIP
     half = half_jacobians(coefs, nvar)
     for s in range(strips):
-        cells = [states[0, v, strip(s), :] for v in range(nvar)]
+        cells = [states[v][strip(s), :] for v in range(nvar)]
         cells_j = transformed(half, cells)
         beside = col_change([cell[1 + d, strip(s), :] for d in range(2)], cells, cells_j)
         factor = pseudo_step / cell[0, strip(s), :]
@@ -310,46 +316,57 @@
                 out_j[d, v, strip(s), :] = cells_j[d][v]
 
 
-def time_kernel(n, nvar, near, beyond, edge, *refs):
+def near_kernel(n, nvar, near, beyond, cell, volumes, part, sizes, *outs):
+    here, _ = families(n)
+    weights = [[step_weight(n, a, b) for b in (0, 1)] for a in here]
+    for s in range(part.shape[1] // STRIP):
+        for a in range(len(here)):
+            sizes[a, strip(s), :] = weighted(weights[a], [cell[0, strip(s), :], volumes[0, strip(s), :]])
+        for v in range(nvar):
+            values = [near[v, strip(s), :], beyond[v, strip(s), :]]
+            outs[0][v, strip(s), :] = part[v, strip(s), :] - weighted(weights[0], values)
+            for a in range(1, len(here)):
+                outs[a][v, strip(s), :] = -weighted(weights[a], values)
+
+
+def time_kernel(n, nvar, near, own, sums, edge, *refs):
     far = n // 2 - 1
-    states, cells, *pieces, beyond_volumes = [refs[far * t : far * (t + 1)] for t in range(6)]
-    parts, outs = refs[6 * far : 7 * far + 1], refs[7 * far + 1 :]
-    beyond_states = [[x.at[v] for x in piece for v in range(x.shape[0])] for piece in zip(*pieces)]
-    count = far + 1
-    weights = [
-        [step_weight(n, 2 * a, 2 * b) for b in range(count)]
-        + [step_weight(n, 2 * a, 2 * b + 1) for b in range(count)]
-        for a in range(count)
-    ]
+    beyond_states, cells, beyond_volumes, *pieces = [refs[far * t : far * (t + 1)] for t in range(3 + len(PIECES))]
+    refs = refs[far * (3 + len(PIECES)) :]
+    begun, parts = refs[: far + 1], refs[far + 1 : 2 * far + 1]
+    rate, outs = refs[2 * far + 1], refs[2 * far + 2 :]
+    states = [planes(x) for x in zip(*pieces)]
+    here, there = families(n)
+    rest = [[step_weight(n, a, b) for b in here[1:] + there[1:]] for a in here]
     strips = outs[0].shape[1] // STRIP
     row = lax.broadcasted_iota(jnp.int32, (STRIP, near.shape[2]), 0)
     for s in range(strips):
-        here = [near[nvar, strip(s), :]] + [x[0, strip(s), :] for x in cells]
-        sizes = here + [beyond[nvar, strip(s), :]] + [x[0, strip(s), :] for x in beyond_volumes]
-        factors = [weighted(weights[a], sizes) / here[a] for a in range(count)]
-        for v in range(nvar):
-            values = [near[v, strip(s), :]] + [x[0, v, strip(s), :] for x in states]
-            values = values + [beyond[v, strip(s), :]] + [x[v][strip(s), :] for x in beyond_states]
+        sizes = [x[0, strip(s), :] for x in (own, *cells)]
+        far_sizes = sizes[1:] + [x[0, strip(s), :] for x in beyond_volumes]
+        rates = [sums[a, strip(s), :] + weighted(rest[a], far_sizes) for a in range(far + 1)]
+        factors = [rates[a] / sizes[a] for a in range(far + 1)]
+        rate[strip(s), :] = factors[0]
+        for v in range(nvar):
+            values = [near[v, strip(s), :]] + [x[v][strip(s), :] for x in states]
+            others = values[1:] + [x[0, v, strip(s), :] for x in beyond_states]
             moved = [
-                parts[a][v, strip(s), :] - weighted(weights[a], values) - factors[a] * values[a]
-                for a in range(count)
+                begun[a][v, strip(s), :] - weighted(rest[a], others) - factors[a] * values[a]
+                for a in range(far + 1)
             ]
+            moved = moved[:1] + [moved[a] + parts[a - 1][v, strip(s), :] for a in range(1, far + 1)]
             if s == 0:
-                moved[0] = moved[0] + jnp.where(row == 0, pseudo_step * edge[pl.ds(v, 1), :], 0.0) / here[0]
+                moved[0] = moved[0] + jnp.where(row == 0, pseudo_step * edge[pl.ds(v, 1), :], 0.0) / sizes[0]
             if s == strips - 1:
                 lacking = jnp.where(row == STRIP - 1, pseudo_step * edge[pl.ds(nvar + v, 1), :], 0.0)
-                moved[0] = moved[0] - lacking / here[0]
-            for a in range(count):
+                moved[0] = moved[0] - lacking / sizes[0]
+            for a in range(far + 1):
                 outs[a][v, strip(s), :] = moved[a]
 
 
-def base_kernel(n, nvar, coefs, stepped, near, beyond, cell, row_normals, *refs):
-    far = n // 2 - 1
-    cells_of, beyond_volumes, out = refs[:far], refs[far : 2 * far], refs[2 * far]
+def base_kernel(n, nvar, coefs, stepped, cell, row_normals, rate, out):
     strips = out.shape[1] // STRIP
     half = half_jacobians(coefs, nvar)
-    weights = [step_weight(n, 0, 2 * b) for b in range(far + 1)]
-    weights = weights + [step_weight(n, 0, 2 * b + 1) for b in range(far + 1)]
+    weight = step_weight(n, 0, 0)
 
     def at(s):
         cells = [stepped[v, strip(s), :] for v in range(nvar)]
@@ -357,28 +374,27 @@
 
     for s, cells, cells_j, along in row_changes(strips, at, lambda v: 0.0, lambda v: 0.0):
         beside = col_change([cell[1 + d, strip(s), :] for d in range(2)], cells, cells_j)
-        sizes = [near[nvar, strip(s), :]] + [x[0, strip(s), :] for x in cells_of]
-        sizes = sizes + [beyond[nvar, strip(s), :]] + [x[0, strip(s), :] for x in beyond_volumes]
-        inverse = 1.0 / sizes[0]
-        kept = (1.0 - weights[0]) - inverse * weighted(weights, sizes)
+        inverse = 1.0 / cell[0, strip(s), :]
+        kept = (1.0 - weight) - rate[strip(s), :]
         for v in range(nvar):
             out[v, strip(s), :] = kept * cells[v] - (pseudo_step * inverse) * (along[v] + beside[v])
 
 
 def far_step_kernel(n, nvar, stepped, edge, *refs):
     far = n // 2 - 1
-    edges, states, cells_of, parts, transforms = [refs[far * t : far * (t + 1)] for t in range(5)]
-    shared, out = refs[5 * far :]
+    edges, cells_of, parts, transforms, *pieces = [refs[far * t : far * (t + 1)] for t in range(4 + len(PIECES))]
+    states = [planes(x) for x in zip(*pieces)]
+    shared, out = refs[(4 + len(PIECES)) * far :]
     depth = stepped.shape[1]
     strips = depth // STRIP
-    mine = [step_weight(n, 0, 2 * b) for b in range(far + 1)]
-    other = [step_weight(n, 1, 2 * b) for b in range(far + 1)]
+    mine = [step_weight(n, 0, b) for b in families(n)[0]]
+    other = [step_weight(n, 1, b) for b in families(n)[0]]
     head = edge.shape[0] - 2 * depth
 
     def changes(a):
         def at(s):
             faces = [edges[a][pl.ds(head + d * depth + s * STRIP, STRIP), :] for d in range(2)]
-            cells = [states[a][0, v, strip(s), :] for v in range(nvar)]
+            cells = [states[a][v][strip(s), :] for v in range(nvar)]
             return faces, cells, [[transforms[a][d, v, strip(s), :] for v in range(nvar)] for d in range(2)]
 
         return row_changes(
@@ -403,12 +419,12 @@
     )
 
 
-def rim_kernel(n, nvar, coefs, edge, kept, others, near, stepped, *refs):
+def rim_kernel(n, nvar, coefs, edge, kept, others, cell, stepped, *refs):
     far = n // 2 - 1
     edges, out = refs[:far], refs[far]
     depth, columns = stepped.shape[1], stepped.shape[2]
     half = half_jacobians(coefs, nvar)
-    weights = [step_weight(n, 0, 2 * b) for b in range(far + 1)]
+    weights = [step_weight(n, 0, b) for b in families(n)[0]]
     is_below = lax.broadcasted_iota(jnp.int32, (2, columns), 0) == 0
     at = 2 * nvar
 
@@ -436,7 +452,7 @@
             + face[1] * inside_j[1][v]
             + jnp.where(is_below, -spread, spread) * inside[v]
         )
-    volume = pair(near[nvar, pl.ds(0, 1), :], near[nvar, pl.ds(depth - 1, 1), :])
+    volume = pair(cell[0, pl.ds(0, 1), :], cell[0, pl.ds(depth - 1, 1), :])
     factor = pseudo_step / volume
     out[3 * nvar] = jnp.where(is_below, factor, -factor)
 
@@ -525,7 +541,7 @@
     near, own_cell, own_rows, own_links, upward, downward = pl.pallas_call(
         pack_kernel,
         out_shape=[
-            f32(nvar + 1, depth, columns),
+            f32(nvar, depth, columns),
             f32(3, depth, columns),
             f32(2, depth, columns),
             jax.ShapeDtypeStruct(face_links.shape, face_links.dtype),
@@ -534,11 +550,11 @@
         ],
         in_specs=[hbm] * 5,
         out_specs=[vmem] * 6,
-        scratch_shapes=[pltpu.SemaphoreType.DMA((6,))],
+        scratch_shapes=[pltpu.SemaphoreType.DMA((5,))],
         compiler_params=params,
         name="pack",
     )(*inputs)
-    cell_of = {k: swapped(own_cell, k) for k in far}
+    cell_of = {k: swapped(own_cell, k + 1) for k in far}
     below = lax.ppermute(upward, "slab", [(i, (i + 1) % slabs) for i in range(slabs)])
     above = lax.ppermute(downward, "slab", [(i, (i - 1) % slabs) for i in range(slabs)])
     field = f32(nvar, depth, columns)
@@ -551,7 +567,7 @@
         own_cell,
         own_rows,
     )
-    parts = [own_part]
+    parts = []
     edge, kept = call(
         functools.partial(edge_kernel, nvar),
         "edges",
@@ -575,14 +591,30 @@
         own_links,
         scratch=[pltpu.VMEM((-(-2 * nvar // 8) * 8, columns), jnp.float32)],
     )
-    edge_of = {k: swapped(edge, k) for k in far}
+    edge_of = {k: swapped(edge, k + 1) for k in far}
     beyond = swapped(near, 1)
-    pieces = [f32(count, depth, columns) for count in (2, 2, nvar - 4)]
-    beyond_states, beyond_volumes = [], dict()
+    sums, *begun = call(
+        functools.partial(near_kernel, n, nvar),
+        "near",
+        [f32(len(far) + 1, depth, columns)] + [field] * (len(far) + 1),
+        near,
+        beyond,
+        own_cell,
+        swapped(call(volume_kernel, "volumes", f32(1, depth, columns), own_cell, edge), 1),
+        own_part,
+    )
+    pieces_of, beyond_volumes = dict(), dict()
     for k in far:
-        copies = call(state_kernel, "states", pieces, state_of[k], edge)
-        beyond_states.append([swapped(x, 1) for x in copies])
-        held = call(volume_kernel, "volumes", f32(1, depth, columns), cell_of[k], others, copies[-1])
+        pieces, at = [], 0
+        for t, count in enumerate(PIECES):
+            before = begun[0] if t + 1 == len(PIECES) else edge
+            shape = f32(count, depth, columns)
+            kernel = functools.partial(state_kernel, at)
+            held = call(kernel, "states", shape, state_of[k], before)
+            pieces.append(swapped(held, 1))
+            at += count
+        pieces_of[k] = pieces
+        held = call(volume_kernel, "volumes", f32(1, depth, columns), cell_of[k], begun[0])
         beyond_volumes[k] = swapped(held, 1)
 
     transforms = {}
@@ -592,23 +624,23 @@
             "far_col",
             [field, f32(2, nvar, depth, columns)],
             coefs,
-            state_of[k],
             cell_of[k],
+            *pieces_of[k],
         )
         parts.append(part)
-    stepped, *parts = call(
+    rate, stepped, *parts = call(
         functools.partial(time_kernel, n, nvar),
         "time",
-        [field] * (len(far) + 1),
+        [f32(depth, columns)] + [field] * (len(far) + 1),
         near,
-        beyond,
+        own_cell,
+        sums,
         edge,
         *[state_of[k] for k in far],
         *[cell_of[k] for k in far],
-        *[x[0] for x in beyond_states],
-        *[x[1] for x in beyond_states],
-        *[x[2] for x in beyond_states],
         *[beyond_volumes[k] for k in far],
+        *[pieces_of[k][t] for t in range(len(PIECES)) for k in far],
+        *begun,
         *parts,
     )
     base = call(
@@ -617,12 +649,9 @@
         field,
         coefs,
         stepped,
-        near,
-        beyond,
         own_cell,
         own_rows,
-        *[cell_of[k] for k in far],
-        *[beyond_volumes[k] for k in far],
+        rate,
     )
     shared, taken = call(
         functools.partial(far_step_kernel, n, nvar),
@@ -631,10 +660,10 @@
         stepped,
         edge,
         *[edge_of[k] for k in far],
-        *[state_of[k] for k in far],
         *[cell_of[k] for k in far],
         *parts,
         *[transforms[k] for k in far],
+        *[pieces_of[k][t] for t in range(len(PIECES)) for k in far],
     )
     rims = call(
         functools.partial(rim_kernel, n, nvar),
@@ -644,7 +673,7 @@
         edge,
         kept,
         others,
-        near,
+        own_cell,
         stepped,
         *[edge_of[k] for k in far],
     )

time: 21.4 us -> 20.8 us (0.972)
  waiting for transfers between devices: 5.2 us -> 3.73 us
  starting transfers between devices: 9.96 us -> 10.9 us
    ppermute x9 -> x10, waiting for transfers between devices: 4.47 us -> 2.98 us  [swapped(): return lax.ppermute(x, 'inst', [(i, i ^ k) for i in range(n)])]
    ppermute x9 -> x10, starting transfers between devices: 5.84 us -> 6.73 us  [swapped(): return lax.ppermute(x, 'inst', [(i, i ^ k) for i in range(n)])]
    pallas_call x11 -> x15, Pallas kernels: 4.76 us -> 4.8 us  [call(): pl.pallas_call(kernel, out_shape=shapes, in_specs=[smem if x is jacobians...]
  transfers between devices with their start and end apart: 11 -> 12, of which waited for: 6 -> 5; matrix products, arithmetic and copies ran while one was open for 0% -> 0% of each run, Pallas kernels for 23% -> 23%
where the time goes in v5:
time: 20.8 us; the launch traced here: 20.7 us
  starting transfers between devices  10.9 us (52%)
  Pallas kernels  5.96 us (29%)
  waiting for transfers between devices  3.73 us (18%)
    ppermute x10, starting transfers between devices, swapped(): return lax.ppermute(x, 'inst', [(i, i ^ k) for i in range(n)])  6.73 us
    pallas_call x15, Pallas kernels, call(): pl.pallas_call(kernel, out_shape=shapes, in_specs=[smem if x is jacobians...  4.8 us
    ppermute x10, waiting for transfers between devices, swapped(): return lax.ppermute(x, 'inst', [(i, i ^ k) for i in range(n)])  2.98 us
    ppermute x1, starting transfers between devices, body(): lax.ppermute(upward, 'slab', [(i, (i + 1) % slabs) for i in range(slabs)])  2.11 us
    ppermute x1, starting transfers between devices, body(): lax.ppermute(downward, 'slab', [(i, (i - 1) % slabs) for i in range(slabs)])  2.03 us
    pallas_call x1, Pallas kernels, body(): pl.pallas_call(pack_kernel, out_shape=[f32(nvar, depth, columns), f32(3,...  1.16 us
    ppermute x1, waiting for transfers between devices, body(): lax.ppermute(downward, 'slab', [(i, (i - 1) % slabs) for i in range(slabs)])  0.74 us
  transfers between devices with their start and end apart: 12, of which 5 were waited for; matrix products, arithmetic and copies ran while one was open for 0% of the time, Pallas kernels for 23%

profile of v5, /device:TPU:0, one launch (start us, length us, event | category | flops | bytes accessed | tf_op | source)
XLA Modules:
  0.0 20.7 jit_solution(6675688224725752669)
XLA Ops:
  0.0 2.9 %collective-permute-start.4 = (f32[1,5,64,256]{3,2,1,0:T(8,128)}, f32[1,5,64,256]{3,2,1,0:T(8,128)S(1)}, u32[]{:S(2)}, u32[]{:S(2)}) collective-permute-start(f32[1,5,64,256]{3,2,1,0:T(8,128)} %states.4), channel_id=1, source_target_pairs={{0,8},{4,12},{8,0},{12,4},{1,9},{5,13},{9,1},{13,5},{2,10},{6,14},... | collective-permute-start | bytes 983048 | tf_op jit(solution)/shard_map/ppermute | solution.py:534
  2.9 1.2 %pack.1 = (f32[5,64,256]{2,1,0:T(8,128)S(1)}, f32[3,64,256]{2,1,0:T(8,128)S(1)}, f32[2,64,256]{2,1,0:T(8,128)S(1)}, s32[1,256]{1,0:T(1,128)S(1)}, f32[32,256]{1,0:T(8,128)S(1)}, /*index=5*/f32[24,256]{1,0:T(8,128)S(1)}) custom-call(f32[1,5,64,256]{3,2,1,0:T(8,128)} %states.4, f32[1,64,256]{2,1,0:T(8,128)} %volumes.3, f32[1,2,64,256]{3,2,1,0:T(8,128)} %row_normals.1, ...), custom_call_target="tpu_custom_call" | custom-call | tf_op jit(solution)/shard_map/pack/pallas_call | solution.py:541
  4.1 0.0 copy-start
  4.1 0.1 collective-permute-start.2
  4.2 0.1 collective-permute-start.5
  4.3 2.1 %collective-permute-start = (f32[32,256]{1,0:T(8,128)S(1)}, f32[32,256]{1,0:T(8,128)S(1)}, u32[]{:S(2)}, u32[]{:S(2)}) collective-permute-start(f32[32,256]{1,0:T(8,128)S(1)} %get-tuple-element.29), channel_id=1, source_target_pairs={{0,1},{1,2},{2,3},{3,0},{4,5},{5,6},{6,7},{7,4},{8,9},{9,10},{10,1... | collective-permute-start | bytes 98312 | tf_op jit(solution)/shard_map/ppermute | solution.py:558
  6.4 2.0 %collective-permute-start.1 = (f32[24,256]{1,0:T(8,128)S(1)}, f32[24,256]{1,0:T(8,128)S(1)}, u32[]{:S(2)}, u32[]{:S(2)}) collective-permute-start(f32[24,256]{1,0:T(8,128)S(1)} %get-tuple-element.30), channel_id=1, source_target_pairs={{0,3},{1,0},{2,1},{3,2},{4,7},{5,4},{6,5},{7,6},{8,11},{9,8},{10,9... | collective-permute-start | bytes 73736 | tf_op jit(solution)/shard_map/ppermute | solution.py:559
  8.5 1.4 %own_flux.1 = (f32[5,64,256]{2,1,0:T(8,128)S(1)}, f32[56,256]{1,0:T(8,128)S(1)}) custom-call(f32[2,5,5]{2,1,0:T(8,128)S(1)} %copy.7.jacobians, f32[5,64,256]{2,1,0:T(8,128)S(1)} %get-tuple-element.25.near, f32[3,64,256]{2,1,0:T(8,128)S(1)} %get-tuple-element.26.cell.cells.own, f32[2,64,256]{2,1,0:T(8,128)S(1)} %get-tuple-element.27.row_normals), custom_call_target="tpu_custom_call" | custom-call | tf_op jit(solution)/shard_map/own_flux/pallas_call | solution.py:523
  9.9 0.7 %collective-permute-done.1.above = f32[24,256]{1,0:T(8,128)S(1)} collective-permute-done((f32[24,256]{1,0:T(8,128)S(1)}, f32[24,256]{1,0:T(8,128)S(1)}, u32[]{:S(2)}, u32[]{:S(2)}) %collective-permute-start.1) | collective-permute-done | bytes 24608 | tf_op jit(solution)/shard_map/ppermute | solution.py:559
  10.6 0.0 collective-permute-done.below
  10.6 0.3 %edges.1 = (f32[152,256]{1,0:T(8,128)S(1)}, f32[13,2,256]{2,1,0:T(2,128)S(1)}) custom-call(f32[56,256]{1,0:T(8,128)S(1)} %get-tuple-element.28.coefs, f32[32,256]{1,0:T(8,128)S(1)} %collective-permute-done.below, f32[24,256]{1,0:T(8,128)S(1)} %collective-permute-done.1.above, f32[5,64,256]{2,1,0:T(8,128)S(1)} %get-tuple-element.25.near, ...), custom_call_target="tpu_custom_call" | custom-call | tf_op jit(solution)/shard_map/edges/pallas_call | solution.py:523
  10.9 0.1 collective-permute-start.3
  11.0 1.6 %collective-permute-start.10 = (f32[152,256]{1,0:T(8,128)S(1)}, f32[152,256]{1,0:T(8,128)S(1)}, u32[]{:S(2)}, u32[]{:S(2)}) collective-permute-start(f32[152,256]{1,0:T(8,128)S(1)} %get-tuple-element.33.before.edge), channel_id=1, source_target_pairs={{0,12},{4,8},{8,4},{12,0},{1,13},{5,9},{9,5},{13,1},{2,14},{6,10},... | collective-permute-start | bytes 466952 | tf_op jit(solution)/shard_map/ppermute | solution.py:534
  12.6 0.1 collective-permute-start.7
  12.7 0.5 %collective-permute-start.8 = (f32[2,64,256]{2,1,0:T(8,128)S(1)}, f32[2,64,256]{2,1,0:T(8,128)S(1)}, u32[]{:S(2)}, u32[]{:S(2)}) collective-permute-start(f32[2,64,256]{2,1,0:T(8,128)S(1)} %states.6), channel_id=1, source_target_pairs={{0,4},{4,0},{8,12},{12,8},{1,5},{5,1},{9,13},{13,9},{2,6},{6,2},{1... | collective-permute-start | bytes 393224 | tf_op jit(solution)/shard_map/ppermute | solution.py:534
  13.3 0.0 collective-permute-done.2.beyond
  13.3 0.1 near.1
  13.4 0.1 collective-permute-start.9
  13.5 2.0 %collective-permute-done.5.cells.cell.refs_1_ = f32[3,64,256]{2,1,0:T(8,128)S(1)} collective-permute-done((f32[3,64,256]{2,1,0:T(8,128)S(1)}, f32[3,64,256]{2,1,0:T(8,128)S(1)}, u32[]{:S(2)}, u32[]{:S(2)}) %collective-permute-start.5) | collective-permute-done | bytes 196640 | tf_op jit(solution)/shard_map/ppermute | solution.py:534
  15.5 0.5 %collective-permute-start.6 = (f32[1,64,256]{2,1,0:T(8,128)S(1)}, f32[1,64,256]{2,1,0:T(8,128)S(1)}, u32[]{:S(2)}, u32[]{:S(2)}) collective-permute-start(f32[1,64,256]{2,1,0:T(8,128)S(1)} %volumes.5), channel_id=1, source_target_pairs={{0,4},{4,0},{8,12},{12,8},{1,5},{5,1},{9,13},{13,9},{2,6},{6,2},{1... | collective-permute-start | bytes 196616 | tf_op jit(solution)/shard_map/ppermute | solution.py:534
  16.0 0.0 collective-permute-done.8.refs_1_.refs_4_.refs_5_
  16.0 0.5 %far_col.1 = (f32[5,64,256]{2,1,0:T(8,128)S(1)}, f32[2,5,64,256]{3,2,1,0:T(8,128)S(1)}) custom-call(f32[56,256]{1,0:T(8,128)S(1)} %get-tuple-element.28.coefs, f32[3,64,256]{2,1,0:T(8,128)S(1)} %collective-permute-done.5.cells.cell.refs_1_, f32[2,64,256]{2,1,0:T(8,128)S(1)} %collective-permute-done.7.refs_0_.refs_3_.refs_4_, ...), custom_call_target="tpu_custom_call" | custom-call | tf_op jit(solution)/shard_map/far_col/pallas_call | solution.py:523
  16.6 0.4 %collective-permute-done.6.refs_2_ = f32[1,64,256]{2,1,0:T(8,128)S(1)} collective-permute-done((f32[1,64,256]{2,1,0:T(8,128)S(1)}, f32[1,64,256]{2,1,0:T(8,128)S(1)}, u32[]{:S(2)}, u32[]{:S(2)}) %collective-permute-start.6) | collective-permute-done | bytes 65568 | tf_op jit(solution)/shard_map/ppermute | solution.py:534
  16.9 0.2 time.1
  17.1 0.5 %collective-permute-done.10.refs_0_ = f32[152,256]{1,0:T(8,128)S(1)} collective-permute-done((f32[152,256]{1,0:T(8,128)S(1)}, f32[152,256]{1,0:T(8,128)S(1)}, u32[]{:S(2)}, u32[]{:S(2)}) %collective-permute-start.10) | collective-permute-done | bytes 155680 | tf_op jit(solution)/shard_map/ppermute | solution.py:534
  17.7 0.3 %far_step.1 = (f32[336,256]{1,0:T(8,128)S(1)}, f32[5,64,256]{2,1,0:T(8,128)S(1)}) custom-call(f32[5,64,256]{2,1,0:T(8,128)S(1)} %get-tuple-element.39.stepped, f32[152,256]{1,0:T(8,128)S(1)} %get-tuple-element.33.before.edge, f32[152,256]{1,0:T(8,128)S(1)} %collective-permute-done.10.refs_0_, f32[3,64,256]{2,1,0:T(8,128)S(1)} %collective-permute-done.5.cells.cell.refs_1_, ...), custom_call_target="tpu_custom_call" | custom-call | tf_op jit(solution)/shard_map/far_step/pallas_call | solution.py:523
  18.0 0.6 %collective-permute-start.11 = (f32[336,256]{1,0:T(8,128)S(1)}, f32[336,256]{1,0:T(8,128)S(1)}, u32[]{:S(2)}, u32[]{:S(2)}) collective-permute-start(f32[336,256]{1,0:T(8,128)S(1)} %get-tuple-element.44), channel_id=1, source_target_pairs={{0,4},{4,0},{8,12},{12,8},{1,5},{5,1},{9,13},{13,9},{2,6},{6,2},{1... | collective-permute-start | bytes 1032200 | tf_op jit(solution)/shard_map/ppermute | solution.py:534
  18.6 0.4 %behind.1.others = f32[5,2,256]{2,1,0:T(2,128)S(1)} custom-call(f32[56,256]{1,0:T(8,128)S(1)} %get-tuple-element.28.coefs, f32[32,256]{1,0:T(8,128)S(1)} %collective-permute-done.below, f32[24,256]{1,0:T(8,128)S(1)} %collective-permute-done.1.above, s32[1,256]{1,0:T(1,128)S(1)} %get-tuple-element.31.links), custom_call_target="tpu_custom_call" | custom-call | tf_op jit(solution)/shard_map/behind/pallas_call | solution.py:523
  19.0 0.7 %base.1 = f32[5,64,256]{2,1,0:T(8,128)S(1)} custom-call(f32[56,256]{1,0:T(8,128)S(1)} %get-tuple-element.28.coefs, f32[5,64,256]{2,1,0:T(8,128)S(1)} %get-tuple-element.39.stepped, f32[3,64,256]{2,1,0:T(8,128)S(1)} %get-tuple-element.26.cell.cells.own, f32[2,64,256]{2,1,0:T(8,128)S(1)} %get-tuple-element.27.row_normals, f32[64,256]{1,0:T(8,128)S(1)} %get-tuple-element.40.rate), custom_call_target="tpu_custom_call" | custom-call | tf_op jit(solution)/shard_map/base/pallas_call | solution.py:523
  19.7 0.1 rims.1
  19.8 0.1 collective-permute-done.11.shared
  19.9 0.8 %final.1 = f32[1,5,64,256]{3,2,1,0:T(8,128)} custom-call(f32[56,256]{1,0:T(8,128)S(1)} %get-tuple-element.28.coefs, f32[16,2,256]{2,1,0:T(2,128)S(1)} %rims.1, f32[13,2,256]{2,1,0:T(2,128)S(1)} %get-tuple-element.34.kept, f32[5,64,256]{2,1,0:T(8,128)S(1)} %base.1, f32[5,64,256]{2,1,0:T(8,128)S(1)} %get-tuple-element.43.taken, ...), custom_call_target="tpu_custom_call" | custom-call | tf_op jit(solution)/shard_map/final/pallas_call | solution.py:523
  (11 shorter events, 0.1 us)
Async XLA Ops:
  0.0 12.6 %collective-permute-start.4 = (f32[1,5,64,256]{3,2,1,0:T(8,128)}, f32[1,5,64,256]{3,2,1,0:T(8,128)S(1)}, u32[]{:S(2)}, u32[]{:S(2)}) collective-permute-start(f32[1,5,64,256]{3,2,1,0:T(8,128)} %states.4), channel_id=1, source_target_pairs={{0,8},{4,12},{8,0},{12,4},{1,9},{5,13},{9,1},{13,5},{2,10},{6,14},... | collective-permute-start | bytes 983048 | tf_op jit(solution)/shard_map/ppermute | solution.py:534
  4.1 4.3 %copy-start = (f32[2,5,5]{2,0,1:T(2,128)S(1)}, f32[2,5,5]{2,0,1:T(2,128)}, u32[]{:S(2)}) copy-start(f32[2,5,5]{2,0,1:T(2,128)} %param.11) | copy-start | bytes 604
  4.1 9.1 %collective-permute-start.2 = (f32[5,64,256]{2,1,0:T(8,128)S(1)}, f32[5,64,256]{2,1,0:T(8,128)S(1)}, u32[]{:S(2)}, u32[]{:S(2)}) collective-permute-start(f32[5,64,256]{2,1,0:T(8,128)S(1)} %get-tuple-element.25.near), channel_id=1, source_target_pairs={{0,4},{4,0},{8,12},{12,8},{1,5},{5,1},{9,13},{13,9},{2,6},{6,2},{1... | collective-permute-start | bytes 983048 | tf_op jit(solution)/shard_map/ppermute | solution.py:534
  4.2 11.3 %collective-permute-start.5 = (f32[3,64,256]{2,1,0:T(8,128)S(1)}, f32[3,64,256]{2,1,0:T(8,128)S(1)}, u32[]{:S(2)}, u32[]{:S(2)}) collective-permute-start(f32[3,64,256]{2,1,0:T(8,128)S(1)} %get-tuple-element.26.cell.cells.own), channel_id=1, source_target_pairs={{0,12},{4,8},{8,4},{12,0},{1,13},{5,9},{9,5},{13,1},{2,14},{6,10},... | collective-permute-start | bytes 589832 | tf_op jit(solution)/shard_map/ppermute | solution.py:534
  4.3 6.3 %collective-permute-start = (f32[32,256]{1,0:T(8,128)S(1)}, f32[32,256]{1,0:T(8,128)S(1)}, u32[]{:S(2)}, u32[]{:S(2)}) collective-permute-start(f32[32,256]{1,0:T(8,128)S(1)} %get-tuple-element.29), channel_id=1, source_target_pairs={{0,1},{1,2},{2,3},{3,0},{4,5},{5,6},{6,7},{7,4},{8,9},{9,10},{10,1... | collective-permute-start | bytes 98312 | tf_op jit(solution)/shard_map/ppermute | solution.py:558
  6.4 4.2 %collective-permute-start.1 = (f32[24,256]{1,0:T(8,128)S(1)}, f32[24,256]{1,0:T(8,128)S(1)}, u32[]{:S(2)}, u32[]{:S(2)}) collective-permute-start(f32[24,256]{1,0:T(8,128)S(1)} %get-tuple-element.30), channel_id=1, source_target_pairs={{0,3},{1,0},{2,1},{3,2},{4,7},{5,4},{6,5},{7,6},{8,11},{9,8},{10,9... | collective-permute-start | bytes 73736 | tf_op jit(solution)/shard_map/ppermute | solution.py:559
  10.9 1.8 %collective-permute-start.3 = (f32[1,64,256]{2,1,0:T(8,128)S(1)}, f32[1,64,256]{2,1,0:T(8,128)S(1)}, u32[]{:S(2)}, u32[]{:S(2)}) collective-permute-start(f32[1,64,256]{2,1,0:T(8,128)S(1)} %volumes.4), channel_id=1, source_target_pairs={{0,4},{4,0},{8,12},{12,8},{1,5},{5,1},{9,13},{13,9},{2,6},{6,2},{1... | collective-permute-start | bytes 196616 | tf_op jit(solution)/shard_map/ppermute | solution.py:534
  11.0 6.7 %collective-permute-start.10 = (f32[152,256]{1,0:T(8,128)S(1)}, f32[152,256]{1,0:T(8,128)S(1)}, u32[]{:S(2)}, u32[]{:S(2)}) collective-permute-start(f32[152,256]{1,0:T(8,128)S(1)} %get-tuple-element.33.before.edge), channel_id=1, source_target_pairs={{0,12},{4,8},{8,4},{12,0},{1,13},{5,9},{9,5},{13,1},{2,14},{6,10},... | collective-permute-start | bytes 466952 | tf_op jit(solution)/shard_map/ppermute | solution.py:534
  12.6 3.4 %collective-permute-start.7 = (f32[2,64,256]{2,1,0:T(8,128)S(1)}, f32[2,64,256]{2,1,0:T(8,128)S(1)}, u32[]{:S(2)}, u32[]{:S(2)}) collective-permute-start(f32[2,64,256]{2,1,0:T(8,128)S(1)} %states.5), channel_id=1, source_target_pairs={{0,4},{4,0},{8,12},{12,8},{1,5},{5,1},{9,13},{13,9},{2,6},{6,2},{1... | collective-permute-start | bytes 393224 | tf_op jit(solution)/shard_map/ppermute | solution.py:534
  12.7 3.3 %collective-permute-start.8 = (f32[2,64,256]{2,1,0:T(8,128)S(1)}, f32[2,64,256]{2,1,0:T(8,128)S(1)}, u32[]{:S(2)}, u32[]{:S(2)}) collective-permute-start(f32[2,64,256]{2,1,0:T(8,128)S(1)} %states.6), channel_id=1, source_target_pairs={{0,4},{4,0},{8,12},{12,8},{1,5},{5,1},{9,13},{13,9},{2,6},{6,2},{1... | collective-permute-start | bytes 393224 | tf_op jit(solution)/shard_map/ppermute | solution.py:534
  13.4 2.6 %collective-permute-start.9 = (f32[1,64,256]{2,1,0:T(8,128)S(1)}, f32[1,64,256]{2,1,0:T(8,128)S(1)}, u32[]{:S(2)}, u32[]{:S(2)}) collective-permute-start(f32[1,64,256]{2,1,0:T(8,128)S(1)} %states.7), channel_id=1, source_target_pairs={{0,4},{4,0},{8,12},{12,8},{1,5},{5,1},{9,13},{13,9},{2,6},{6,2},{1... | collective-permute-start | bytes 196616 | tf_op jit(solution)/shard_map/ppermute | solution.py:534
  15.5 1.4 %collective-permute-start.6 = (f32[1,64,256]{2,1,0:T(8,128)S(1)}, f32[1,64,256]{2,1,0:T(8,128)S(1)}, u32[]{:S(2)}, u32[]{:S(2)}) collective-permute-start(f32[1,64,256]{2,1,0:T(8,128)S(1)} %volumes.5), channel_id=1, source_target_pairs={{0,4},{4,0},{8,12},{12,8},{1,5},{5,1},{9,13},{13,9},{2,6},{6,2},{1... | collective-permute-start | bytes 196616 | tf_op jit(solution)/shard_map/ppermute | solution.py:534
  18.0 1.9 %collective-permute-start.11 = (f32[336,256]{1,0:T(8,128)S(1)}, f32[336,256]{1,0:T(8,128)S(1)}, u32[]{:S(2)}, u32[]{:S(2)}) collective-permute-start(f32[336,256]{1,0:T(8,128)S(1)} %get-tuple-element.44), channel_id=1, source_target_pairs={{0,4},{4,0},{8,12},{12,8},{1,5},{5,1},{9,13},{13,9},{2,6},{6,2},{1... | collective-permute-start | bytes 1032200 | tf_op jit(solution)/shard_map/ppermute | solution.py:534

commit v6 on v5

--- a/solution.py
+++ b/solution.py
@@ -229,17 +229,15 @@
     across = [
         face[0] * summed[0][v] + face[1] * summed[1][v] - spread * (high[v] - low[v]) for v in range(nvar)
     ]
-    at = 2 * nvar
     for v in range(nvar):
-        out[pl.ds(v, 1), :] = across[v][0:1]
-        out[pl.ds(nvar + v, 1), :] = across[v][1:2]
         kept[v] = rim[v]
         kept[nvar + v] = jnp.where(is_below, across[v], -across[v])
     for v, x in enumerate(rim + [volume]):
-        out[pl.ds(at + v, 1), :] = x[0:1]
-        out[pl.ds(at + nvar + 1 + v, 1), :] = x[1:2]
+        out[pl.ds(v, 1), :] = x[0:1]
+        out[pl.ds(nvar + 1 + v, 1), :] = x[1:2]
     kept[2 * nvar] = volume
     for d in range(2):
+        out[pl.ds(2 * nvar + 2 + d, 1), :] = face[d][1:2]
         kept[2 * nvar + 1 + d] = face[d]
     head = out.shape[0] - 2 * depth
     for d in range(2):
@@ -302,18 +300,31 @@
 
 
 def far_col_kernel(nvar, coefs, cell, *refs):
-    states, (out, out_j) = planes(refs[:-2]), refs[-2:]
-    strips = out.shape[1] // STRIP
-    half = half_jacobians(coefs, nvar)
-    for s in range(strips):
+    states, out = planes(refs[:-1]), refs[-1]
+    half = half_jacobians(coefs, nvar)
+    for s in range(out.shape[1] // STRIP):
         cells = [states[v][strip(s), :] for v in range(nvar)]
-        cells_j = transformed(half, cells)
-        beside = col_change([cell[1 + d, strip(s), :] for d in range(2)], cells, cells_j)
+        beside = col_change([cell[1 + d, strip(s), :] for d in range(2)], cells, transformed(half, cells))
         factor = pseudo_step / cell[0, strip(s), :]
         for v in range(nvar):
             out[v, strip(s), :] = cells[v] - factor * beside[v]
-            for d in range(2):
-                out_j[d, v, strip(s), :] = cells_j[d][v]
+
+
+def far_face_kernel(nvar, coefs, *refs):
+    states, out = planes(refs[:-1]), refs[-1]
+    half = half_jacobians(coefs, nvar)
+    row = lax.broadcasted_iota(jnp.int32, (STRIP, out.shape[3]), 0)
+    before = None
+    for s in range(out.shape[2] // STRIP):
+        cells = [states[v][strip(s), :] for v in range(nvar)]
+        rolled = [pltpu.roll(x, 1, 0) for x in cells]
+        lower = rolled if s == 0 else [jnp.where(row == 0, x, y) for x, y in zip(before, rolled)]
+        summed = transformed(half, [x + y for x, y in zip(lower, cells)])
+        for v in range(nvar):
+            out[0, v, strip(s), :] = summed[0][v]
+            out[1, v, strip(s), :] = summed[1][v]
+            out[2, v, strip(s), :] = cells[v] - lower[v]
+        before = rolled
 
 
 def near_kernel(n, nvar, near, beyond, cell, volumes, part, sizes, *outs):
@@ -329,7 +340,7 @@
                 outs[a][v, strip(s), :] = -weighted(weights[a], values)
 
 
-def time_kernel(n, nvar, near, own, sums, edge, *refs):
+def time_kernel(n, nvar, near, own, sums, kept, *refs):
     far = n // 2 - 1
     beyond_states, cells, beyond_volumes, *pieces = [refs[far * t : far * (t + 1)] for t in range(3 + len(PIECES))]
     refs = refs[far * (3 + len(PIECES)) :]
@@ -355,10 +366,10 @@
             ]
             moved = moved[:1] + [moved[a] + parts[a - 1][v, strip(s), :] for a in range(1, far + 1)]
             if s == 0:
-                moved[0] = moved[0] + jnp.where(row == 0, pseudo_step * edge[pl.ds(v, 1), :], 0.0) / sizes[0]
+                moved[0] = moved[0] + jnp.where(row == 0, pseudo_step * kept[nvar + v][0:1], 0.0) / sizes[0]
             if s == strips - 1:
-                lacking = jnp.where(row == STRIP - 1, pseudo_step * edge[pl.ds(nvar + v, 1), :], 0.0)
-                moved[0] = moved[0] - lacking / sizes[0]
+                lacking = jnp.where(row == STRIP - 1, pseudo_step * kept[nvar + v][1:2], 0.0)
+                moved[0] = moved[0] + lacking / sizes[0]
             for a in range(far + 1):
                 outs[a][v, strip(s), :] = moved[a]
 
@@ -380,9 +391,9 @@
             out[v, strip(s), :] = kept * cells[v] - (pseudo_step * inverse) * (along[v] + beside[v])
 
 
-def far_step_kernel(n, nvar, stepped, edge, *refs):
+def far_step_kernel(n, nvar, coefs, stepped, edge, *refs):
     far = n // 2 - 1
-    edges, cells_of, parts, transforms, *pieces = [refs[far * t : far * (t + 1)] for t in range(4 + len(PIECES))]
+    edges, cells_of, parts, beside, *pieces = [refs[far * t : far * (t + 1)] for t in range(4 + len(PIECES))]
     states = [planes(x) for x in zip(*pieces)]
     shared, out = refs[(4 + len(PIECES)) * far :]
     depth = stepped.shape[1]
@@ -390,16 +401,46 @@
     mine = [step_weight(n, 0, b) for b in families(n)[0]]
     other = [step_weight(n, 1, b) for b in families(n)[0]]
     head = edge.shape[0] - 2 * depth
+    half = half_jacobians(coefs, nvar)
+    is_below = lax.broadcasted_iota(jnp.int32, (2, stepped.shape[2]), 0) == 0
+    row = lax.broadcasted_iota(jnp.int32, (STRIP, stepped.shape[2]), 0)
 
     def changes(a):
-        def at(s):
-            faces = [edges[a][pl.ds(head + d * depth + s * STRIP, STRIP), :] for d in range(2)]
-            cells = [states[a][v][strip(s), :] for v in range(nvar)]
-            return faces, cells, [[transforms[a][d, v, strip(s), :] for v in range(nvar)] for d in range(2)]
-
-        return row_changes(
-            strips, at, lambda v: edges[a][pl.ds(v, 1), :], lambda v: edges[a][pl.ds(nvar + v, 1), :]
-        )
+        def behind_rows(v):
+            return pair(edges[a][pl.ds(v, 1), :], edges[a][pl.ds(nvar + 1 + v, 1), :])
+
+        ends = [pair(states[a][v][pl.ds(0, 1), :], states[a][v][pl.ds(depth - 1, 1), :]) for v in range(nvar)]
+        rims = [behind_rows(v) for v in range(nvar)]
+        face = [
+            pair(edges[a][pl.ds(head + d * depth, 1), :], edges[a][pl.ds(2 * nvar + 2 + d, 1), :])
+            for d in range(2)
+        ]
+        ends_j = transformed(half, [x + y for x, y in zip(ends, rims)])
+        spread = jnp.where(is_below, spread_of(face), -spread_of(face))
+        across = [
+            face[0] * ends_j[0][v] + face[1] * ends_j[1][v] - spread * (ends[v] - rims[v])
+            for v in range(nvar)
+        ]
+        last = None
+        for s in range(strips + 1):
+            if s < strips:
+                normal = [edges[a][pl.ds(head + d * depth + s * STRIP, STRIP), :] for d in range(2)]
+                spread = spread_of(normal)
+                flux = []
+                for v in range(nvar):
+                    sums, difference = [beside[a][d, v, strip(s), :] for d in range(2)], beside[a][2, v, strip(s), :]
+                    flux.append(normal[0] * sums[0] + normal[1] * sums[1] - spread * difference)
+                if s == 0:
+                    flux = [jnp.where(row == 0, across[v][0:1], flux[v]) for v in range(nvar)]
+                lifted = [pltpu.roll(x, STRIP - 1, 0) for x in flux]
+            else:
+                lifted = [across[v][1:2] for v in range(nvar)]
+            if s > 0:
+                yield (
+                    s - 1,
+                    [jnp.where(row == STRIP - 1, lifted[v], last[1][v]) - last[0][v] for v in range(nvar)],
+                )
+            last = (flux, lifted)
 
     for moves in zip(*[changes(a) for a in range(far)]):
         s = moves[0][0]
@@ -408,12 +449,12 @@
             given = other[0] * stepped[v, strip(s), :]
             taken = None
             for a in range(far):
-                value = parts[a][v, strip(s), :] - factors[a] * moves[a][3][v]
+                value = parts[a][v, strip(s), :] - factors[a] * moves[a][1][v]
                 given = given + other[1 + a] * value
                 taken = mine[1 + a] * value if taken is None else taken + mine[1 + a] * value
             shared[pl.ds(v * depth + s * STRIP, STRIP), :] = given
             out[v, strip(s), :] = taken
-    rims = pl.ds(2 * nvar, 2 * nvar + 2)
+    rims = pl.ds(0, 2 * nvar + 2)
     shared[pl.ds(nvar * depth, 2 * nvar + 2), :] = weighted(
         other, [edge[rims, :]] + [edges[a][rims, :] for a in range(far)]
     )
@@ -426,13 +467,12 @@
     half = half_jacobians(coefs, nvar)
     weights = [step_weight(n, 0, b) for b in families(n)[0]]
     is_below = lax.broadcasted_iota(jnp.int32, (2, columns), 0) == 0
-    at = 2 * nvar
 
     def rim(v):
         return weighted(
             weights,
             [
-                pair(ref[pl.ds(at + v, 1), :], ref[pl.ds(at + nvar + 1 + v, 1), :])
+                pair(ref[pl.ds(v, 1), :], ref[pl.ds(nvar + 1 + v, 1), :])
                 for ref in [edge] + list(edges)
             ],
         )
@@ -508,7 +548,7 @@
     far = list(range(2, n, 2))
     down_rows = -(-(2 * nvar + 8) // 8) * 8
     up_rows = down_rows + 8
-    head = -(-(4 * nvar + 2) // 8) * 8
+    head = -(-(2 * nvar + 4) // 8) * 8
 
     def f32(*shape):
         return jax.ShapeDtypeStruct(shape, jnp.float32)
@@ -617,17 +657,13 @@
         held = call(volume_kernel, "volumes", f32(1, depth, columns), cell_of[k], begun[0])
         beyond_volumes[k] = swapped(held, 1)
 
-    transforms = {}
+    faces = {}
     for k in far:
-        part, transforms[k] = call(
-            functools.partial(far_col_kernel, nvar),
-            "far_col",
-            [field, f32(2, nvar, depth, columns)],
-            coefs,
-            cell_of[k],
-            *pieces_of[k],
+        shape = f32(3, nvar, depth, columns)
+        faces[k] = call(functools.partial(far_face_kernel, nvar), "far_faces", shape, coefs, *pieces_of[k])
+        parts.append(
+            call(functools.partial(far_col_kernel, nvar), "far_col", field, coefs, cell_of[k], *pieces_of[k])
         )
-        parts.append(part)
     rate, stepped, *parts = call(
         functools.partial(time_kernel, n, nvar),
         "time",
@@ -635,7 +671,7 @@
         near,
         own_cell,
         sums,
-        edge,
+        kept,
         *[state_of[k] for k in far],
         *[cell_of[k] for k in far],
         *[beyond_volumes[k] for k in far],
@@ -657,12 +693,13 @@
         functools.partial(far_step_kernel, n, nvar),
         "far_step",
         [f32(nvar * depth + 16, columns), field],
+        coefs,
         stepped,
         edge,
         *[edge_of[k] for k in far],
         *[cell_of[k] for k in far],
         *parts,
-        *[transforms[k] for k in far],
+        *[faces[k] for k in far],
         *[pieces_of[k][t] for t in range(len(PIECES)) for k in far],
     )
     rims = call(

time: 20.8 us -> 20.6 us (level)
  waiting for transfers between devices: 3.73 us -> 3.22 us
  Pallas kernels: 5.96 us -> 6.24 us
    ppermute x10, waiting for transfers between devices: 2.98 us -> 2.49 us  [swapped(): return lax.ppermute(x, 'inst', [(i, i ^ k) for i in range(n)])]
    pallas_call x15 -> x16, Pallas kernels: 4.8 us -> 5.08 us  [call(): pl.pallas_call(kernel, out_shape=shapes, in_specs=[smem if x is jacobians...]
  transfers between devices with their start and end apart: 12 -> 12, of which waited for: 5 -> 5; matrix products, arithmetic and copies ran while one was open for 0% -> 0% of each run, Pallas kernels for 23% -> 25%
where the time goes in v6:
time: 20.6 us; the launch traced here: 20.5 us
  starting transfers between devices  10.9 us (53%)
  Pallas kernels  6.24 us (30%)
  waiting for transfers between devices  3.22 us (16%)
    ppermute x10, starting transfers between devices, swapped(): return lax.ppermute(x, 'inst', [(i, i ^ k) for i in range(n)])  6.73 us
    pallas_call x16, Pallas kernels, call(): pl.pallas_call(kernel, out_shape=shapes, in_specs=[smem if x is jacobians...  5.08 us
    ppermute x10, waiting for transfers between devices, swapped(): return lax.ppermute(x, 'inst', [(i, i ^ k) for i in range(n)])  2.49 us
    ppermute x1, starting transfers between devices, body(): lax.ppermute(upward, 'slab', [(i, (i + 1) % slabs) for i in range(slabs)])  2.11 us
    ppermute x1, starting transfers between devices, body(): lax.ppermute(downward, 'slab', [(i, (i - 1) % slabs) for i in range(slabs)])  2.03 us
    pallas_call x1, Pallas kernels, body(): pl.pallas_call(pack_kernel, out_shape=[f32(nvar, depth, columns), f32(3,...  1.16 us
    ppermute x1, waiting for transfers between devices, body(): lax.ppermute(downward, 'slab', [(i, (i - 1) % slabs) for i in range(slabs)])  0.73 us
  transfers between devices with their start and end apart: 12, of which 5 were waited for; matrix products, arithmetic and copies ran while one was open for 0% of the time, Pallas kernels for 25%

profile of v6, /device:TPU:0, one launch (start us, length us, event | category | flops | bytes accessed | tf_op | source)
XLA Modules:
  0.0 20.5 jit_solution(2505321429674045022)
XLA Ops:
  0.0 2.9 %collective-permute-start.4 = (f32[1,5,64,256]{3,2,1,0:T(8,128)}, f32[1,5,64,256]{3,2,1,0:T(8,128)S(1)}, u32[]{:S(2)}, u32[]{:S(2)}) collective-permute-start(f32[1,5,64,256]{3,2,1,0:T(8,128)} %states.4), channel_id=1, source_target_pairs={{0,8},{4,12},{8,0},{12,4},{1,9},{5,13},{9,1},{13,5},{2,10},{6,14},... | collective-permute-start | bytes 983048 | tf_op jit(solution)/shard_map/ppermute | solution.py:574
  2.9 1.2 %pack.1 = (f32[5,64,256]{2,1,0:T(8,128)S(1)}, f32[3,64,256]{2,1,0:T(8,128)S(1)}, f32[2,64,256]{2,1,0:T(8,128)S(1)}, s32[1,256]{1,0:T(1,128)S(1)}, f32[32,256]{1,0:T(8,128)S(1)}, /*index=5*/f32[24,256]{1,0:T(8,128)S(1)}) custom-call(f32[1,5,64,256]{3,2,1,0:T(8,128)} %states.4, f32[1,64,256]{2,1,0:T(8,128)} %volumes.3, f32[1,2,64,256]{3,2,1,0:T(8,128)} %row_normals.1, ...), custom_call_target="tpu_custom_call" | custom-call | tf_op jit(solution)/shard_map/pack/pallas_call | solution.py:581
  4.1 0.0 copy-start
  4.1 0.1 collective-permute-start.2
  4.2 0.1 collective-permute-start.5
  4.3 2.1 %collective-permute-start = (f32[32,256]{1,0:T(8,128)S(1)}, f32[32,256]{1,0:T(8,128)S(1)}, u32[]{:S(2)}, u32[]{:S(2)}) collective-permute-start(f32[32,256]{1,0:T(8,128)S(1)} %get-tuple-element.27), channel_id=1, source_target_pairs={{0,1},{1,2},{2,3},{3,0},{4,5},{5,6},{6,7},{7,4},{8,9},{9,10},{10,1... | collective-permute-start | bytes 98312 | tf_op jit(solution)/shard_map/ppermute | solution.py:598
  6.4 2.0 %collective-permute-start.1 = (f32[24,256]{1,0:T(8,128)S(1)}, f32[24,256]{1,0:T(8,128)S(1)}, u32[]{:S(2)}, u32[]{:S(2)}) collective-permute-start(f32[24,256]{1,0:T(8,128)S(1)} %get-tuple-element.28), channel_id=1, source_target_pairs={{0,3},{1,0},{2,1},{3,2},{4,7},{5,4},{6,5},{7,6},{8,11},{9,8},{10,9... | collective-permute-start | bytes 73736 | tf_op jit(solution)/shard_map/ppermute | solution.py:599
  8.5 1.4 %own_flux.1 = (f32[5,64,256]{2,1,0:T(8,128)S(1)}, f32[56,256]{1,0:T(8,128)S(1)}) custom-call(f32[2,5,5]{2,1,0:T(8,128)S(1)} %copy.7.jacobians, f32[5,64,256]{2,1,0:T(8,128)S(1)} %get-tuple-element.23.near, f32[3,64,256]{2,1,0:T(8,128)S(1)} %get-tuple-element.24.cell.cells.own, f32[2,64,256]{2,1,0:T(8,128)S(1)} %get-tuple-element.25.row_normals), custom_call_target="tpu_custom_call" | custom-call | tf_op jit(solution)/shard_map/own_flux/pallas_call | solution.py:563
  9.9 0.7 %collective-permute-done.1.above = f32[24,256]{1,0:T(8,128)S(1)} collective-permute-done((f32[24,256]{1,0:T(8,128)S(1)}, f32[24,256]{1,0:T(8,128)S(1)}, u32[]{:S(2)}, u32[]{:S(2)}) %collective-permute-start.1) | collective-permute-done | bytes 24608 | tf_op jit(solution)/shard_map/ppermute | solution.py:599
  10.6 0.0 collective-permute-done.below
  10.6 0.3 %edges.1 = (f32[144,256]{1,0:T(8,128)S(1)}, f32[13,2,256]{2,1,0:T(2,128)S(1)}) custom-call(f32[56,256]{1,0:T(8,128)S(1)} %get-tuple-element.26.coefs, f32[32,256]{1,0:T(8,128)S(1)} %collective-permute-done.below, f32[24,256]{1,0:T(8,128)S(1)} %collective-permute-done.1.above, f32[5,64,256]{2,1,0:T(8,128)S(1)} %get-tuple-element.23.near, ...), custom_call_target="tpu_custom_call" | custom-call | tf_op jit(solution)/shard_map/edges/pallas_call | solution.py:563
  10.9 0.1 collective-permute-start.3
  11.0 1.6 %collective-permute-start.10 = (f32[144,256]{1,0:T(8,128)S(1)}, f32[144,256]{1,0:T(8,128)S(1)}, u32[]{:S(2)}, u32[]{:S(2)}) collective-permute-start(f32[144,256]{1,0:T(8,128)S(1)} %get-tuple-element.31.before.edge), channel_id=1, source_target_pairs={{0,12},{4,8},{8,4},{12,0},{1,13},{5,9},{9,5},{13,1},{2,14},{6,10},... | collective-permute-start | bytes 442376 | tf_op jit(solution)/shard_map/ppermute | solution.py:574
  12.6 0.1 collective-permute-start.7
  12.7 0.5 %collective-permute-start.8 = (f32[2,64,256]{2,1,0:T(8,128)S(1)}, f32[2,64,256]{2,1,0:T(8,128)S(1)}, u32[]{:S(2)}, u32[]{:S(2)}) collective-permute-start(f32[2,64,256]{2,1,0:T(8,128)S(1)} %states.6), channel_id=1, source_target_pairs={{0,4},{4,0},{8,12},{12,8},{1,5},{5,1},{9,13},{13,9},{2,6},{6,2},{1... | collective-permute-start | bytes 393224 | tf_op jit(solution)/shard_map/ppermute | solution.py:574
  13.3 0.1 near.1
  13.4 0.1 collective-permute-start.9
  13.5 2.0 %collective-permute-done.5.cells.cell.refs_1_ = f32[3,64,256]{2,1,0:T(8,128)S(1)} collective-permute-done((f32[3,64,256]{2,1,0:T(8,128)S(1)}, f32[3,64,256]{2,1,0:T(8,128)S(1)}, u32[]{:S(2)}, u32[]{:S(2)}) %collective-permute-start.5) | collective-permute-done | bytes 196640 | tf_op jit(solution)/shard_map/ppermute | solution.py:574
  15.5 0.5 %collective-permute-start.6 = (f32[1,64,256]{2,1,0:T(8,128)S(1)}, f32[1,64,256]{2,1,0:T(8,128)S(1)}, u32[]{:S(2)}, u32[]{:S(2)}) collective-permute-start(f32[1,64,256]{2,1,0:T(8,128)S(1)} %volumes.5), channel_id=1, source_target_pairs={{0,4},{4,0},{8,12},{12,8},{1,5},{5,1},{9,13},{13,9},{2,6},{6,2},{1... | collective-permute-start | bytes 196616 | tf_op jit(solution)/shard_map/ppermute | solution.py:574
  16.0 0.0 collective-permute-done.8.refs_1_.refs_4_.refs_5_
  16.0 0.5 %far_col.1.refs_8_ = f32[5,64,256]{2,1,0:T(8,128)S(1)} custom-call(f32[56,256]{1,0:T(8,128)S(1)} %get-tuple-element.26.coefs, f32[3,64,256]{2,1,0:T(8,128)S(1)} %collective-permute-done.5.cells.cell.refs_1_, f32[2,64,256]{2,1,0:T(8,128)S(1)} %collective-permute-done.7.refs_0_.refs_3_.refs_4_, ...), custom_call_target="tpu_custom_call" | custom-call | tf_op jit(solution)/shard_map/far_col/pallas_call | solution.py:563
  16.6 0.3 %far_faces.1.refs_3_ = f32[3,5,64,256]{3,2,1,0:T(8,128)S(1)} custom-call(f32[56,256]{1,0:T(8,128)S(1)} %get-tuple-element.26.coefs, f32[2,64,256]{2,1,0:T(8,128)S(1)} %collective-permute-done.7.refs_0_.refs_3_.refs_4_, f32[2,64,256]{2,1,0:T(8,128)S(1)} %collective-permute-done.8.refs_1_.refs_4_.refs_5_, ...), custom_call_target="tpu_custom_call" | custom-call | tf_op jit(solution)/shard_map/far_faces/pallas_call | solution.py:563
  16.8 0.1 collective-permute-done.6.refs_2_
  16.9 0.2 %time.1 = (f32[64,256]{1,0:T(8,128)S(1)}, f32[5,64,256]{2,1,0:T(8,128)S(1)}, f32[5,64,256]{2,1,0:T(8,128)S(1)}) custom-call(f32[5,64,256]{2,1,0:T(8,128)S(1)} %get-tuple-element.23.near, f32[3,64,256]{2,1,0:T(8,128)S(1)} %get-tuple-element.24.cell.cells.own, f32[2,64,256]{2,1,0:T(8,128)S(1)} %get-tuple-element.33.sums, ...), custom_call_target="tpu_custom_call" | custom-call | tf_op jit(solution)/shard_map/time/pallas_call | solution.py:563
  17.1 0.4 %collective-permute-done.10.refs_0_ = f32[144,256]{1,0:T(8,128)S(1)} collective-permute-done((f32[144,256]{1,0:T(8,128)S(1)}, f32[144,256]{1,0:T(8,128)S(1)}, u32[]{:S(2)}, u32[]{:S(2)}) %collective-permute-start.10) | collective-permute-done | bytes 147488 | tf_op jit(solution)/shard_map/ppermute | solution.py:574
  17.5 0.3 %far_step.1 = (f32[336,256]{1,0:T(8,128)S(1)}, f32[5,64,256]{2,1,0:T(8,128)S(1)}) custom-call(f32[56,256]{1,0:T(8,128)S(1)} %get-tuple-element.26.coefs, f32[5,64,256]{2,1,0:T(8,128)S(1)} %get-tuple-element.36.stepped, f32[144,256]{1,0:T(8,128)S(1)} %get-tuple-element.31.before.edge, f32[144,256]{1,0:T(8,128)S(1)} %collective-permute-done.10.refs_0_, ...), custom_call_target="tpu_custom_call" | custom-call | tf_op jit(solution)/shard_map/far_step/pallas_call | solution.py:563
  17.8 0.6 %collective-permute-start.11 = (f32[336,256]{1,0:T(8,128)S(1)}, f32[336,256]{1,0:T(8,128)S(1)}, u32[]{:S(2)}, u32[]{:S(2)}) collective-permute-start(f32[336,256]{1,0:T(8,128)S(1)} %get-tuple-element.40), channel_id=1, source_target_pairs={{0,4},{4,0},{8,12},{12,8},{1,5},{5,1},{9,13},{13,9},{2,6},{6,2},{1... | collective-permute-start | bytes 1032200 | tf_op jit(solution)/shard_map/ppermute | solution.py:574
  18.4 0.4 %behind.1.others = f32[5,2,256]{2,1,0:T(2,128)S(1)} custom-call(f32[56,256]{1,0:T(8,128)S(1)} %get-tuple-element.26.coefs, f32[32,256]{1,0:T(8,128)S(1)} %collective-permute-done.below, f32[24,256]{1,0:T(8,128)S(1)} %collective-permute-done.1.above, s32[1,256]{1,0:T(1,128)S(1)} %get-tuple-element.29.links), custom_call_target="tpu_custom_call" | custom-call | tf_op jit(solution)/shard_map/behind/pallas_call | solution.py:563
  18.7 0.8 %base.1 = f32[5,64,256]{2,1,0:T(8,128)S(1)} custom-call(f32[56,256]{1,0:T(8,128)S(1)} %get-tuple-element.26.coefs, f32[5,64,256]{2,1,0:T(8,128)S(1)} %get-tuple-element.36.stepped, f32[3,64,256]{2,1,0:T(8,128)S(1)} %get-tuple-element.24.cell.cells.own, f32[2,64,256]{2,1,0:T(8,128)S(1)} %get-tuple-element.25.row_normals, f32[64,256]{1,0:T(8,128)S(1)} %get-tuple-element.37.rate), custom_call_target="tpu_custom_call" | custom-call | tf_op jit(solution)/shard_map/base/pallas_call | solution.py:563
  19.5 0.1 rims.1
  19.6 0.1 collective-permute-done.11.shared
  19.7 0.8 %final.1 = f32[1,5,64,256]{3,2,1,0:T(8,128)} custom-call(f32[56,256]{1,0:T(8,128)S(1)} %get-tuple-element.26.coefs, f32[16,2,256]{2,1,0:T(2,128)S(1)} %rims.1, f32[13,2,256]{2,1,0:T(2,128)S(1)} %get-tuple-element.32.kept, f32[5,64,256]{2,1,0:T(8,128)S(1)} %base.1, f32[5,64,256]{2,1,0:T(8,128)S(1)} %get-tuple-element.39.taken, ...), custom_call_target="tpu_custom_call" | custom-call | tf_op jit(solution)/shard_map/final/pallas_call | solution.py:563
  (12 shorter events, 0.1 us)
Async XLA Ops:
  0.0 12.6 %collective-permute-start.4 = (f32[1,5,64,256]{3,2,1,0:T(8,128)}, f32[1,5,64,256]{3,2,1,0:T(8,128)S(1)}, u32[]{:S(2)}, u32[]{:S(2)}) collective-permute-start(f32[1,5,64,256]{3,2,1,0:T(8,128)} %states.4), channel_id=1, source_target_pairs={{0,8},{4,12},{8,0},{12,4},{1,9},{5,13},{9,1},{13,5},{2,10},{6,14},... | collective-permute-start | bytes 983048 | tf_op jit(solution)/shard_map/ppermute | solution.py:574
  4.1 4.3 %copy-start = (f32[2,5,5]{2,0,1:T(2,128)S(1)}, f32[2,5,5]{2,0,1:T(2,128)}, u32[]{:S(2)}) copy-start(f32[2,5,5]{2,0,1:T(2,128)} %param.11) | copy-start | bytes 604
  4.1 9.1 %collective-permute-start.2 = (f32[5,64,256]{2,1,0:T(8,128)S(1)}, f32[5,64,256]{2,1,0:T(8,128)S(1)}, u32[]{:S(2)}, u32[]{:S(2)}) collective-permute-start(f32[5,64,256]{2,1,0:T(8,128)S(1)} %get-tuple-element.23.near), channel_id=1, source_target_pairs={{0,4},{4,0},{8,12},{12,8},{1,5},{5,1},{9,13},{13,9},{2,6},{6,2},{1... | collective-permute-start | bytes 983048 | tf_op jit(solution)/shard_map/ppermute | solution.py:574
  4.2 11.3 %collective-permute-start.5 = (f32[3,64,256]{2,1,0:T(8,128)S(1)}, f32[3,64,256]{2,1,0:T(8,128)S(1)}, u32[]{:S(2)}, u32[]{:S(2)}) collective-permute-start(f32[3,64,256]{2,1,0:T(8,128)S(1)} %get-tuple-element.24.cell.cells.own), channel_id=1, source_target_pairs={{0,12},{4,8},{8,4},{12,0},{1,13},{5,9},{9,5},{13,1},{2,14},{6,10},... | collective-permute-start | bytes 589832 | tf_op jit(solution)/shard_map/ppermute | solution.py:574
  4.3 6.3 %collective-permute-start = (f32[32,256]{1,0:T(8,128)S(1)}, f32[32,256]{1,0:T(8,128)S(1)}, u32[]{:S(2)}, u32[]{:S(2)}) collective-permute-start(f32[32,256]{1,0:T(8,128)S(1)} %get-tuple-element.27), channel_id=1, source_target_pairs={{0,1},{1,2},{2,3},{3,0},{4,5},{5,6},{6,7},{7,4},{8,9},{9,10},{10,1... | collective-permute-start | bytes 98312 | tf_op jit(solution)/shard_map/ppermute | solution.py:598
  6.4 4.2 %collective-permute-start.1 = (f32[24,256]{1,0:T(8,128)S(1)}, f32[24,256]{1,0:T(8,128)S(1)}, u32[]{:S(2)}, u32[]{:S(2)}) collective-permute-start(f32[24,256]{1,0:T(8,128)S(1)} %get-tuple-element.28), channel_id=1, source_target_pairs={{0,3},{1,0},{2,1},{3,2},{4,7},{5,4},{6,5},{7,6},{8,11},{9,8},{10,9... | collective-permute-start | bytes 73736 | tf_op jit(solution)/shard_map/ppermute | solution.py:599
  10.9 1.8 %collective-permute-start.3 = (f32[1,64,256]{2,1,0:T(8,128)S(1)}, f32[1,64,256]{2,1,0:T(8,128)S(1)}, u32[]{:S(2)}, u32[]{:S(2)}) collective-permute-start(f32[1,64,256]{2,1,0:T(8,128)S(1)} %volumes.4), channel_id=1, source_target_pairs={{0,4},{4,0},{8,12},{12,8},{1,5},{5,1},{9,13},{13,9},{2,6},{6,2},{1... | collective-permute-start | bytes 196616 | tf_op jit(solution)/shard_map/ppermute | solution.py:574
  11.0 6.5 %collective-permute-start.10 = (f32[144,256]{1,0:T(8,128)S(1)}, f32[144,256]{1,0:T(8,128)S(1)}, u32[]{:S(2)}, u32[]{:S(2)}) collective-permute-start(f32[144,256]{1,0:T(8,128)S(1)} %get-tuple-element.31.before.edge), channel_id=1, source_target_pairs={{0,12},{4,8},{8,4},{12,0},{1,13},{5,9},{9,5},{13,1},{2,14},{6,10},... | collective-permute-start | bytes 442376 | tf_op jit(solution)/shard_map/ppermute | solution.py:574
  12.6 3.4 %collective-permute-start.7 = (f32[2,64,256]{2,1,0:T(8,128)S(1)}, f32[2,64,256]{2,1,0:T(8,128)S(1)}, u32[]{:S(2)}, u32[]{:S(2)}) collective-permute-start(f32[2,64,256]{2,1,0:T(8,128)S(1)} %states.5), channel_id=1, source_target_pairs={{0,4},{4,0},{8,12},{12,8},{1,5},{5,1},{9,13},{13,9},{2,6},{6,2},{1... | collective-permute-start | bytes 393224 | tf_op jit(solution)/shard_map/ppermute | solution.py:574
  12.7 3.3 %collective-permute-start.8 = (f32[2,64,256]{2,1,0:T(8,128)S(1)}, f32[2,64,256]{2,1,0:T(8,128)S(1)}, u32[]{:S(2)}, u32[]{:S(2)}) collective-permute-start(f32[2,64,256]{2,1,0:T(8,128)S(1)} %states.6), channel_id=1, source_target_pairs={{0,4},{4,0},{8,12},{12,8},{1,5},{5,1},{9,13},{13,9},{2,6},{6,2},{1... | collective-permute-start | bytes 393224 | tf_op jit(solution)/shard_map/ppermute | solution.py:574
  13.4 2.6 %collective-permute-start.9 = (f32[1,64,256]{2,1,0:T(8,128)S(1)}, f32[1,64,256]{2,1,0:T(8,128)S(1)}, u32[]{:S(2)}, u32[]{:S(2)}) collective-permute-start(f32[1,64,256]{2,1,0:T(8,128)S(1)} %states.7), channel_id=1, source_target_pairs={{0,4},{4,0},{8,12},{12,8},{1,5},{5,1},{9,13},{13,9},{2,6},{6,2},{1... | collective-permute-start | bytes 196616 | tf_op jit(solution)/shard_map/ppermute | solution.py:574
  15.5 1.4 %collective-permute-start.6 = (f32[1,64,256]{2,1,0:T(8,128)S(1)}, f32[1,64,256]{2,1,0:T(8,128)S(1)}, u32[]{:S(2)}, u32[]{:S(2)}) collective-permute-start(f32[1,64,256]{2,1,0:T(8,128)S(1)} %volumes.5), channel_id=1, source_target_pairs={{0,4},{4,0},{8,12},{12,8},{1,5},{5,1},{9,13},{13,9},{2,6},{6,2},{1... | collective-permute-start | bytes 196616 | tf_op jit(solution)/shard_map/ppermute | solution.py:574
  17.8 1.9 %collective-permute-start.11 = (f32[336,256]{1,0:T(8,128)S(1)}, f32[336,256]{1,0:T(8,128)S(1)}, u32[]{:S(2)}, u32[]{:S(2)}) collective-permute-start(f32[336,256]{1,0:T(8,128)S(1)} %get-tuple-element.40), channel_id=1, source_target_pairs={{0,4},{4,0},{8,12},{12,8},{1,5},{5,1},{9,13},{13,9},{2,6},{6,2},{1... | collective-permute-start | bytes 1032200 | tf_op jit(solution)/shard_map/ppermute | solution.py:574

commit v7 on v6

--- a/solution.py
+++ b/solution.py
@@ -345,7 +345,8 @@
     beyond_states, cells, beyond_volumes, *pieces = [refs[far * t : far * (t + 1)] for t in range(3 + len(PIECES))]
     refs = refs[far * (3 + len(PIECES)) :]
     begun, parts = refs[: far + 1], refs[far + 1 : 2 * far + 1]
-    rate, outs = refs[2 * far + 1], refs[2 * far + 2 :]
+    rate, early, outs = refs[2 * far + 1], refs[2 * far + 2], refs[2 * far + 3 :]
+    other = [step_weight(n, 1, b) for b in families(n)[0]]
     states = [planes(x) for x in zip(*pieces)]
     here, there = families(n)
     rest = [[step_weight(n, a, b) for b in here[1:] + there[1:]] for a in here]
@@ -372,12 +373,14 @@
                 moved[0] = moved[0] + lacking / sizes[0]
             for a in range(far + 1):
                 outs[a][v, strip(s), :] = moved[a]
-
-
-def base_kernel(n, nvar, coefs, stepped, cell, row_normals, rate, out):
+            early[v, strip(s), :] = weighted(other, moved)
+
+
+def base_kernel(n, nvar, coefs, stepped, cell, row_normals, rate, *refs):
+    parts, out = refs[:-1], refs[-1]
     strips = out.shape[1] // STRIP
     half = half_jacobians(coefs, nvar)
-    weight = step_weight(n, 0, 0)
+    weight, *rest = [step_weight(n, 0, b) for b in families(n)[0]]
 
     def at(s):
         cells = [stepped[v, strip(s), :] for v in range(nvar)]
@@ -388,72 +391,68 @@
         inverse = 1.0 / cell[0, strip(s), :]
         kept = (1.0 - weight) - rate[strip(s), :]
         for v in range(nvar):
-            out[v, strip(s), :] = kept * cells[v] - (pseudo_step * inverse) * (along[v] + beside[v])
-
-
-def far_step_kernel(n, nvar, coefs, stepped, edge, *refs):
+            value = kept * cells[v] - (pseudo_step * inverse) * (along[v] + beside[v])
+            out[v, strip(s), :] = value - weighted(rest, [x[v, strip(s), :] for x in parts])
+
+
+def far_step_kernel(n, nvar, coefs, early, edge, *refs):
     far = n // 2 - 1
-    edges, cells_of, parts, beside, *pieces = [refs[far * t : far * (t + 1)] for t in range(4 + len(PIECES))]
+    edges, cells_of, beside, *pieces = [refs[far * t : far * (t + 1)] for t in range(3 + len(PIECES))]
     states = [planes(x) for x in zip(*pieces)]
-    shared, out = refs[(4 + len(PIECES)) * far :]
-    depth = stepped.shape[1]
+    shared, outs = refs[far * (3 + len(PIECES))], refs[far * (3 + len(PIECES)) + 1 :]
+    depth, columns = early.shape[1], early.shape[2]
     strips = depth // STRIP
-    mine = [step_weight(n, 0, b) for b in families(n)[0]]
     other = [step_weight(n, 1, b) for b in families(n)[0]]
     head = edge.shape[0] - 2 * depth
     half = half_jacobians(coefs, nvar)
-    is_below = lax.broadcasted_iota(jnp.int32, (2, stepped.shape[2]), 0) == 0
-    row = lax.broadcasted_iota(jnp.int32, (STRIP, stepped.shape[2]), 0)
-
-    def changes(a):
-        def behind_rows(v):
-            return pair(edges[a][pl.ds(v, 1), :], edges[a][pl.ds(nvar + 1 + v, 1), :])
-
+    is_below = lax.broadcasted_iota(jnp.int32, (2, columns), 0) == 0
+    row = lax.broadcasted_iota(jnp.int32, (STRIP, columns), 0)
+
+    def interface(a):
         ends = [pair(states[a][v][pl.ds(0, 1), :], states[a][v][pl.ds(depth - 1, 1), :]) for v in range(nvar)]
-        rims = [behind_rows(v) for v in range(nvar)]
+        rims = [pair(edges[a][pl.ds(v, 1), :], edges[a][pl.ds(nvar + 1 + v, 1), :]) for v in range(nvar)]
         face = [
             pair(edges[a][pl.ds(head + d * depth, 1), :], edges[a][pl.ds(2 * nvar + 2 + d, 1), :])
             for d in range(2)
         ]
         ends_j = transformed(half, [x + y for x, y in zip(ends, rims)])
         spread = jnp.where(is_below, spread_of(face), -spread_of(face))
-        across = [
-            face[0] * ends_j[0][v] + face[1] * ends_j[1][v] - spread * (ends[v] - rims[v])
-            for v in range(nvar)
+        return [
+            face[0] * ends_j[0][v] + face[1] * ends_j[1][v] - spread * (ends[v] - rims[v]) for v in range(nvar)
         ]
-        last = None
-        for s in range(strips + 1):
-            if s < strips:
-                normal = [edges[a][pl.ds(head + d * depth + s * STRIP, STRIP), :] for d in range(2)]
-                spread = spread_of(normal)
-                flux = []
-                for v in range(nvar):
-                    sums, difference = [beside[a][d, v, strip(s), :] for d in range(2)], beside[a][2, v, strip(s), :]
-                    flux.append(normal[0] * sums[0] + normal[1] * sums[1] - spread * difference)
-                if s == 0:
-                    flux = [jnp.where(row == 0, across[v][0:1], flux[v]) for v in range(nvar)]
-                lifted = [pltpu.roll(x, STRIP - 1, 0) for x in flux]
+
+    def flux_of(a, s):
+        normal = [edges[a][pl.ds(head + d * depth + s * STRIP, STRIP), :] for d in range(2)]
+        spread = spread_of(normal)
+        flux = []
+        for v in range(nvar):
+            sums, difference = [beside[a][d, v, strip(s), :] for d in range(2)], beside[a][2, v, strip(s), :]
+            flux.append(normal[0] * sums[0] + normal[1] * sums[1] - spread * difference)
+        return flux, [pltpu.roll(x, STRIP - 1, 0) for x in flux]
+
+    across = [None] * far
+    fluxes = [[None] * (strips + 1) for _ in range(far)]
+    for s in list(range(2, strips)) + [1, strips, 0]:
+        for a in range(far):
+            if s in (strips, 0) and across[a] is None:
+                across[a] = interface(a)
+            if s == strips:
+                fluxes[a][s] = (None, [across[a][v][1:2] for v in range(nvar)])
             else:
-                lifted = [across[v][1:2] for v in range(nvar)]
-            if s > 0:
-                yield (
-                    s - 1,
-                    [jnp.where(row == STRIP - 1, lifted[v], last[1][v]) - last[0][v] for v in range(nvar)],
-                )
-            last = (flux, lifted)
-
-    for moves in zip(*[changes(a) for a in range(far)]):
-        s = moves[0][0]
-        factors = [pseudo_step / cells_of[a][0, strip(s), :] for a in range(far)]
-        for v in range(nvar):
-            given = other[0] * stepped[v, strip(s), :]
-            taken = None
-            for a in range(far):
-                value = parts[a][v, strip(s), :] - factors[a] * moves[a][1][v]
-                given = given + other[1 + a] * value
-                taken = mine[1 + a] * value if taken is None else taken + mine[1 + a] * value
-            shared[pl.ds(v * depth + s * STRIP, STRIP), :] = given
-            out[v, strip(s), :] = taken
+                fluxes[a][s] = flux_of(a, s)
+            if s == 0:
+                flux = [jnp.where(row == 0, across[a][v][0:1], fluxes[a][0][0][v]) for v in range(nvar)]
+                fluxes[a][0] = (flux, fluxes[a][0][1])
+        for t in {2: [], 1: [1], strips: [strips - 1], 0: [0]}.get(s, [s - 1]):
+            factors = [pseudo_step / cells_of[a][0, strip(t), :] for a in range(far)]
+            for v in range(nvar):
+                total = early[v, strip(t), :]
+                for a in range(far):
+                    above = jnp.where(row == STRIP - 1, fluxes[a][t + 1][1][v], fluxes[a][t][1][v])
+                    value = factors[a] * (above - fluxes[a][t][0][v])
+                    outs[a][v, strip(t), :] = value
+                    total = total - other[1 + a] * value
+                shared[pl.ds(v * depth + t * STRIP, STRIP), :] = total
     rims = pl.ds(0, 2 * nvar + 2)
     shared[pl.ds(nvar * depth, 2 * nvar + 2), :] = weighted(
         other, [edge[rims, :]] + [edges[a][rims, :] for a in range(far)]
@@ -497,7 +496,9 @@
     out[3 * nvar] = jnp.where(is_below, factor, -factor)
 
 
-def final_kernel(nvar, coefs, rims, kept, base, taken, shared, out, held, sems):
+def final_kernel(n, nvar, coefs, rims, kept, base, shared, *refs):
+    rows, (out, held, sems) = refs[:-3], refs[-3:]
+    weights = [step_weight(n, 0, b) for b in families(n)[0][1:]]
     depth, columns = base.shape[1], base.shape[2]
     strips = depth // STRIP
     half = half_jacobians(coefs, nvar)
@@ -507,8 +508,8 @@
         return pair(shared[pl.ds(nvar * depth + v, 1), :], shared[pl.ds(nvar * depth + nvar + 1 + v, 1), :])
 
     def value(v, s):
-        other = taken[v, strip(s), :] + shared[pl.ds(v * depth + s * STRIP, STRIP), :]
-        return base[v, strip(s), :] - other
+        total = base[v, strip(s), :] - shared[pl.ds(v * depth + s * STRIP, STRIP), :]
+        return total + weighted(weights, [x[v, strip(s), :] for x in rows])
 
     copies = []
 
@@ -664,10 +665,10 @@
         parts.append(
             call(functools.partial(far_col_kernel, nvar), "far_col", field, coefs, cell_of[k], *pieces_of[k])
         )
-    rate, stepped, *parts = call(
+    rate, early, stepped, *parts = call(
         functools.partial(time_kernel, n, nvar),
         "time",
-        [f32(depth, columns)] + [field] * (len(far) + 1),
+        [f32(depth, columns)] + [field] * (len(far) + 2),
         near,
         own_cell,
         sums,
@@ -688,17 +689,17 @@
         own_cell,
         own_rows,
         rate,
-    )
-    shared, taken = call(
+        *parts,
+    )
+    shared, *rows = call(
         functools.partial(far_step_kernel, n, nvar),
         "far_step",
-        [f32(nvar * depth + 16, columns), field],
+        [f32(nvar * depth + 16, columns)] + [field] * len(far),
         coefs,
-        stepped,
+        early,
         edge,
         *[edge_of[k] for k in far],
         *[cell_of[k] for k in far],
-        *parts,
         *[faces[k] for k in far],
         *[pieces_of[k][t] for t in range(len(PIECES)) for k in far],
     )
@@ -715,15 +716,15 @@
         *[edge_of[k] for k in far],
     )
     return call(
-        functools.partial(final_kernel, nvar),
+        functools.partial(final_kernel, n, nvar),
         "final",
         f32(1, nvar, depth, columns),
         coefs,
         rims,
         kept,
         base,
-        taken,
         swapped(shared, 1),
+        *rows,
         scratch=[pltpu.VMEM((nvar, depth, columns), jnp.float32), pltpu.SemaphoreType.DMA((3,))],
         out_spec=hbm,
     )

time: 20.6 us -> 20.5 us (level)
  transfers between devices with their start and end apart: 12 -> 12, of which waited for: 5 -> 4; matrix products, arithmetic and copies ran while one was open for 0% -> 0% of each run, Pallas kernels for 25% -> 26%
where the time goes in v7:
time: 20.5 us; the launch traced here: 20.4 us
  starting transfers between devices  10.9 us (53%)
  Pallas kernels  6.23 us (30%)
  waiting for transfers between devices  3.16 us (15%)
    ppermute x10, starting transfers between devices, swapped(): return lax.ppermute(x, 'inst', [(i, i ^ k) for i in range(n)])  6.73 us
    pallas_call x16, Pallas kernels, call(): pl.pallas_call(kernel, out_shape=shapes, in_specs=[smem if x is jacobians...  5.07 us
    ppermute x10, waiting for transfers between devices, swapped(): return lax.ppermute(x, 'inst', [(i, i ^ k) for i in range(n)])  2.43 us
    ppermute x1, starting transfers between devices, body(): lax.ppermute(upward, 'slab', [(i, (i + 1) % slabs) for i in range(slabs)])  2.11 us
    ppermute x1, starting transfers between devices, body(): lax.ppermute(downward, 'slab', [(i, (i - 1) % slabs) for i in range(slabs)])  2.03 us
    pallas_call x1, Pallas kernels, body(): pl.pallas_call(pack_kernel, out_shape=[f32(nvar, depth, columns), f32(3,...  1.16 us
    ppermute x1, waiting for transfers between devices, body(): lax.ppermute(downward, 'slab', [(i, (i - 1) % slabs) for i in range(slabs)])  0.73 us
  transfers between devices with their start and end apart: 12, of which 4 were waited for; matrix products, arithmetic and copies ran while one was open for 0% of the time, Pallas kernels for 26%

profile of v7, /device:TPU:0, one launch (start us, length us, event | category | flops | bytes accessed | tf_op | source)
XLA Modules:
  0.0 20.4 jit_solution(4988891117183918115)
XLA Ops:
  0.0 2.9 %collective-permute-start.4 = (f32[1,5,64,256]{3,2,1,0:T(8,128)}, f32[1,5,64,256]{3,2,1,0:T(8,128)S(1)}, u32[]{:S(2)}, u32[]{:S(2)}) collective-permute-start(f32[1,5,64,256]{3,2,1,0:T(8,128)} %states.4), channel_id=1, source_target_pairs={{0,8},{4,12},{8,0},{12,4},{1,9},{5,13},{9,1},{13,5},{2,10},{6,14},... | collective-permute-start | bytes 983048 | tf_op jit(solution)/shard_map/ppermute | solution.py:575
  2.9 1.2 %pack.1 = (f32[5,64,256]{2,1,0:T(8,128)S(1)}, f32[3,64,256]{2,1,0:T(8,128)S(1)}, f32[2,64,256]{2,1,0:T(8,128)S(1)}, s32[1,256]{1,0:T(1,128)S(1)}, f32[32,256]{1,0:T(8,128)S(1)}, /*index=5*/f32[24,256]{1,0:T(8,128)S(1)}) custom-call(f32[1,5,64,256]{3,2,1,0:T(8,128)} %states.4, f32[1,64,256]{2,1,0:T(8,128)} %volumes.3, f32[1,2,64,256]{3,2,1,0:T(8,128)} %row_normals.1, ...), custom_call_target="tpu_custom_call" | custom-call | tf_op jit(solution)/shard_map/pack/pallas_call | solution.py:582
  4.1 0.0 copy-start
  4.1 0.1 collective-permute-start.2
  4.2 0.1 collective-permute-start.5
  4.3 2.1 %collective-permute-start = (f32[32,256]{1,0:T(8,128)S(1)}, f32[32,256]{1,0:T(8,128)S(1)}, u32[]{:S(2)}, u32[]{:S(2)}) collective-permute-start(f32[32,256]{1,0:T(8,128)S(1)} %get-tuple-element.28), channel_id=1, source_target_pairs={{0,1},{1,2},{2,3},{3,0},{4,5},{5,6},{6,7},{7,4},{8,9},{9,10},{10,1... | collective-permute-start | bytes 98312 | tf_op jit(solution)/shard_map/ppermute | solution.py:599
  6.4 2.0 %collective-permute-start.1 = (f32[24,256]{1,0:T(8,128)S(1)}, f32[24,256]{1,0:T(8,128)S(1)}, u32[]{:S(2)}, u32[]{:S(2)}) collective-permute-start(f32[24,256]{1,0:T(8,128)S(1)} %get-tuple-element.29), channel_id=1, source_target_pairs={{0,3},{1,0},{2,1},{3,2},{4,7},{5,4},{6,5},{7,6},{8,11},{9,8},{10,9... | collective-permute-start | bytes 73736 | tf_op jit(solution)/shard_map/ppermute | solution.py:600
  8.5 1.4 %own_flux.1 = (f32[5,64,256]{2,1,0:T(8,128)S(1)}, f32[56,256]{1,0:T(8,128)S(1)}) custom-call(f32[2,5,5]{2,1,0:T(8,128)S(1)} %copy.7.jacobians, f32[5,64,256]{2,1,0:T(8,128)S(1)} %get-tuple-element.24.near, f32[3,64,256]{2,1,0:T(8,128)S(1)} %get-tuple-element.25.cell.cells.own, f32[2,64,256]{2,1,0:T(8,128)S(1)} %get-tuple-element.26.row_normals), custom_call_target="tpu_custom_call" | custom-call | tf_op jit(solution)/shard_map/own_flux/pallas_call | solution.py:564
  9.9 0.7 %collective-permute-done.1.above = f32[24,256]{1,0:T(8,128)S(1)} collective-permute-done((f32[24,256]{1,0:T(8,128)S(1)}, f32[24,256]{1,0:T(8,128)S(1)}, u32[]{:S(2)}, u32[]{:S(2)}) %collective-permute-start.1) | collective-permute-done | bytes 24608 | tf_op jit(solution)/shard_map/ppermute | solution.py:600
  10.6 0.0 collective-permute-done.below
  10.6 0.3 %edges.1 = (f32[144,256]{1,0:T(8,128)S(1)}, f32[13,2,256]{2,1,0:T(2,128)S(1)}) custom-call(f32[56,256]{1,0:T(8,128)S(1)} %get-tuple-element.27.coefs, f32[32,256]{1,0:T(8,128)S(1)} %collective-permute-done.below, f32[24,256]{1,0:T(8,128)S(1)} %collective-permute-done.1.above, f32[5,64,256]{2,1,0:T(8,128)S(1)} %get-tuple-element.24.near, ...), custom_call_target="tpu_custom_call" | custom-call | tf_op jit(solution)/shard_map/edges/pallas_call | solution.py:564
  10.9 0.1 collective-permute-start.3
  11.0 1.6 %collective-permute-start.10 = (f32[144,256]{1,0:T(8,128)S(1)}, f32[144,256]{1,0:T(8,128)S(1)}, u32[]{:S(2)}, u32[]{:S(2)}) collective-permute-start(f32[144,256]{1,0:T(8,128)S(1)} %get-tuple-element.32.before.edge), channel_id=1, source_target_pairs={{0,12},{4,8},{8,4},{12,0},{1,13},{5,9},{9,5},{13,1},{2,14},{6,10},... | collective-permute-start | bytes 442376 | tf_op jit(solution)/shard_map/ppermute | solution.py:575
  12.6 0.1 collective-permute-start.7
  12.7 0.5 %collective-permute-start.8 = (f32[2,64,256]{2,1,0:T(8,128)S(1)}, f32[2,64,256]{2,1,0:T(8,128)S(1)}, u32[]{:S(2)}, u32[]{:S(2)}) collective-permute-start(f32[2,64,256]{2,1,0:T(8,128)S(1)} %states.6), channel_id=1, source_target_pairs={{0,4},{4,0},{8,12},{12,8},{1,5},{5,1},{9,13},{13,9},{2,6},{6,2},{1... | collective-permute-start | bytes 393224 | tf_op jit(solution)/shard_map/ppermute | solution.py:575
  13.3 0.1 near.1
  13.4 0.1 collective-permute-start.9
  13.5 2.0 %collective-permute-done.5.cells.cell.refs_1_ = f32[3,64,256]{2,1,0:T(8,128)S(1)} collective-permute-done((f32[3,64,256]{2,1,0:T(8,128)S(1)}, f32[3,64,256]{2,1,0:T(8,128)S(1)}, u32[]{:S(2)}, u32[]{:S(2)}) %collective-permute-start.5) | collective-permute-done | bytes 196640 | tf_op jit(solution)/shard_map/ppermute | solution.py:575
  15.5 0.5 %collective-permute-start.6 = (f32[1,64,256]{2,1,0:T(8,128)S(1)}, f32[1,64,256]{2,1,0:T(8,128)S(1)}, u32[]{:S(2)}, u32[]{:S(2)}) collective-permute-start(f32[1,64,256]{2,1,0:T(8,128)S(1)} %volumes.5), channel_id=1, source_target_pairs={{0,4},{4,0},{8,12},{12,8},{1,5},{5,1},{9,13},{13,9},{2,6},{6,2},{1... | collective-permute-start | bytes 196616 | tf_op jit(solution)/shard_map/ppermute | solution.py:575
  16.0 0.0 collective-permute-done.8.refs_1_.refs_4_
  16.0 0.5 %far_col.1.refs_8_ = f32[5,64,256]{2,1,0:T(8,128)S(1)} custom-call(f32[56,256]{1,0:T(8,128)S(1)} %get-tuple-element.27.coefs, f32[3,64,256]{2,1,0:T(8,128)S(1)} %collective-permute-done.5.cells.cell.refs_1_, f32[2,64,256]{2,1,0:T(8,128)S(1)} %collective-permute-done.7.refs_0_.refs_3_, f32[2,64,256]{2,1,0:T(8,128)S(1)} %collective-permute-done.8.refs_1_.refs_4_, ...), custom_call_target="tpu_custom_call" | custom-call | tf_op jit(solution)/shard_map/far_col/pallas_call | solution.py:564
  16.6 0.3 %far_faces.1.refs_2_ = f32[3,5,64,256]{3,2,1,0:T(8,128)S(1)} custom-call(f32[56,256]{1,0:T(8,128)S(1)} %get-tuple-element.27.coefs, f32[2,64,256]{2,1,0:T(8,128)S(1)} %collective-permute-done.7.refs_0_.refs_3_, f32[2,64,256]{2,1,0:T(8,128)S(1)} %collective-permute-done.8.refs_1_.refs_4_, f32[1,64,256]{2,1,0:T(8,128)S(1)} %collective-permute-done.9.refs_2_.refs_5_), custom_call_target="tpu_custom_call" | custom-call | tf_op jit(solution)/shard_map/far_faces/pallas_call | solution.py:564
  16.8 0.1 collective-permute-done.6.refs_2_
  16.9 0.2 %time.1 = (f32[64,256]{1,0:T(8,128)S(1)}, f32[5,64,256]{2,1,0:T(8,128)S(1)}, f32[5,64,256]{2,1,0:T(8,128)S(1)}, f32[5,64,256]{2,1,0:T(8,128)S(1)}) custom-call(f32[5,64,256]{2,1,0:T(8,128)S(1)} %get-tuple-element.24.near, f32[3,64,256]{2,1,0:T(8,128)S(1)} %get-tuple-element.25.cell.cells.own, f32[2,64,256]{2,1,0:T(8,128)S(1)} %get-tuple-element.34.sums, ...), custom_call_target="tpu_custom_call" | custom-call | tf_op jit(solution)/shard_map/time/pallas_call | solution.py:564
  17.2 0.3 %collective-permute-done.10.refs_0_ = f32[144,256]{1,0:T(8,128)S(1)} collective-permute-done((f32[144,256]{1,0:T(8,128)S(1)}, f32[144,256]{1,0:T(8,128)S(1)}, u32[]{:S(2)}, u32[]{:S(2)}) %collective-permute-start.10) | collective-permute-done | bytes 147488 | tf_op jit(solution)/shard_map/ppermute | solution.py:575
  17.5 0.2 far_step.1
  17.7 0.6 %collective-permute-start.11 = (f32[336,256]{1,0:T(8,128)S(1)}, f32[336,256]{1,0:T(8,128)S(1)}, u32[]{:S(2)}, u32[]{:S(2)}) collective-permute-start(f32[336,256]{1,0:T(8,128)S(1)} %get-tuple-element.41), channel_id=1, source_target_pairs={{0,4},{4,0},{8,12},{12,8},{1,5},{5,1},{9,13},{13,9},{2,6},{6,2},{1... | collective-permute-start | bytes 1032200 | tf_op jit(solution)/shard_map/ppermute | solution.py:575
  18.3 0.4 %behind.1.others = f32[5,2,256]{2,1,0:T(2,128)S(1)} custom-call(f32[56,256]{1,0:T(8,128)S(1)} %get-tuple-element.27.coefs, f32[32,256]{1,0:T(8,128)S(1)} %collective-permute-done.below, f32[24,256]{1,0:T(8,128)S(1)} %collective-permute-done.1.above, s32[1,256]{1,0:T(1,128)S(1)} %get-tuple-element.30.links), custom_call_target="tpu_custom_call" | custom-call | tf_op jit(solution)/shard_map/behind/pallas_call | solution.py:564
  18.7 0.8 %base.1 = f32[5,64,256]{2,1,0:T(8,128)S(1)} custom-call(f32[56,256]{1,0:T(8,128)S(1)} %get-tuple-element.27.coefs, f32[5,64,256]{2,1,0:T(8,128)S(1)} %get-tuple-element.37.stepped, f32[3,64,256]{2,1,0:T(8,128)S(1)} %get-tuple-element.25.cell.cells.own, f32[2,64,256]{2,1,0:T(8,128)S(1)} %get-tuple-element.26.row_normals, ...), custom_call_target="tpu_custom_call" | custom-call | tf_op jit(solution)/shard_map/base/pallas_call | solution.py:564
  19.5 0.1 rims.1
  19.5 0.0 collective-permute-done.11.shared
  19.6 0.8 %final.1 = f32[1,5,64,256]{3,2,1,0:T(8,128)} custom-call(f32[56,256]{1,0:T(8,128)S(1)} %get-tuple-element.27.coefs, f32[16,2,256]{2,1,0:T(2,128)S(1)} %rims.1, f32[13,2,256]{2,1,0:T(2,128)S(1)} %get-tuple-element.33.kept, f32[5,64,256]{2,1,0:T(8,128)S(1)} %base.1, f32[336,256]{1,0:T(8,128)S(1)} %collective-permute-done.11.shared, ...), custom_call_target="tpu_custom_call" | custom-call | tf_op jit(solution)/shard_map/final/pallas_call | solution.py:564
  (12 shorter events, 0.1 us)
Async XLA Ops:
  0.0 12.6 %collective-permute-start.4 = (f32[1,5,64,256]{3,2,1,0:T(8,128)}, f32[1,5,64,256]{3,2,1,0:T(8,128)S(1)}, u32[]{:S(2)}, u32[]{:S(2)}) collective-permute-start(f32[1,5,64,256]{3,2,1,0:T(8,128)} %states.4), channel_id=1, source_target_pairs={{0,8},{4,12},{8,0},{12,4},{1,9},{5,13},{9,1},{13,5},{2,10},{6,14},... | collective-permute-start | bytes 983048 | tf_op jit(solution)/shard_map/ppermute | solution.py:575
  4.1 4.3 %copy-start = (f32[2,5,5]{2,0,1:T(2,128)S(1)}, f32[2,5,5]{2,0,1:T(2,128)}, u32[]{:S(2)}) copy-start(f32[2,5,5]{2,0,1:T(2,128)} %param.11) | copy-start | bytes 604
  4.1 9.1 %collective-permute-start.2 = (f32[5,64,256]{2,1,0:T(8,128)S(1)}, f32[5,64,256]{2,1,0:T(8,128)S(1)}, u32[]{:S(2)}, u32[]{:S(2)}) collective-permute-start(f32[5,64,256]{2,1,0:T(8,128)S(1)} %get-tuple-element.24.near), channel_id=1, source_target_pairs={{0,4},{4,0},{8,12},{12,8},{1,5},{5,1},{9,13},{13,9},{2,6},{6,2},{1... | collective-permute-start | bytes 983048 | tf_op jit(solution)/shard_map/ppermute | solution.py:575
  4.2 11.3 %collective-permute-start.5 = (f32[3,64,256]{2,1,0:T(8,128)S(1)}, f32[3,64,256]{2,1,0:T(8,128)S(1)}, u32[]{:S(2)}, u32[]{:S(2)}) collective-permute-start(f32[3,64,256]{2,1,0:T(8,128)S(1)} %get-tuple-element.25.cell.cells.own), channel_id=1, source_target_pairs={{0,12},{4,8},{8,4},{12,0},{1,13},{5,9},{9,5},{13,1},{2,14},{6,10},... | collective-permute-start | bytes 589832 | tf_op jit(solution)/shard_map/ppermute | solution.py:575
  4.3 6.3 %collective-permute-start = (f32[32,256]{1,0:T(8,128)S(1)}, f32[32,256]{1,0:T(8,128)S(1)}, u32[]{:S(2)}, u32[]{:S(2)}) collective-permute-start(f32[32,256]{1,0:T(8,128)S(1)} %get-tuple-element.28), channel_id=1, source_target_pairs={{0,1},{1,2},{2,3},{3,0},{4,5},{5,6},{6,7},{7,4},{8,9},{9,10},{10,1... | collective-permute-start | bytes 98312 | tf_op jit(solution)/shard_map/ppermute | solution.py:599
  6.4 4.2 %collective-permute-start.1 = (f32[24,256]{1,0:T(8,128)S(1)}, f32[24,256]{1,0:T(8,128)S(1)}, u32[]{:S(2)}, u32[]{:S(2)}) collective-permute-start(f32[24,256]{1,0:T(8,128)S(1)} %get-tuple-element.29), channel_id=1, source_target_pairs={{0,3},{1,0},{2,1},{3,2},{4,7},{5,4},{6,5},{7,6},{8,11},{9,8},{10,9... | collective-permute-start | bytes 73736 | tf_op jit(solution)/shard_map/ppermute | solution.py:600
  10.9 1.8 %collective-permute-start.3 = (f32[1,64,256]{2,1,0:T(8,128)S(1)}, f32[1,64,256]{2,1,0:T(8,128)S(1)}, u32[]{:S(2)}, u32[]{:S(2)}) collective-permute-start(f32[1,64,256]{2,1,0:T(8,128)S(1)} %volumes.4), channel_id=1, source_target_pairs={{0,4},{4,0},{8,12},{12,8},{1,5},{5,1},{9,13},{13,9},{2,6},{6,2},{1... | collective-permute-start | bytes 196616 | tf_op jit(solution)/shard_map/ppermute | solution.py:575
  11.0 6.5 %collective-permute-start.10 = (f32[144,256]{1,0:T(8,128)S(1)}, f32[144,256]{1,0:T(8,128)S(1)}, u32[]{:S(2)}, u32[]{:S(2)}) collective-permute-start(f32[144,256]{1,0:T(8,128)S(1)} %get-tuple-element.32.before.edge), channel_id=1, source_target_pairs={{0,12},{4,8},{8,4},{12,0},{1,13},{5,9},{9,5},{13,1},{2,14},{6,10},... | collective-permute-start | bytes 442376 | tf_op jit(solution)/shard_map/ppermute | solution.py:575
  12.6 3.4 %collective-permute-start.7 = (f32[2,64,256]{2,1,0:T(8,128)S(1)}, f32[2,64,256]{2,1,0:T(8,128)S(1)}, u32[]{:S(2)}, u32[]{:S(2)}) collective-permute-start(f32[2,64,256]{2,1,0:T(8,128)S(1)} %states.5), channel_id=1, source_target_pairs={{0,4},{4,0},{8,12},{12,8},{1,5},{5,1},{9,13},{13,9},{2,6},{6,2},{1... | collective-permute-start | bytes 393224 | tf_op jit(solution)/shard_map/ppermute | solution.py:575
  12.7 3.3 %collective-permute-start.8 = (f32[2,64,256]{2,1,0:T(8,128)S(1)}, f32[2,64,256]{2,1,0:T(8,128)S(1)}, u32[]{:S(2)}, u32[]{:S(2)}) collective-permute-start(f32[2,64,256]{2,1,0:T(8,128)S(1)} %states.6), channel_id=1, source_target_pairs={{0,4},{4,0},{8,12},{12,8},{1,5},{5,1},{9,13},{13,9},{2,6},{6,2},{1... | collective-permute-start | bytes 393224 | tf_op jit(solution)/shard_map/ppermute | solution.py:575
  13.4 2.6 %collective-permute-start.9 = (f32[1,64,256]{2,1,0:T(8,128)S(1)}, f32[1,64,256]{2,1,0:T(8,128)S(1)}, u32[]{:S(2)}, u32[]{:S(2)}) collective-permute-start(f32[1,64,256]{2,1,0:T(8,128)S(1)} %states.7), channel_id=1, source_target_pairs={{0,4},{4,0},{8,12},{12,8},{1,5},{5,1},{9,13},{13,9},{2,6},{6,2},{1... | collective-permute-start | bytes 196616 | tf_op jit(solution)/shard_map/ppermute | solution.py:575
  15.5 1.4 %collective-permute-start.6 = (f32[1,64,256]{2,1,0:T(8,128)S(1)}, f32[1,64,256]{2,1,0:T(8,128)S(1)}, u32[]{:S(2)}, u32[]{:S(2)}) collective-permute-start(f32[1,64,256]{2,1,0:T(8,128)S(1)} %volumes.5), channel_id=1, source_target_pairs={{0,4},{4,0},{8,12},{12,8},{1,5},{5,1},{9,13},{13,9},{2,6},{6,2},{1... | collective-permute-start | bytes 196616 | tf_op jit(solution)/shard_map/ppermute | solution.py:575
  17.7 1.9 %collective-permute-start.11 = (f32[336,256]{1,0:T(8,128)S(1)}, f32[336,256]{1,0:T(8,128)S(1)}, u32[]{:S(2)}, u32[]{:S(2)}) collective-permute-start(f32[336,256]{1,0:T(8,128)S(1)} %get-tuple-element.41), channel_id=1, source_target_pairs={{0,4},{4,0},{8,12},{12,8},{1,5},{5,1},{9,13},{13,9},{2,6},{6,2},{1... | collective-permute-start | bytes 1032200 | tf_op jit(solution)/shard_map/ppermute | solution.py:575

commit v8 on v7

--- a/solution.py
+++ b/solution.py
@@ -641,7 +641,7 @@
         near,
         beyond,
         own_cell,
-        swapped(call(volume_kernel, "volumes", f32(1, depth, columns), own_cell, edge), 1),
+        swapped(call(volume_kernel, "volumes", f32(1, depth, columns), own_cell, others), 1),
         own_part,
     )
     pieces_of, beyond_volumes = dict(), dict()

time: 20.5 us -> 20.5 us (level)
  transfers between devices with their start and end apart: 12 -> 12, of which waited for: 4 -> 5; matrix products, arithmetic and copies ran while one was open for 0% -> 0% of each run, Pallas kernels for 26% -> 26%
where the time goes in v8:
time: 20.5 us; the launch traced here: 20.4 us
  starting transfers between devices  10.8 us (53%)
  Pallas kernels  6.23 us (30%)
  waiting for transfers between devices  3.22 us (16%)
    ppermute x10, starting transfers between devices, swapped(): return lax.ppermute(x, 'inst', [(i, i ^ k) for i in range(n)])  6.68 us
    pallas_call x16, Pallas kernels, call(): pl.pallas_call(kernel, out_shape=shapes, in_specs=[smem if x is jacobians...  5.07 us
    ppermute x10, waiting for transfers between devices, swapped(): return lax.ppermute(x, 'inst', [(i, i ^ k) for i in range(n)])  2.49 us
    ppermute x1, starting transfers between devices, body(): lax.ppermute(upward, 'slab', [(i, (i + 1) % slabs) for i in range(slabs)])  2.11 us
    ppermute x1, starting transfers between devices, body(): lax.ppermute(downward, 'slab', [(i, (i - 1) % slabs) for i in range(slabs)])  2.03 us
    pallas_call x1, Pallas kernels, body(): pl.pallas_call(pack_kernel, out_shape=[f32(nvar, depth, columns), f32(3,...  1.16 us
    ppermute x1, waiting for transfers between devices, body(): lax.ppermute(downward, 'slab', [(i, (i - 1) % slabs) for i in range(slabs)])  0.73 us
  transfers between devices with their start and end apart: 12, of which 5 were waited for; matrix products, arithmetic and copies ran while one was open for 0% of the time, Pallas kernels for 26%

profile of v8, /device:TPU:0, one launch (start us, length us, event | category | flops | bytes accessed | tf_op | source)
XLA Modules:
  0.0 20.4 jit_solution(3445167900751893700)
XLA Ops:
  0.0 2.9 %collective-permute-start.4 = (f32[1,5,64,256]{3,2,1,0:T(8,128)}, f32[1,5,64,256]{3,2,1,0:T(8,128)S(1)}, u32[]{:S(2)}, u32[]{:S(2)}) collective-permute-start(f32[1,5,64,256]{3,2,1,0:T(8,128)} %states.4), channel_id=1, source_target_pairs={{0,8},{4,12},{8,0},{12,4},{1,9},{5,13},{9,1},{13,5},{2,10},{6,14},... | collective-permute-start | bytes 983048 | tf_op jit(solution)/shard_map/ppermute | solution.py:575
  2.9 1.2 %pack.1 = (f32[5,64,256]{2,1,0:T(8,128)S(1)}, f32[3,64,256]{2,1,0:T(8,128)S(1)}, f32[2,64,256]{2,1,0:T(8,128)S(1)}, s32[1,256]{1,0:T(1,128)S(1)}, f32[32,256]{1,0:T(8,128)S(1)}, /*index=5*/f32[24,256]{1,0:T(8,128)S(1)}) custom-call(f32[1,5,64,256]{3,2,1,0:T(8,128)} %states.4, f32[1,64,256]{2,1,0:T(8,128)} %volumes.3, f32[1,2,64,256]{3,2,1,0:T(8,128)} %row_normals.1, ...), custom_call_target="tpu_custom_call" | custom-call | tf_op jit(solution)/shard_map/pack/pallas_call | solution.py:582
  4.1 0.0 copy-start
  4.1 0.1 collective-permute-start.2
  4.2 0.1 collective-permute-start.5
  4.3 2.1 %collective-permute-start = (f32[32,256]{1,0:T(8,128)S(1)}, f32[32,256]{1,0:T(8,128)S(1)}, u32[]{:S(2)}, u32[]{:S(2)}) collective-permute-start(f32[32,256]{1,0:T(8,128)S(1)} %get-tuple-element.28), channel_id=1, source_target_pairs={{0,1},{1,2},{2,3},{3,0},{4,5},{5,6},{6,7},{7,4},{8,9},{9,10},{10,1... | collective-permute-start | bytes 98312 | tf_op jit(solution)/shard_map/ppermute | solution.py:599
  6.4 2.0 %collective-permute-start.1 = (f32[24,256]{1,0:T(8,128)S(1)}, f32[24,256]{1,0:T(8,128)S(1)}, u32[]{:S(2)}, u32[]{:S(2)}) collective-permute-start(f32[24,256]{1,0:T(8,128)S(1)} %get-tuple-element.29), channel_id=1, source_target_pairs={{0,3},{1,0},{2,1},{3,2},{4,7},{5,4},{6,5},{7,6},{8,11},{9,8},{10,9... | collective-permute-start | bytes 73736 | tf_op jit(solution)/shard_map/ppermute | solution.py:600
  8.5 1.4 %own_flux.1 = (f32[5,64,256]{2,1,0:T(8,128)S(1)}, f32[56,256]{1,0:T(8,128)S(1)}) custom-call(f32[2,5,5]{2,1,0:T(8,128)S(1)} %copy.7.jacobians, f32[5,64,256]{2,1,0:T(8,128)S(1)} %get-tuple-element.24.near, f32[3,64,256]{2,1,0:T(8,128)S(1)} %get-tuple-element.25.cell.cells.own, f32[2,64,256]{2,1,0:T(8,128)S(1)} %get-tuple-element.26.row_normals), custom_call_target="tpu_custom_call" | custom-call | tf_op jit(solution)/shard_map/own_flux/pallas_call | solution.py:564
  9.9 0.7 %collective-permute-done.1.above = f32[24,256]{1,0:T(8,128)S(1)} collective-permute-done((f32[24,256]{1,0:T(8,128)S(1)}, f32[24,256]{1,0:T(8,128)S(1)}, u32[]{:S(2)}, u32[]{:S(2)}) %collective-permute-start.1) | collective-permute-done | bytes 24608 | tf_op jit(solution)/shard_map/ppermute | solution.py:600
  10.6 0.0 collective-permute-done.below
  10.6 0.4 %behind.1.before.others = f32[5,2,256]{2,1,0:T(2,128)S(1)} custom-call(f32[56,256]{1,0:T(8,128)S(1)} %get-tuple-element.27.coefs, f32[32,256]{1,0:T(8,128)S(1)} %collective-permute-done.below, f32[24,256]{1,0:T(8,128)S(1)} %collective-permute-done.1.above, s32[1,256]{1,0:T(1,128)S(1)} %get-tuple-element.30.links), custom_call_target="tpu_custom_call" | custom-call | tf_op jit(solution)/shard_map/behind/pallas_call | solution.py:564
  11.0 0.1 collective-permute-start.3
  11.1 0.3 %edges.1 = (f32[144,256]{1,0:T(8,128)S(1)}, f32[13,2,256]{2,1,0:T(2,128)S(1)}) custom-call(f32[56,256]{1,0:T(8,128)S(1)} %get-tuple-element.27.coefs, f32[32,256]{1,0:T(8,128)S(1)} %collective-permute-done.below, f32[24,256]{1,0:T(8,128)S(1)} %collective-permute-done.1.above, f32[5,64,256]{2,1,0:T(8,128)S(1)} %get-tuple-element.24.near, ...), custom_call_target="tpu_custom_call" | custom-call | tf_op jit(solution)/shard_map/edges/pallas_call | solution.py:564
  11.3 1.7 %collective-permute-start.10 = (f32[144,256]{1,0:T(8,128)S(1)}, f32[144,256]{1,0:T(8,128)S(1)}, u32[]{:S(2)}, u32[]{:S(2)}) collective-permute-start(f32[144,256]{1,0:T(8,128)S(1)} %get-tuple-element.32.before.edge), channel_id=1, source_target_pairs={{0,12},{4,8},{8,4},{12,0},{1,13},{5,9},{9,5},{13,1},{2,14},{6,10},... | collective-permute-start | bytes 442376 | tf_op jit(solution)/shard_map/ppermute | solution.py:575
  13.0 0.1 collective-permute-start.7
  13.1 0.6 %collective-permute-start.8 = (f32[2,64,256]{2,1,0:T(8,128)S(1)}, f32[2,64,256]{2,1,0:T(8,128)S(1)}, u32[]{:S(2)}, u32[]{:S(2)}) collective-permute-start(f32[2,64,256]{2,1,0:T(8,128)S(1)} %states.6), channel_id=1, source_target_pairs={{0,4},{4,0},{8,12},{12,8},{1,5},{5,1},{9,13},{13,9},{2,6},{6,2},{1... | collective-permute-start | bytes 393224 | tf_op jit(solution)/shard_map/ppermute | solution.py:575
  13.7 0.1 near.1
  13.8 0.1 collective-permute-start.9
  13.9 1.3 %collective-permute-done.5.cells.cell.refs_1_ = f32[3,64,256]{2,1,0:T(8,128)S(1)} collective-permute-done((f32[3,64,256]{2,1,0:T(8,128)S(1)}, f32[3,64,256]{2,1,0:T(8,128)S(1)}, u32[]{:S(2)}, u32[]{:S(2)}) %collective-permute-start.5) | collective-permute-done | bytes 196640 | tf_op jit(solution)/shard_map/ppermute | solution.py:575
  15.2 0.6 %collective-permute-start.6 = (f32[1,64,256]{2,1,0:T(8,128)S(1)}, f32[1,64,256]{2,1,0:T(8,128)S(1)}, u32[]{:S(2)}, u32[]{:S(2)}) collective-permute-start(f32[1,64,256]{2,1,0:T(8,128)S(1)} %volumes.5), channel_id=1, source_target_pairs={{0,4},{4,0},{8,12},{12,8},{1,5},{5,1},{9,13},{13,9},{2,6},{6,2},{1... | collective-permute-start | bytes 196616 | tf_op jit(solution)/shard_map/ppermute | solution.py:575
  15.8 0.0 collective-permute-done.9.refs_2_.refs_5_
  15.8 0.5 %far_col.1.refs_8_ = f32[5,64,256]{2,1,0:T(8,128)S(1)} custom-call(f32[56,256]{1,0:T(8,128)S(1)} %get-tuple-element.27.coefs, f32[3,64,256]{2,1,0:T(8,128)S(1)} %collective-permute-done.5.cells.cell.refs_1_, f32[2,64,256]{2,1,0:T(8,128)S(1)} %collective-permute-done.7.refs_0_.refs_3_, f32[2,64,256]{2,1,0:T(8,128)S(1)} %collective-permute-done.8.refs_1_.refs_4_, ...), custom_call_target="tpu_custom_call" | custom-call | tf_op jit(solution)/shard_map/far_col/pallas_call | solution.py:564
  16.3 0.3 %far_faces.1.refs_2_ = f32[3,5,64,256]{3,2,1,0:T(8,128)S(1)} custom-call(f32[56,256]{1,0:T(8,128)S(1)} %get-tuple-element.27.coefs, f32[2,64,256]{2,1,0:T(8,128)S(1)} %collective-permute-done.7.refs_0_.refs_3_, f32[2,64,256]{2,1,0:T(8,128)S(1)} %collective-permute-done.8.refs_1_.refs_4_, f32[1,64,256]{2,1,0:T(8,128)S(1)} %collective-permute-done.9.refs_2_.refs_5_), custom_call_target="tpu_custom_call" | custom-call | tf_op jit(solution)/shard_map/far_faces/pallas_call | solution.py:564
  16.6 0.1 collective-permute-done.6.refs_2_
  16.7 0.2 %time.1 = (f32[64,256]{1,0:T(8,128)S(1)}, f32[5,64,256]{2,1,0:T(8,128)S(1)}, f32[5,64,256]{2,1,0:T(8,128)S(1)}, f32[5,64,256]{2,1,0:T(8,128)S(1)}) custom-call(f32[5,64,256]{2,1,0:T(8,128)S(1)} %get-tuple-element.24.near, f32[3,64,256]{2,1,0:T(8,128)S(1)} %get-tuple-element.25.cell.cells.own, f32[2,64,256]{2,1,0:T(8,128)S(1)} %get-tuple-element.34.sums, ...), custom_call_target="tpu_custom_call" | custom-call | tf_op jit(solution)/shard_map/time/pallas_call | solution.py:564
  16.9 0.7 %collective-permute-done.10.refs_0_ = f32[144,256]{1,0:T(8,128)S(1)} collective-permute-done((f32[144,256]{1,0:T(8,128)S(1)}, f32[144,256]{1,0:T(8,128)S(1)}, u32[]{:S(2)}, u32[]{:S(2)}) %collective-permute-start.10) | collective-permute-done | bytes 147488 | tf_op jit(solution)/shard_map/ppermute | solution.py:575
  17.6 0.2 far_step.1
  17.8 0.5 %collective-permute-start.11 = (f32[336,256]{1,0:T(8,128)S(1)}, f32[336,256]{1,0:T(8,128)S(1)}, u32[]{:S(2)}, u32[]{:S(2)}) collective-permute-start(f32[336,256]{1,0:T(8,128)S(1)} %get-tuple-element.41), channel_id=1, source_target_pairs={{0,4},{4,0},{8,12},{12,8},{1,5},{5,1},{9,13},{13,9},{2,6},{6,2},{1... | collective-permute-start | bytes 1032200 | tf_op jit(solution)/shard_map/ppermute | solution.py:575
  18.3 0.8 %base.1 = f32[5,64,256]{2,1,0:T(8,128)S(1)} custom-call(f32[56,256]{1,0:T(8,128)S(1)} %get-tuple-element.27.coefs, f32[5,64,256]{2,1,0:T(8,128)S(1)} %get-tuple-element.37.stepped, f32[3,64,256]{2,1,0:T(8,128)S(1)} %get-tuple-element.25.cell.cells.own, f32[2,64,256]{2,1,0:T(8,128)S(1)} %get-tuple-element.26.row_normals, ...), custom_call_target="tpu_custom_call" | custom-call | tf_op jit(solution)/shard_map/base/pallas_call | solution.py:564
  19.1 0.1 rims.1
  19.2 0.4 %collective-permute-done.11.shared = f32[336,256]{1,0:T(8,128)S(1)} collective-permute-done((f32[336,256]{1,0:T(8,128)S(1)}, f32[336,256]{1,0:T(8,128)S(1)}, u32[]{:S(2)}, u32[]{:S(2)}) %collective-permute-start.11) | collective-permute-done | bytes 344096 | tf_op jit(solution)/shard_map/ppermute | solution.py:575
  19.6 0.8 %final.1 = f32[1,5,64,256]{3,2,1,0:T(8,128)} custom-call(f32[56,256]{1,0:T(8,128)S(1)} %get-tuple-element.27.coefs, f32[16,2,256]{2,1,0:T(2,128)S(1)} %rims.1, f32[13,2,256]{2,1,0:T(2,128)S(1)} %get-tuple-element.33.kept, f32[5,64,256]{2,1,0:T(8,128)S(1)} %base.1, f32[336,256]{1,0:T(8,128)S(1)} %collective-permute-done.11.shared, ...), custom_call_target="tpu_custom_call" | custom-call | tf_op jit(solution)/shard_map/final/pallas_call | solution.py:564
  (12 shorter events, 0.1 us)
Async XLA Ops:
  0.0 13.0 %collective-permute-start.4 = (f32[1,5,64,256]{3,2,1,0:T(8,128)}, f32[1,5,64,256]{3,2,1,0:T(8,128)S(1)}, u32[]{:S(2)}, u32[]{:S(2)}) collective-permute-start(f32[1,5,64,256]{3,2,1,0:T(8,128)} %states.4), channel_id=1, source_target_pairs={{0,8},{4,12},{8,0},{12,4},{1,9},{5,13},{9,1},{13,5},{2,10},{6,14},... | collective-permute-start | bytes 983048 | tf_op jit(solution)/shard_map/ppermute | solution.py:575
  4.1 4.3 %copy-start = (f32[2,5,5]{2,0,1:T(2,128)S(1)}, f32[2,5,5]{2,0,1:T(2,128)}, u32[]{:S(2)}) copy-start(f32[2,5,5]{2,0,1:T(2,128)} %param.11) | copy-start | bytes 604
  4.1 9.6 %collective-permute-start.2 = (f32[5,64,256]{2,1,0:T(8,128)S(1)}, f32[5,64,256]{2,1,0:T(8,128)S(1)}, u32[]{:S(2)}, u32[]{:S(2)}) collective-permute-start(f32[5,64,256]{2,1,0:T(8,128)S(1)} %get-tuple-element.24.near), channel_id=1, source_target_pairs={{0,4},{4,0},{8,12},{12,8},{1,5},{5,1},{9,13},{13,9},{2,6},{6,2},{1... | collective-permute-start | bytes 983048 | tf_op jit(solution)/shard_map/ppermute | solution.py:575
  4.2 11.0 %collective-permute-start.5 = (f32[3,64,256]{2,1,0:T(8,128)S(1)}, f32[3,64,256]{2,1,0:T(8,128)S(1)}, u32[]{:S(2)}, u32[]{:S(2)}) collective-permute-start(f32[3,64,256]{2,1,0:T(8,128)S(1)} %get-tuple-element.25.cell.cells.own), channel_id=1, source_target_pairs={{0,12},{4,8},{8,4},{12,0},{1,13},{5,9},{9,5},{13,1},{2,14},{6,10},... | collective-permute-start | bytes 589832 | tf_op jit(solution)/shard_map/ppermute | solution.py:575
  4.3 6.3 %collective-permute-start = (f32[32,256]{1,0:T(8,128)S(1)}, f32[32,256]{1,0:T(8,128)S(1)}, u32[]{:S(2)}, u32[]{:S(2)}) collective-permute-start(f32[32,256]{1,0:T(8,128)S(1)} %get-tuple-element.28), channel_id=1, source_target_pairs={{0,1},{1,2},{2,3},{3,0},{4,5},{5,6},{6,7},{7,4},{8,9},{9,10},{10,1... | collective-permute-start | bytes 98312 | tf_op jit(solution)/shard_map/ppermute | solution.py:599
  6.4 4.2 %collective-permute-start.1 = (f32[24,256]{1,0:T(8,128)S(1)}, f32[24,256]{1,0:T(8,128)S(1)}, u32[]{:S(2)}, u32[]{:S(2)}) collective-permute-start(f32[24,256]{1,0:T(8,128)S(1)} %get-tuple-element.29), channel_id=1, source_target_pairs={{0,3},{1,0},{2,1},{3,2},{4,7},{5,4},{6,5},{7,6},{8,11},{9,8},{10,9... | collective-permute-start | bytes 73736 | tf_op jit(solution)/shard_map/ppermute | solution.py:600
  11.0 2.1 %collective-permute-start.3 = (f32[1,64,256]{2,1,0:T(8,128)S(1)}, f32[1,64,256]{2,1,0:T(8,128)S(1)}, u32[]{:S(2)}, u32[]{:S(2)}) collective-permute-start(f32[1,64,256]{2,1,0:T(8,128)S(1)} %volumes.4), channel_id=1, source_target_pairs={{0,4},{4,0},{8,12},{12,8},{1,5},{5,1},{9,13},{13,9},{2,6},{6,2},{1... | collective-permute-start | bytes 196616 | tf_op jit(solution)/shard_map/ppermute | solution.py:575
  11.3 6.3 %collective-permute-start.10 = (f32[144,256]{1,0:T(8,128)S(1)}, f32[144,256]{1,0:T(8,128)S(1)}, u32[]{:S(2)}, u32[]{:S(2)}) collective-permute-start(f32[144,256]{1,0:T(8,128)S(1)} %get-tuple-element.32.before.edge), channel_id=1, source_target_pairs={{0,12},{4,8},{8,4},{12,0},{1,13},{5,9},{9,5},{13,1},{2,14},{6,10},... | collective-permute-start | bytes 442376 | tf_op jit(solution)/shard_map/ppermute | solution.py:575
  13.0 2.8 %collective-permute-start.7 = (f32[2,64,256]{2,1,0:T(8,128)S(1)}, f32[2,64,256]{2,1,0:T(8,128)S(1)}, u32[]{:S(2)}, u32[]{:S(2)}) collective-permute-start(f32[2,64,256]{2,1,0:T(8,128)S(1)} %states.5), channel_id=1, source_target_pairs={{0,4},{4,0},{8,12},{12,8},{1,5},{5,1},{9,13},{13,9},{2,6},{6,2},{1... | collective-permute-start | bytes 393224 | tf_op jit(solution)/shard_map/ppermute | solution.py:575
  13.1 2.7 %collective-permute-start.8 = (f32[2,64,256]{2,1,0:T(8,128)S(1)}, f32[2,64,256]{2,1,0:T(8,128)S(1)}, u32[]{:S(2)}, u32[]{:S(2)}) collective-permute-start(f32[2,64,256]{2,1,0:T(8,128)S(1)} %states.6), channel_id=1, source_target_pairs={{0,4},{4,0},{8,12},{12,8},{1,5},{5,1},{9,13},{13,9},{2,6},{6,2},{1... | collective-permute-start | bytes 393224 | tf_op jit(solution)/shard_map/ppermute | solution.py:575
  13.8 2.0 %collective-permute-start.9 = (f32[1,64,256]{2,1,0:T(8,128)S(1)}, f32[1,64,256]{2,1,0:T(8,128)S(1)}, u32[]{:S(2)}, u32[]{:S(2)}) collective-permute-start(f32[1,64,256]{2,1,0:T(8,128)S(1)} %states.7), channel_id=1, source_target_pairs={{0,4},{4,0},{8,12},{12,8},{1,5},{5,1},{9,13},{13,9},{2,6},{6,2},{1... | collective-permute-start | bytes 196616 | tf_op jit(solution)/shard_map/ppermute | solution.py:575
  15.2 1.5 %collective-permute-start.6 = (f32[1,64,256]{2,1,0:T(8,128)S(1)}, f32[1,64,256]{2,1,0:T(8,128)S(1)}, u32[]{:S(2)}, u32[]{:S(2)}) collective-permute-start(f32[1,64,256]{2,1,0:T(8,128)S(1)} %volumes.5), channel_id=1, source_target_pairs={{0,4},{4,0},{8,12},{12,8},{1,5},{5,1},{9,13},{13,9},{2,6},{6,2},{1... | collective-permute-start | bytes 196616 | tf_op jit(solution)/shard_map/ppermute | solution.py:575
  17.8 1.8 %collective-permute-start.11 = (f32[336,256]{1,0:T(8,128)S(1)}, f32[336,256]{1,0:T(8,128)S(1)}, u32[]{:S(2)}, u32[]{:S(2)}) collective-permute-start(f32[336,256]{1,0:T(8,128)S(1)} %get-tuple-element.41), channel_id=1, source_target_pairs={{0,4},{4,0},{8,12},{12,8},{1,5},{5,1},{9,13},{13,9},{2,6},{6,2},{1... | collective-permute-start | bytes 1032200 | tf_op jit(solution)/shard_map/ppermute | solution.py:575
